TPU v7x, 32 devices: a whole 2x2x4 slice. The times are simulated.
32 devices in a mesh: grp: 4 (over y, x), row: 8 (over z, core).
Axes of the slice: x: 2, y: 2, z: 4, core: 2. Of those that a mesh axis runs over, the one named last changes fastest.
Arguments:
- vectors: bfloat16 [131072, 1024], P(('grp', 'row')), may hold values from -6 to 6
- keep_bits: int32 [131072], P(('grp', 'row')), may hold values 0 or 1
- counts: int32 [1024], P(('grp', 'row')), may hold values from 1 to 128
- block_list: int32 [1024], replicated, may hold values from 0 to 2047, as said below
- home_pos: int32 [2048], replicated, may hold values from 0 to 2047, as said below
- old_centroids: bfloat16 [2048, 1024], P('grp'), may hold values from -1.5 to 1.5
Outputs:
- new_centroids: bfloat16 [2048, 1024], P(('grp', 'row'))
- scores: float32 [131072, 512], P(('grp', 'row'))
Inputs may be any that keep to these rules, and one draw needn't show every extreme that they name: `block_list`: every block's list is one of the lists of the block's own group; on one device at most one block has a list whose new position lies in any given other group, and this most is reached in every draw. `home_pos`: A permutation of the positions; position p lies in group p // 512.
All inputs are finite; a program needn't handle non-finite values. No bound on the sum of `keep_bits` on one device may be relied on, other than what follows from the above.
Results may differ from a plain program's by a relative error of at most 0.002.
Values may be sent and summed in bfloat16 or wider, within the bound.
No kernel may reach another device: no remote copies, remote signals or barrier semaphores. Data moves between devices by JAX's collectives and lax.ppermute only.
A program may use at most 128 MiB of HBM per device.

v0:
```python
import math

import jax
import jax.numpy as jnp
from jax import lax
from jax.sharding import PartitionSpec as P

PRIOR = 16


def centroid_rows(sums, totals, previous):
    prior_weight = 1.0 * PRIOR
    return (
        (sums + prior_weight * previous.astype(jnp.float32)) / (totals + prior_weight)[:, None]
    ).astype(jnp.bfloat16)


def score_rows(rows, table, norms, factor):
    dots = lax.dot_general(
        rows, table, (((1,), (1,)), ((), ())), preferred_element_type=jnp.float32
    )
    return (2.0 * dots - norms[None, :]) * factor


def local(vectors, keep_bits, counts, block_list, home_pos, old_centroids):
    n_groups = lax.axis_size("grp")
    n_rows = lax.axis_size("row")
    group_index = lax.axis_index("grp")
    row_index = lax.axis_index("row")
    blocks = counts.shape[0]
    block_rows = vectors.shape[0] // blocks
    width = vectors.shape[1]
    lists_group = old_centroids.shape[0]
    factor = 1.0 / math.sqrt(width)
    row_blocks = vectors.reshape(blocks, block_rows, width)
    position = lax.broadcasted_iota(jnp.int32, (blocks, block_rows), 1)
    alive = (
        keep_bits.reshape(blocks, block_rows) * (position < counts[:, None]).astype(jnp.int32)
    ).astype(jnp.float32)
    alive_half = alive.astype(jnp.bfloat16)
    masked = row_blocks * alive_half[:, :, None]
    homes = jnp.take(home_pos, block_list)
    home_groups = (homes // lists_group).reshape(n_groups, n_rows, blocks)
    home_slots = (homes % lists_group).reshape(n_groups, n_rows, blocks)
    peer_groups = lax.dynamic_index_in_dim(home_groups, row_index, 1, keepdims=False)
    peer_slots = lax.dynamic_index_in_dim(home_slots, row_index, 1, keepdims=False)
    mine_groups = lax.dynamic_index_in_dim(peer_groups, group_index, 0, keepdims=False)
    mine_slots = lax.dynamic_index_in_dim(peer_slots, group_index, 0, keepdims=False)
    staying = mine_groups == group_index
    block_sums = jnp.einsum(
        "bi,bid->bd", alive_half, row_blocks, preferred_element_type=jnp.float32
    )
    block_counts = jnp.sum(alive, axis=1)
    list_iota = lax.broadcasted_iota(jnp.int32, (lists_group, blocks), 0)
    stay_onehot = ((mine_slots[None, :] == list_iota) & staying[None, :]).astype(jnp.float32)
    sums = jnp.dot(
        stay_onehot, block_sums, precision=lax.Precision.HIGHEST, preferred_element_type=jnp.float32
    )
    totals = jnp.dot(
        stay_onehot,
        block_counts,
        precision=lax.Precision.HIGHEST,
        preferred_element_type=jnp.float32,
    )
    group_iota = lax.broadcasted_iota(jnp.int32, (n_groups, blocks), 0)
    outgoing = (mine_groups[None, :] == group_iota) & jnp.logical_not(staying)[None, :]
    present = jnp.any(outgoing, axis=1)
    pick_index = jnp.argmax(outgoing, axis=1)
    incoming = (peer_groups == group_index) & (group_iota != group_index)
    arriving = jnp.any(incoming, axis=1)
    arrive_index = jnp.argmax(incoming, axis=1)
    arrive_slots = jnp.take_along_axis(peer_slots, arrive_index[:, None], axis=1)[:, 0]
    slot_iota = lax.broadcasted_iota(jnp.int32, (lists_group, n_groups), 0)
    arrive_onehot = ((arrive_slots[None, :] == slot_iota) & arriving[None, :]).astype(jnp.float32)
    send_sums = jnp.take(block_sums, pick_index, axis=0) * present.astype(jnp.float32)[:, None]
    send_counts = jnp.take(block_counts, pick_index) * present.astype(jnp.float32)
    got_sums, got_counts = (
        lax.all_to_all(send_sums, "grp", split_axis=0, concat_axis=0, tiled=True),
        lax.all_to_all(send_counts, "grp", split_axis=0, concat_axis=0, tiled=True),
    )
    sums = sums + jnp.dot(
        arrive_onehot, got_sums, precision=lax.Precision.HIGHEST, preferred_element_type=jnp.float32
    )
    totals = totals + jnp.dot(
        arrive_onehot,
        got_counts,
        precision=lax.Precision.HIGHEST,
        preferred_element_type=jnp.float32,
    )
    share = lists_group // n_rows
    all_sums, all_totals = lax.psum((sums, totals), "row")
    table = centroid_rows(all_sums, all_totals, old_centroids)
    new_centroids = lax.dynamic_slice_in_dim(table, row_index * share, share, 0)
    tables = lax.all_gather(table, "grp", axis=0, tiled=True)
    all_norms = jnp.sum(jnp.square(tables.astype(jnp.float32)), axis=1)

    def one_block(item):
        rows, weights, group_of = item
        start = group_of * lists_group
        part = lax.dynamic_slice_in_dim(tables, start, lists_group, 0)
        part_norms = lax.dynamic_slice_in_dim(all_norms, start, lists_group, 0)
        return score_rows(rows, part, part_norms, factor) * weights[:, None]

    scores = lax.map(one_block, (masked, alive, mine_groups))
    return (new_centroids, scores.reshape(blocks * block_rows, lists_group))


def solution(mesh):
    in_specs = (
        P(("grp", "row"), None),
        P(("grp", "row")),
        P(("grp", "row")),
        P(),
        P(),
        P("grp", None),
    )
    out_specs = (P(("grp", "row"), None), P(("grp", "row"), None))
    return jax.shard_map(local, mesh=mesh, in_specs=in_specs, out_specs=out_specs, check_vma=False)
```

profile of v0, /device:TPU:0, one launch (start us, length us, event | category | flops | bytes accessed | tf_op | source)
XLA Modules:
  0.0 288.3 jit_solution(11035277695180719423)
XLA Ops:
  7.9 6.1 %gather_fusion = s32[1024]{0:T(1024)S(1)} fusion(s32[2048]{0:T(1024)S(1)} %copy-done, s32[1024]{0:T(1024)S(1)} %fusion.35), kind=kCustom, calls=%fused_computation | custom fusion | bytes 12288 | tf_op jit(solution)/shard_map/jit(_take)/gather | solution.py:42
  17.2 4.6 %fusion.31 = f32[32,1,1024]{2,1,0:T(1,128)S(1)} fusion(bf16[32,128,1024]{2,1,0:T(8,128)(2,1)} %bitcast.65, bf16[32,128,1]{1,0,2:T(8,128)(2,1)S(1)} %convert_bitcast_fusion), kind=kOutput, calls=%fused_computation.47 | convolution fusion | flops 8388608 | bytes 8527872 | tf_op jit(solution)/shard_map/bi,bid->bd/dot_general | solution.py:50
  23.1 5.2 %all-to-all-start = ((f32[4,1,1024]{2,1,0:T(1,128)}), f32[4,1,1024]{2,1,0:T(1,128)S(1)}, u32[]{:S(2)}, u32[]{:S(2)}) async-start(f32[4,1,1024]{2,1,0:T(1,128)} %copy.12), calls=%async_computation | async-start | bytes 32768 | tf_op jit(solution)/shard_map/all_to_all | solution.py:78
  36.0 3.2 %all-to-all-start.1 = ((f32[4,1,1]{2,1,0:T(1,128)}), f32[4,1,1]{2,1,0:T(1,128)S(1)}, u32[]{:S(2)}, u32[]{:S(2)}) async-start(f32[4,1,1]{2,1,0:T(1,128)} %copy.13), calls=%async_computation.1 | async-start | bytes 4096 | tf_op jit(solution)/shard_map/all_to_all | solution.py:79
  39.5 4.2 %all-to-all-done.1 = f32[4,1,1]{2,1,0:T(1,128)S(1)} async-done(((f32[4,1,1]{2,1,0:T(1,128)}), f32[4,1,1]{2,1,0:T(1,128)S(1)}, u32[]{:S(2)}, u32[]{:S(2)}) %all-to-all-start.1) | async-done | bytes 48 | tf_op jit(solution)/shard_map/all_to_all | solution.py:79
  44.1 14.5 %psum.15 = f32[512]{0:T(512)S(1)} all-reduce(f32[512]{0:T(512)S(1)} %add.82), channel_id=1, replica_groups=mesh['grp'=4,'row'=8] {'row'}, use_global_device_ids=true, to_apply=%region_6.7 | all-reduce | flops 512 | bytes 4096 | tf_op jit(solution)/shard_map/psum | solution.py:91
  58.6 41.5 %all-reduce.2.cloned.1.call-done = f32[512,1024]{1,0:T(8,128)} async-done(((f32[512,1024]{1,0:T(8,128)}), f32[512,1024]{1,0:T(8,128)}) %all-reduce.2.cloned.1.call-update) | async-done | bytes 2097168 | tf_op jit(solution)/shard_map/psum | solution.py:91
  100.1 3.1 %divide_convert_fusion = bf16[512,1024]{1,0:T(8,128)(2,1)} fusion(f32[512,1024]{1,0:T(8,128)} %all-reduce.2.cloned.1.call-done, bf16[512,1024]{1,0:T(8,128)(2,1)S(1)} %copy-done.1, f32[512]{0:T(512)S(1)} %broadcast_add_fusion), kind=kLoop, calls=%fused_computation.18 | loop fusion | flops 2621440 | bytes 4196352 | tf_op jit(solution)/shard_map/convert_element_type | solution.py:15
  103.3 7.4 %broadcast_multiply_fusion = bf16[32,128,1024]{2,1,0:T(8,128)(2,1)} fusion(bf16[32,128,1024]{2,1,0:T(8,128)(2,1)} %bitcast.66, bf16[32,128]{1,0:T(8,128)(2,1)S(1)} %convert_element_type.35), kind=kLoop, calls=%fused_computation.17 | loop fusion | flops 4194304 | bytes 16785408 | tf_op jit(solution)/shard_map/mul | solution.py:41
  112.3 43.4 %all-gather.2.cloned.1.call-done = bf16[2048,1024]{1,0:T(8,128)(2,1)} async-done(((bf16[512,1024]{1,0:T(8,128)(2,1)}), bf16[2048,1024]{1,0:T(8,128)(2,1)}) %all-gather.2.cloned.1.call-update) | async-done | bytes 4194320 | tf_op jit(solution)/shard_map/all_gather | solution.py:94
  155.8 3.1 %multiply_reduce_fusion = f32[2048]{0:T(1024)S(1)} fusion(bf16[2048,1024]{1,0:T(8,128)(2,1)} %all-gather.2.cloned.1.call-done), kind=kLoop, calls=%fused_computation.16 | loop fusion | flops 6289408 | bytes 4202496 | tf_op jit(solution)/shard_map/reduce_sum | solution.py:95
  158.8 122.6 %while.10 = (s32[]{:T(128)}, f32[32,128,512]{2,1,0:T(8,128)}, bf16[32,128,1024]{2,1,0:T(8,128)(2,1)}, s32[32]{0:T(128)S(1)}, bf16[2048,1024]{1,0:T(8,128)(2,1)},...) while((s32[]{:T(128)}, f32[32,128,512]{2,1,0:T(8,128)}, ...), condition=%wide.region_9.10_spmd, body=%wide.region_8.9_spmd.sunk | while | flops 134414464 | bytes 1582263 | solution.py:104
  160.2 2.5 fusion.56
  164.0 2.5 fusion.56
  167.8 2.5 fusion.56
  171.7 2.5 fusion.56
  175.5 2.5 fusion.56
  179.3 2.5 fusion.56
  183.2 2.5 fusion.56
  187.0 2.5 fusion.56
  190.8 2.5 fusion.56
  194.7 2.5 fusion.56
  198.5 2.5 fusion.56
  202.3 2.5 fusion.56
  206.2 2.5 fusion.56
  210.0 2.5 fusion.56
  213.8 2.5 fusion.56
  217.7 2.5 fusion.56
  221.5 2.5 fusion.56
  256.0 2.5 fusion.56
  259.8 2.5 fusion.56
  263.6 2.5 fusion.56
  (158 shorter events, 67.6 us)
Async XLA Ops:
  7.2 0.7 copy-start
  21.8 78.3 %copy-start.1 = (bf16[512,1024]{1,0:T(8,128)(2,1)S(1)}, bf16[512,1024]{1,0:T(8,128)(2,1)}, u32[]{:S(2)}) copy-start(bf16[512,1024]{1,0:T(8,128)(2,1)} %param.13) | copy-start | bytes 3145732
  23.1 9.9 %all-to-all-start = ((f32[4,1,1024]{2,1,0:T(1,128)}), f32[4,1,1024]{2,1,0:T(1,128)S(1)}, u32[]{:S(2)}, u32[]{:S(2)}) async-start(f32[4,1,1024]{2,1,0:T(1,128)} %copy.12), calls=%async_computation | async-start | bytes 32768 | tf_op jit(solution)/shard_map/all_to_all | solution.py:78
  28.2 71.9 %all-reduce.2.cloned.1.call-start = ((), (), s32[]{:S(2)}) async-start(), calls=%async_computation.2 | async-start | bytes 4194304 | tf_op jit(solution)/shard_map/psum | solution.py:91
  36.0 7.8 %all-to-all-start.1 = ((f32[4,1,1]{2,1,0:T(1,128)}), f32[4,1,1]{2,1,0:T(1,128)S(1)}, u32[]{:S(2)}, u32[]{:S(2)}) async-start(f32[4,1,1]{2,1,0:T(1,128)} %copy.13), calls=%async_computation.1 | async-start | bytes 4096 | tf_op jit(solution)/shard_map/all_to_all | solution.py:79
  39.2 116.5 %all-gather.2.cloned.1.call-start = ((), (), s32[]{:S(2)}) async-start(), calls=%async_computation.3 | async-start | bytes 5242880 | tf_op jit(solution)/shard_map/all_gather | solution.py:94
Sparse Core Ops, SparseCore 0:
  35.4 64.6 all-reduce.1
  103.4 52.3 all-gather.1
where the time goes:
time: 290 us; the launch traced here: 288 us
  waiting for transfers between devices  91.4 us (32%)
  matrix products  88.5 us (31%)
  local copies, waits for them, and re-layouts  33.1 us (11%)
  loops' own time  20 us (7%)
  other arithmetic  18.2 us (6%)
  blocking collectives  14.5 us (5%)
  between operations  14.2 us (5%)
  starting transfers between devices  8.43 us (3%)
    dot_general x32, matrix products, score_rows(): lax.dot_general(rows, table, (((1,), (1,)), ((), ())), preferred_element_...  80.2 us
    all_gather x1, waiting for transfers between devices, local(): tables = lax.all_gather(table, 'grp', axis=0, tiled=True)  43.4 us
    psum x1, waiting for transfers between devices, local(): all_sums, all_totals = lax.psum((sums, totals), 'row')  41.5 us
    another operation x1, loops' own time, local(): scores = lax.map(one_block, (masked, alive, mine_groups))  20 us
    dynamic_slice x32, local copies, waits for them, and re-layouts, local(): scores = lax.map(one_block, (masked, alive, mine_groups))  19.5 us
    psum x1, blocking collectives, local(): all_sums, all_totals = lax.psum((sums, totals), 'row')  14.5 us
    mul x1, other arithmetic, local(): masked = row_blocks * alive_half[:, :, None]  7.45 us
    gather x1, local copies, waits for them, and re-layouts, local(): homes = jnp.take(home_pos, block_list)  6.15 us
  transfers between devices with their start and end apart: 4, of which 4 were waited for; matrix products, arithmetic and copies ran while one was open for 4% of the time, Pallas kernels for 0%

commit v1 on v0

v1 whole, which is shorter than its diff:
```python
import functools
import math

import jax
import jax.numpy as jnp
from jax import lax
from jax.experimental import pallas as pl
from jax.experimental.pallas import tpu as pltpu
from jax.sharding import PartitionSpec as P

PRIOR = 16
MIB = 1 << 20
F32 = jnp.float32
BF16 = jnp.bfloat16
ROW_DIMS = (((1,), (1,)), ((), ()))
COL_DIMS = (((0,), (0,)), ((), ()))
VMEM = pl.BlockSpec(memory_space=pltpu.VMEM)
SMEM = pl.BlockSpec(memory_space=pltpu.SMEM)
HBM = pl.BlockSpec(memory_space=pl.ANY)


def peer(index, step, size):
    if size & (size - 1) == 0:
        return index ^ step
    return (index + step) % size


def power(exponent):
    return jnp.exp2(exponent).astype(BF16).astype(F32)


def iota(shape, dim):
    return lax.broadcasted_iota(jnp.int32, shape, dim)


def movers_kernel(
    n_groups, lists_group, list_ref, pos_ref, counts_ref, keep_ref, vec_ref, alive_ref, meta_ref, picks_ref, *rest
):
    steps = n_groups - 1
    head_refs, row_refs, (held, sems) = rest[:steps], rest[steps : 2 * steps], rest[2 * steps :]
    blocks, block = keep_ref.shape
    group = lax.axis_index("grp")
    base = (group * lax.axis_size("row") + lax.axis_index("row")) * blocks
    lane = iota((1, block), 1)
    row = iota((blocks, block), 0)
    slots = jnp.full((1, block), -1, jnp.int32)
    filled = jnp.zeros((blocks, block), jnp.int32)
    picks = [jnp.int32(-1)] * steps
    homes = [jnp.int32(-1)] * steps
    for b in range(blocks):
        home = pos_ref[list_ref[base + b]]
        home_group = home // lists_group
        slot = home - home_group * lists_group
        slots = jnp.where((lane == b) & (home_group == group), slot, slots)
        filled = jnp.where(row == b, counts_ref[b], filled)
        for k in range(steps):
            hit = home_group == peer(group, k + 1, n_groups)
            picks[k] = jnp.where(hit, b, picks[k])
            homes[k] = jnp.where(hit, slot, homes[k])
    fetches = []
    for k in range(steps):
        picks_ref[k] = picks[k]
        start = pl.multiple_of(jnp.maximum(picks[k], 0) * block, block)
        fetches.append(pltpu.make_async_copy(vec_ref.at[pl.ds(start, block), :], held.at[k], sems.at[k]))
        fetches[k].start()
    alive = keep_ref[...].astype(F32) * (iota((blocks, block), 1) < filled).astype(F32)
    alive_ref[...] = alive
    ones = jnp.ones((8, block), BF16)
    block_counts = lax.dot_general(ones, alive.astype(BF16), ROW_DIMS, preferred_element_type=F32)
    meta_ref[...] = jnp.zeros_like(meta_ref)
    meta_ref[0:1, :] = slots.astype(F32)
    meta_ref[1:2, 0:blocks] = block_counts[0:1, :]
    stores = []
    for k in range(steps):
        fetches[k].wait()
        stores.append(pltpu.make_async_copy(held.at[k], row_refs[k], sems.at[steps + k]))
        stores[k].start()
        weights = alive_ref[pl.ds(jnp.maximum(picks[k], 0), 1), :]
        wide = jnp.broadcast_to(weights, (16, block)).astype(BF16)
        total = jnp.dot(wide, held[k], preferred_element_type=F32)
        for j in range(total.shape[1] // 128):
            head_refs[k][j : j + 1, :] = total[0:1, j * 128 : (j + 1) * 128]
        tail = total.shape[1] // 128
        head_refs[k][tail : tail + 8, :] = jnp.concatenate(
            [
                jnp.broadcast_to(jnp.sum(weights, axis=1, keepdims=True), (1, 128)),
                jnp.broadcast_to(homes[k].astype(F32), (1, 128)),
                jnp.zeros((6, 128), F32),
            ],
            axis=0,
        )
    for k in range(steps):
        stores[k].wait()


def movers(n_groups, lists_group, block_list, home_pos, counts, keep, vectors):
    steps = n_groups - 1
    blocks, block = keep.shape
    width = vectors.shape[1]
    outs = pl.pallas_call(
        functools.partial(movers_kernel, n_groups, lists_group),
        out_shape=[
            jax.ShapeDtypeStruct((blocks, block), F32),
            jax.ShapeDtypeStruct((8, block), F32),
            jax.ShapeDtypeStruct((steps,), jnp.int32),
        ]
        + [jax.ShapeDtypeStruct((width // 128 + 8, 128), F32)] * steps
        + [jax.ShapeDtypeStruct((block, width), BF16)] * steps,
        in_specs=[SMEM, SMEM, SMEM, VMEM, HBM],
        out_specs=[VMEM, VMEM, SMEM] + [VMEM] * steps + [HBM] * steps,
        scratch_shapes=[pltpu.VMEM((steps, block, width), BF16), pltpu.SemaphoreType.DMA((2 * steps,))],
        compiler_params=pltpu.CompilerParams(vmem_limit_bytes=16 * MIB),
        cost_estimate=pl.CostEstimate(
            flops=2 * steps * block * width, bytes_accessed=6 * steps * block * width, transcendentals=0
        ),
        name="movers",
    )(block_list, home_pos, counts, keep, vectors)
    return outs[0], outs[1], outs[2], outs[3 : 3 + steps], outs[3 + steps :]


def sums_kernel(alive_ref, vec_ref, sums_ref):
    tile_blocks, block = alive_ref.shape
    alive = alive_ref[...]
    row = iota((tile_blocks, block), 0)
    spread = jnp.concatenate([jnp.where(row == j, alive, 0.0) for j in range(tile_blocks)], axis=1)
    sums_ref[...] = jnp.dot(spread.astype(BF16), vec_ref[...], preferred_element_type=F32)


def block_sums(alive, vectors):
    blocks, block = alive.shape
    rows, width = vectors.shape
    tile = 8
    return pl.pallas_call(
        sums_kernel,
        out_shape=jax.ShapeDtypeStruct((blocks, width), F32),
        grid=(blocks // tile,),
        in_specs=[
            pl.BlockSpec((tile, block), lambda t: (t, 0)),
            pl.BlockSpec((tile * block, width), lambda t: (t, 0)),
        ],
        out_specs=pl.BlockSpec((tile, width), lambda t: (t, 0)),
        compiler_params=pltpu.CompilerParams(vmem_limit_bytes=24 * MIB),
        cost_estimate=pl.CostEstimate(
            flops=2 * tile * rows * width, bytes_accessed=2 * rows * width, transcendentals=0
        ),
        name="block_sums",
    )(alive, vectors)


def pack_kernel(meta_ref, sums_ref, *rest):
    heads, out_ref = rest[:-1], rest[-1]
    blocks, width = sums_ref.shape
    rows = out_ref.shape[0]
    chunks = width // 128
    lane = iota((1, 128), 1)
    slots, counts = meta_ref[0:1, :], meta_ref[1:2, :]
    arrived = []
    for k, head in enumerate(heads):
        arrived.append(jnp.concatenate([head[j : j + 1, :] for j in range(chunks)], axis=1))
        slots = jnp.where(lane == blocks + k, head[chunks + 1 : chunks + 2, :], slots)
        counts = jnp.where(lane == blocks + k, head[chunks : chunks + 1, :], counts)
    spare = rows - blocks - len(heads)
    values = jnp.concatenate([sums_ref[...]] + arrived + [jnp.zeros((spare, width), F32)], axis=0)
    largest = jnp.maximum(jnp.max(jnp.abs(values), axis=1, keepdims=True), 2.0**-80)
    exponent = jnp.ceil(jnp.log2(largest) + 0.001) - 15.0
    coded = jnp.round(values * power(-exponent))
    column = jnp.concatenate(
        [jnp.broadcast_to(exponent, (rows, 128)), jnp.zeros((128 - rows, 128), F32)], axis=0
    )
    exponents = jnp.transpose(column)[0:1, :]
    extra = jnp.concatenate([slots, counts, exponents], axis=0)
    extra = jnp.concatenate([extra, jnp.zeros((3, width - 128), F32)], axis=1)
    coded = jnp.concatenate([coded[: rows - 3], extra], axis=0)
    out_ref[...] = coded.astype(jnp.int32).astype(jnp.int16)


def pack(meta, sums, heads):
    blocks, width = sums.shape
    rows = -(-(blocks + len(heads) + 3) // 8) * 8
    return pl.pallas_call(
        pack_kernel,
        out_shape=jax.ShapeDtypeStruct((rows, width), jnp.int16),
        in_specs=[VMEM] * (2 + len(heads)),
        out_specs=VMEM,
        compiler_params=pltpu.CompilerParams(vmem_limit_bytes=16 * MIB),
        cost_estimate=pl.CostEstimate(flops=8 * rows * width, bytes_accessed=6 * rows * width, transcendentals=0),
        name="pack",
    )(meta, sums, *heads)


def table_kernel(n_own, n_steps, *refs):
    own, far, old_ref = refs[:n_own], refs[n_own], refs[n_own + 1]
    row_refs = refs[n_own + 2 : n_own + 2 + n_steps]
    table_ref, norms_ref, share_ref = refs[n_own + 2 + n_steps : n_own + 5 + n_steps]
    part_refs = refs[n_own + 5 + n_steps :]
    lists, width = old_ref.shape
    rows = own[0].shape[0]
    coded = [ref[...].astype(jnp.int32) for ref in own]
    far_all = far[...].astype(jnp.int32)
    coded += [far_all[j * rows : (j + 1) * rows] for j in range(far.shape[0] // rows)]
    sources = len(coded)
    spot = iota((rows, lists), 1)
    high, low, pick_high, pick_low, hits, counts = [], [], [], [], [], []
    for values in coded:
        extra = values[rows - 3 : rows, 0:128].astype(F32)
        turned = jnp.transpose(jnp.concatenate([extra, jnp.zeros((125, 128), F32)], axis=0))
        valid = iota((rows, 1), 0) < rows - 3
        slot = jnp.where(valid, turned[0:rows, 0:1], -1.0).astype(jnp.int32)
        hit = spot == slot
        scale = power(turned[0:rows, 2:3])
        hits.append(jnp.where(hit, 1.0, 0.0).astype(BF16))
        pick_high.append(jnp.where(hit, scale * 256.0, 0.0).astype(BF16))
        pick_low.append(jnp.where(hit, scale, 0.0).astype(BF16))
        counts.append(jnp.broadcast_to(turned[0:rows, 1:2], (rows, 128)).astype(BF16))
        high.append((values >> 8).astype(F32).astype(BF16))
        low.append((values & 255).astype(F32).astype(BF16))
    totals = lax.dot_general(
        jnp.concatenate(hits, axis=0), jnp.concatenate(counts, axis=0), COL_DIMS, preferred_element_type=F32
    )
    sums = lax.dot_general(
        jnp.concatenate(pick_high + pick_low, axis=0),
        jnp.concatenate(high + low, axis=0),
        COL_DIMS,
        preferred_element_type=F32,
    )
    prior = 1.0 * PRIOR
    weight = totals[:, 0:1] + prior
    table = ((sums + prior * old_ref[...].astype(F32)) / weight).astype(BF16)
    table_ref[...] = table
    share = share_ref.shape[0]
    start = pl.multiple_of(lax.axis_index("row") * share, share)
    share_ref[...] = table_ref[pl.ds(start, share), :]
    squares = jnp.square(table.astype(F32))
    head = squares.astype(BF16)
    tail = (squares - head.astype(F32)).astype(BF16)
    ones = jnp.ones((16, width), BF16)
    norms = lax.dot_general(ones, head, ROW_DIMS, preferred_element_type=F32)
    norms = norms + lax.dot_general(ones, tail, ROW_DIMS, preferred_element_type=F32)
    norms_ref[...] = norms[0:8]
    factor = 1.0 / math.sqrt(width)
    for row_ref, part_ref in zip(row_refs, part_refs):
        dots = lax.dot_general(row_ref[...], table, ROW_DIMS, preferred_element_type=F32)
        part_ref[...] = ((2.0 * dots - norms[0:1, :]) * factor).astype(part_ref.dtype)


def make_table(n_rows, own, far, old, rows):
    lists, width = old.shape
    return pl.pallas_call(
        functools.partial(table_kernel, len(own), len(rows)),
        out_shape=[
            jax.ShapeDtypeStruct((lists, width), BF16),
            jax.ShapeDtypeStruct((8, lists), F32),
            jax.ShapeDtypeStruct((lists // n_rows, width), BF16),
        ]
        + [jax.ShapeDtypeStruct((r.shape[0], lists), BF16) for r in rows],
        in_specs=[VMEM] * (len(own) + 2 + len(rows)),
        out_specs=[VMEM] * (3 + len(rows)),
        compiler_params=pltpu.CompilerParams(vmem_limit_bytes=40 * MIB),
        cost_estimate=pl.CostEstimate(
            flops=2 * lists * width * (1000), bytes_accessed=8 * lists * width, transcendentals=0
        ),
        name="table",
    )(*own, far, old, *rows)


def turned_weights(weights):
    return jnp.transpose(jnp.broadcast_to(weights, (128, 128)))


def scores_kernel(alive_ref, norms_ref, table_ref, vec_ref, out_ref):
    tile_blocks, block = alive_ref.shape
    lists, width = table_ref.shape
    factor = 1.0 / math.sqrt(width)
    norms = norms_ref[0:1, :]
    for j in range(tile_blocks):
        at = slice(j * block, (j + 1) * block)
        dots = lax.dot_general(vec_ref[at, :], table_ref[...], ROW_DIMS, preferred_element_type=F32)
        weights = jnp.concatenate([turned_weights(alive_ref[j : j + 1, :])] * (lists // 128), axis=1)
        out_ref[at, :] = (2.0 * dots - norms) * factor * weights


def scores_of(alive, norms, table, vectors):
    blocks, block = alive.shape
    rows, width = vectors.shape
    lists = table.shape[0]
    tile = 8
    return pl.pallas_call(
        scores_kernel,
        out_shape=jax.ShapeDtypeStruct((rows, lists), F32),
        grid=(blocks // tile,),
        in_specs=[
            pl.BlockSpec((tile, block), lambda t: (t, 0)),
            pl.BlockSpec((8, lists), lambda t: (0, 0)),
            pl.BlockSpec((lists, width), lambda t: (0, 0)),
            pl.BlockSpec((tile * block, width), lambda t: (t, 0)),
        ],
        out_specs=pl.BlockSpec((tile * block, lists), lambda t: (t, 0)),
        compiler_params=pltpu.CompilerParams(vmem_limit_bytes=32 * MIB),
        cost_estimate=pl.CostEstimate(
            flops=2 * lists * rows * width, bytes_accessed=2 * rows * width + 4 * rows * lists, transcendentals=0
        ),
        name="scores",
    )(alive, norms, table, vectors)


def merge_kernel(picks_ref, alive_ref, *refs):
    steps = picks_ref.shape[0]
    parts, out_ref, held, sems = refs[:steps], refs[steps + 1], refs[steps + 2], refs[steps + 3]
    block, lists = parts[0].shape
    for k in range(steps):
        pick = picks_ref[k]

        @pl.when(pick >= 0)
        def _():
            weights = turned_weights(alive_ref[pl.ds(pick, 1), :])
            weights = jnp.concatenate([weights] * (lists // 128), axis=1)
            held[k] = parts[k][...].astype(F32) * weights
            start = pl.multiple_of(pick * block, block)
            pltpu.make_async_copy(held.at[k], out_ref.at[pl.ds(start, block), :], sems.at[k]).start()

    for k in range(steps):
        pick = picks_ref[k]

        @pl.when(pick >= 0)
        def _():
            start = pl.multiple_of(pick * block, block)
            pltpu.make_async_copy(held.at[k], out_ref.at[pl.ds(start, block), :], sems.at[k]).wait()


def merge(picks, alive, parts, scores):
    steps = len(parts)
    block, lists = parts[0].shape
    return pl.pallas_call(
        merge_kernel,
        out_shape=jax.ShapeDtypeStruct(scores.shape, scores.dtype),
        in_specs=[SMEM, VMEM] + [VMEM] * steps + [HBM],
        out_specs=HBM,
        scratch_shapes=[pltpu.VMEM((steps, block, lists), F32), pltpu.SemaphoreType.DMA((steps,))],
        input_output_aliases={2 + steps: 0},
        compiler_params=pltpu.CompilerParams(vmem_limit_bytes=16 * MIB),
        cost_estimate=pl.CostEstimate(
            flops=2 * steps * block * lists, bytes_accessed=6 * steps * block * lists, transcendentals=0
        ),
        name="merge",
    )(picks, alive, *parts, scores)


def local(vectors, keep_bits, counts, block_list, home_pos, old_centroids):
    n_groups = lax.axis_size("grp")
    n_rows = lax.axis_size("row")
    blocks = counts.shape[0]
    block = vectors.shape[0] // blocks
    lists_group = old_centroids.shape[0]
    keep = keep_bits.reshape(blocks, block)
    there = [[(i, peer(i, k, n_groups)) for i in range(n_groups)] for k in range(1, n_groups)]
    back = [[(j, i) for i, j in pairs] for pairs in there]

    alive, meta, picks, heads, rows = movers(
        n_groups, lists_group, block_list, home_pos, counts, keep, vectors
    )
    heads = [lax.ppermute(x, "grp", pairs) for x, pairs in zip(heads, there)]
    rows = [lax.ppermute(x, "grp", pairs) for x, pairs in zip(rows, there)]
    sums = block_sums(alive, vectors)
    mine = pack(meta, sums, heads)
    chips = n_rows // 2
    own = [mine]
    for k in range(chips - 1, 0, -1):
        pairs = [(i, 2 * peer(i // 2, k, chips) + i % 2) for i in range(n_rows)]
        own.append(lax.ppermute(mine, "row", pairs))
    far = lax.ppermute(jnp.concatenate(own, axis=0), "row", [(i, i ^ 1) for i in range(n_rows)])
    table, norms, share, *parts = make_table(n_rows, own, far, old_centroids, rows)
    parts = [lax.ppermute(x, "grp", pairs) for x, pairs in zip(parts, back)]
    scores = scores_of(alive, norms, table, vectors)
    scores = merge(picks, alive, parts, scores)
    return (share, scores)


def solution(mesh):
    in_specs = (
        P(("grp", "row"), None),
        P(("grp", "row")),
        P(("grp", "row")),
        P(),
        P(),
        P("grp", None),
    )
    out_specs = (P(("grp", "row"), None), P(("grp", "row"), None))
    return jax.shard_map(local, mesh=mesh, in_specs=in_specs, out_specs=out_specs, check_vma=False)
```

time: 290 us -> 65.6 us (0.23)
  matrix products: 88.5 us -> 0 us
  waiting for transfers between devices: 91.4 us -> 20 us
  local copies, waits for them, and re-layouts: 33.1 us -> 6.14 us
  Pallas kernels: 0 us -> 22.3 us
  loops' own time: 20 us -> 0 us
  other arithmetic: 18.2 us -> 0.02 us
  blocking collectives: 14.5 us -> 0 us
  between operations: 14.2 us -> 0.69 us
  starting transfers between devices: 8.43 us -> 16.1 us
    dot_general x37 -> x0, matrix products: 88.5 us -> none  [the longest x32 80.2 us: score_rows(): lax.dot_general(rows, table, (((1,), (1,)), ((), ())), preferred_element_...]
    all_gather x1 -> x0, waiting for transfers between devices: 43.4 us -> none  [local(): tables = lax.all_gather(table, 'grp', axis=0, tiled=True)]
    psum x1 -> x0, waiting for transfers between devices: 41.5 us -> none  [local(): all_sums, all_totals = lax.psum((sums, totals), 'row')]
    dynamic_slice x66 -> x0, local copies, waits for them, and re-layouts: 23.7 us -> none  [the longest x32 19.5 us: local(): scores = lax.map(one_block, (masked, alive, mine_groups))]
    pallas_call x0 -> x6, Pallas kernels: none -> 22.3 us  [the longest x1 13.1 us: scores_of(): pl.pallas_call(scores_kernel, out_shape=jax.ShapeDtypeStruct((rows, lists...]
    ppermute x0 -> x13, waiting for transfers between devices: none -> 20 us  [the longest x3 11 us: local(): rows = [lax.ppermute(x, 'grp', pairs) for x, pairs in zip(rows, there)]]
    another operation x1 -> x0, loops' own time: 20 us -> none  [local(): scores = lax.map(one_block, (masked, alive, mine_groups))]
    ppermute x0 -> x13, starting transfers between devices: none -> 16.1 us  [the longest x3 4.54 us: local(): heads = [lax.ppermute(x, 'grp', pairs) for x, pairs in zip(heads, there)]]
  transfers between devices with their start and end apart: 4 -> 13, of which waited for: 4 -> 7; matrix products, arithmetic and copies ran while one was open for 4% -> 0% of each run, Pallas kernels for 0% -> 22%
where the time goes in v1:
time: 65.6 us; the launch traced here: 65.3 us
  Pallas kernels  22.3 us (34%)
  waiting for transfers between devices  20 us (30%)
  starting transfers between devices  16.1 us (25%)
  local copies, waits for them, and re-layouts  6.14 us (9%)
  between operations  0.69 us (1%)
    pallas_call x1, Pallas kernels, scores_of(): pl.pallas_call(scores_kernel, out_shape=jax.ShapeDtypeStruct((rows, lists...  13.1 us
    ppermute x3, waiting for transfers between devices, local(): rows = [lax.ppermute(x, 'grp', pairs) for x, pairs in zip(rows, there)]  11 us
    unnamed x14, local copies, waits for them, and re-layouts  6.14 us
    ppermute x3, waiting for transfers between devices, local(): own.append(lax.ppermute(mine, 'row', pairs))  6.04 us
    ppermute x3, starting transfers between devices, local(): heads = [lax.ppermute(x, 'grp', pairs) for x, pairs in zip(heads, there)]  4.54 us
    ppermute x3, starting transfers between devices, local(): own.append(lax.ppermute(mine, 'row', pairs))  4.42 us
    pallas_call x1, Pallas kernels, make_table(): pl.pallas_call(functools.partial(table_kernel, len(own), len(rows)), out_...  3.58 us
    ppermute x3, starting transfers between devices, local(): rows = [lax.ppermute(x, 'grp', pairs) for x, pairs in zip(rows, there)]  3.55 us
  transfers between devices with their start and end apart: 13, of which 7 were waited for; matrix products, arithmetic and copies ran while one was open for 0% of the time, Pallas kernels for 22%

profile of v1, /device:TPU:0, one launch (start us, length us, event | category | flops | bytes accessed | tf_op | source)
XLA Modules:
  0.0 65.3 jit_solution(8830667925391177922)
XLA Ops:
  0.6 3.4 %copy-done = bf16[4096,1024]{1,0:T(8,128)(2,1)S(1)} copy-done((bf16[4096,1024]{1,0:T(8,128)(2,1)S(1)}, bf16[4096,1024]{1,0:T(8,128)(2,1)}, u32[]{:S(2)}) %copy-start) | copy-done | bytes 8388632
  4.0 0.7 %copy-done.2 = s32[4096]{0:T(1024)S(1)} copy-done((s32[4096]{0:T(1024)S(1)}, s32[4096]{0:T(1024)}, u32[]{:S(2)}) %copy-start.2) | copy-done | bytes 16408
  4.7 0.7 %copy-done.3 = s32[2048]{0:T(1024)S(1)} copy-done((s32[2048]{0:T(1024)S(1)}, s32[2048]{0:T(1024)}, u32[]{:S(2)}) %copy-start.3) | copy-done | bytes 8216
  5.4 0.7 %copy-done.4 = s32[1024]{0:T(1024)S(1)} copy-done((s32[1024]{0:T(1024)S(1)}, s32[1024]{0:T(1024)}, u32[]{:S(2)}) %copy-start.4) | copy-done | bytes 4120
  6.1 0.7 %copy-done.5 = s32[32]{0:T(128)S(1)} copy-done((s32[32]{0:T(128)S(1)}, s32[32]{0:T(128)}, u32[]{:S(2)}) %copy-start.5) | copy-done | bytes 152
  6.8 2.4 %movers.1 = (f32[32,128]{1,0:T(8,128)S(1)}, f32[8,128]{1,0:T(8,128)S(1)}, s32[3]{0:T(128)S(1)}, f32[16,128]{1,0:T(8,128)S(1)}, f32[16,128]{1,0:T(8,128)S(1)}, /*...) custom-call(s32[1024]{0:T(1024)S(1)} %copy-done.4, ...), custom_call_target="tpu_custom_call" | custom-call | flops 786432 | bytes 2359296 | tf_op jit(solution)/shard_map/movers/pallas_call | solution.py:100
  9.2 3.0 %collective-permute-start = (f32[16,128]{1,0:T(8,128)S(1)}, f32[16,128]{1,0:T(8,128)S(1)}, u32[]{:S(2)}, u32[]{:S(2)}) collective-permute-start(f32[16,128]{1,0:T(8,128)S(1)} %get-tuple-element.19), channel_id=1, source_target_pairs={{0,8},{8,0},{16,24},{24,16},{1,9},{9,1},{17,25},{25,17},{2,10},{10... | collective-permute-start | bytes 24584 | tf_op jit(solution)/shard_map/ppermute | solution.py:361
  12.2 1.5 %collective-permute-start.1 = (f32[16,128]{1,0:T(8,128)S(1)}, f32[16,128]{1,0:T(8,128)S(1)}, u32[]{:S(2)}, u32[]{:S(2)}) collective-permute-start(f32[16,128]{1,0:T(8,128)S(1)} %get-tuple-element.20), channel_id=1, source_target_pairs={{0,16},{8,24},{16,0},{24,8},{1,17},{9,25},{17,1},{25,9},{2,18},{10... | collective-permute-start | bytes 24584 | tf_op jit(solution)/shard_map/ppermute | solution.py:361
  13.8 0.0 collective-permute-start.2
  13.8 1.6 %block_sums.1.sums_ref = f32[32,1024]{1,0:T(8,128)S(1)} custom-call(f32[32,128]{1,0:T(8,128)S(1)} %get-tuple-element.18.alive_ref, bf16[4096,1024]{1,0:T(8,128)(2,1)S(1)} %copy-done.1), custom_call_target="tpu_custom_call" | custom-call | flops 67108864 | bytes 8388608 | tf_op jit(solution)/shard_map/block_sums/pallas_call | solution.py:133
  15.3 0.0 collective-permute-done.rest_0_
  15.4 0.5 collective-permute-done.1.rest_1_
  15.9 2.4 %collective-permute-done.2.rest_2_ = f32[16,128]{1,0:T(8,128)S(1)} collective-permute-done((f32[16,128]{1,0:T(8,128)S(1)}, f32[16,128]{1,0:T(8,128)S(1)}, u32[]{:S(2)}, u32[]{:S(2)}) %collective-permute-start.2) | collective-permute-done | bytes 8224 | tf_op jit(solution)/shard_map/ppermute | solution.py:361
  18.3 0.2 pack.1.refs_0_
  18.5 1.6 %collective-permute-start.5 = (s16[40,1024]{1,0:T(8,128)(2,1)S(1)}, s16[40,1024]{1,0:T(8,128)(2,1)S(1)}, u32[]{:S(2)}, u32[]{:S(2)}) collective-permute-start(s16[40,1024]{1,0:T(8,128)(2,1)S(1)} %pack.1.refs_0_), channel_id=1, source_target_pairs={{0,2},{1,3},{2,0},{3,1},{4,6},{5,7},{6,4},{7,5},{8,10},{9,11},{10,... | collective-permute-start | bytes 245768 | tf_op jit(solution)/shard_map/ppermute | solution.py:369
  20.1 2.6 %collective-permute-start.4 = (s16[40,1024]{1,0:T(8,128)(2,1)S(1)}, s16[40,1024]{1,0:T(8,128)(2,1)S(1)}, u32[]{:S(2)}, u32[]{:S(2)}) collective-permute-start(s16[40,1024]{1,0:T(8,128)(2,1)S(1)} %pack.1.refs_0_), channel_id=1, source_target_pairs={{0,4},{1,5},{2,6},{3,7},{4,0},{5,1},{6,2},{7,3},{8,12},{9,13},{10,... | collective-permute-start | bytes 245768 | tf_op jit(solution)/shard_map/ppermute | solution.py:369
  22.7 0.2 collective-permute-start.3
  22.9 0.2 collective-permute-done.5.refs_3_
  23.1 4.1 %collective-permute-done.4.refs_2_ = s16[40,1024]{1,0:T(8,128)(2,1)S(1)} collective-permute-done((s16[40,1024]{1,0:T(8,128)(2,1)S(1)}, s16[40,1024]{1,0:T(8,128)(2,1)S(1)}, u32[]{:S(2)}, u32[]{:S(2)}) %collective-permute-start.4) | collective-permute-done | bytes 81952 | tf_op jit(solution)/shard_map/ppermute | solution.py:369
  27.2 1.8 %collective-permute-done.3.refs_1_ = s16[40,1024]{1,0:T(8,128)(2,1)S(1)} collective-permute-done((s16[40,1024]{1,0:T(8,128)(2,1)S(1)}, s16[40,1024]{1,0:T(8,128)(2,1)S(1)}, u32[]{:S(2)}, u32[]{:S(2)}) %collective-permute-start.3) | collective-permute-done | bytes 81952 | tf_op jit(solution)/shard_map/ppermute | solution.py:369
  29.0 0.1 collective-permute-start.6
  29.0 0.6 collective-permute-start.7
  29.6 0.5 collective-permute-start.8
  30.1 2.4 %collective-permute-start.9 = (bf16[128,1024]{1,0:T(8,128)(2,1)S(1)}, bf16[128,1024]{1,0:T(8,128)(2,1)S(1)}, u32[]{:S(2)}, u32[]{:S(2)}) collective-permute-start(bf16[128,1024]{1,0:T(8,128)(2,1)S(1)} %get-tuple-element.24), channel_id=1, source_target_pairs={{0,24},{8,16},{16,8},{24,0},{1,25},{9,17},{17,9},{25,1},{2,26},{10... | collective-permute-start | bytes 786440 | tf_op jit(solution)/shard_map/ppermute | solution.py:362
  32.6 5.6 %collective-permute-done.7.refs_6_ = bf16[128,1024]{1,0:T(8,128)(2,1)S(1)} collective-permute-done((bf16[128,1024]{1,0:T(8,128)(2,1)S(1)}, bf16[128,1024]{1,0:T(8,128)(2,1)S(1)}, u32[]{:S(2)}, u32[]{:S(2)}) %collective-permute-start.7) | collective-permute-done | bytes 262176 | tf_op jit(solution)/shard_map/ppermute | solution.py:362
  38.2 5.4 %collective-permute-done.8.refs_7_ = bf16[128,1024]{1,0:T(8,128)(2,1)S(1)} collective-permute-done((bf16[128,1024]{1,0:T(8,128)(2,1)S(1)}, bf16[128,1024]{1,0:T(8,128)(2,1)S(1)}, u32[]{:S(2)}, u32[]{:S(2)}) %collective-permute-start.8) | collective-permute-done | bytes 262176 | tf_op jit(solution)/shard_map/ppermute | solution.py:362
  43.6 3.6 %table.1 = (bf16[512,1024]{1,0:T(8,128)(2,1)S(1)}, f32[8,512]{1,0:T(8,128)S(1)}, bf16[64,1024]{1,0:T(8,128)(2,1)}, bf16[128,512]{1,0:T(8,128)(2,1)S(1)}, bf16[12...) custom-call(s16[40,1024]{1,0:T(8,128)(2,1)S(1)} %pack.1.refs_0_, s16[40,1024]{1,0:T(8,128)(2,1)S(1)} %collective-permute-done.3.refs_1_, ...), custom_call_target="tpu_custom_call" | custom-call | flops 1048576000 | bytes 4194304 | tf_op jit(solution)/shard_map/table/pallas_call | solution.py:248
  47.2 1.5 %collective-permute-start.10 = (bf16[128,512]{1,0:T(8,128)(2,1)S(1)}, bf16[128,512]{1,0:T(8,128)(2,1)S(1)}, u32[]{:S(2)}, u32[]{:S(2)}) collective-permute-start(bf16[128,512]{1,0:T(8,128)(2,1)S(1)} %get-tuple-element.27), channel_id=1, source_target_pairs={{8,0},{0,8},{24,16},{16,24},{9,1},{1,9},{25,17},{17,25},{10,2},{2,... | collective-permute-start | bytes 393224 | tf_op jit(solution)/shard_map/ppermute | solution.py:372
  48.7 0.5 collective-permute-start.11
  49.2 1.5 %collective-permute-start.12 = (bf16[128,512]{1,0:T(8,128)(2,1)S(1)}, bf16[128,512]{1,0:T(8,128)(2,1)S(1)}, u32[]{:S(2)}, u32[]{:S(2)}) collective-permute-start(bf16[128,512]{1,0:T(8,128)(2,1)S(1)} %get-tuple-element.29), channel_id=1, source_target_pairs={{24,0},{16,8},{8,16},{0,24},{25,1},{17,9},{9,17},{1,25},{26,2},{18... | collective-permute-start | bytes 393224 | tf_op jit(solution)/shard_map/ppermute | solution.py:372
  50.7 13.1 %scores.1.refs_3_ = f32[4096,512]{1,0:T(8,128)} custom-call(f32[32,128]{1,0:T(8,128)S(1)} %get-tuple-element.18.alive_ref, f32[8,512]{1,0:T(8,128)S(1)} %get-tuple-element.30.norms_ref, bf16[512,1024]{1,0:T(8,128)(2,1)S(1)} %get-tuple-element.31.table_ref, bf16[4096,1024]{1,0:T(8,128)(2,1)S(1)} %copy-done.1), custom_call_target="tpu_custom_call" | custom-call | flops 4294967296 | bytes 16777216 | tf_op jit(solution)/shard_map/scores/pallas_call | solution.py:287
  63.8 1.5 %merge.1 = f32[4096,512]{1,0:T(8,128)} custom-call(s32[3]{0:T(128)S(1)} %get-tuple-element.26.picks_ref, f32[32,128]{1,0:T(8,128)S(1)} %get-tuple-element.18.alive_ref, bf16[128,512]{1,0:T(8,128)(2,1)S(1)} %collective-permute-done.10.refs_0_, bf16[128,512]{1,0:T(8,128)(2,1)S(1)} %collective-permute-done.11.refs_1_, ...), custom_call_target="tpu_custom_call", output_to_operand_aliasing={{}: (5, {})} | custom-call | flops 393216 | bytes 1179648 | tf_op jit(solution)/shard_map/merge/pallas_call | solution.py:333
  (15 shorter events, 0.1 us)
Async XLA Ops:
  0.6 3.4 %copy-start = (bf16[4096,1024]{1,0:T(8,128)(2,1)S(1)}, bf16[4096,1024]{1,0:T(8,128)(2,1)}, u32[]{:S(2)}) copy-start(bf16[4096,1024]{1,0:T(8,128)(2,1)} %vec_ref.5) | copy-start | bytes 25165828
  4.0 0.7 %copy-start.2 = (s32[4096]{0:T(1024)S(1)}, s32[4096]{0:T(1024)}, u32[]{:S(2)}) copy-start(s32[4096]{0:T(1024)} %param.7) | copy-start | bytes 49156
  4.7 0.7 %copy-start.3 = (s32[2048]{0:T(1024)S(1)}, s32[2048]{0:T(1024)}, u32[]{:S(2)}) copy-start(s32[2048]{0:T(1024)} %pos_ref.1) | copy-start | bytes 24580
  5.4 0.7 %copy-start.4 = (s32[1024]{0:T(1024)S(1)}, s32[1024]{0:T(1024)}, u32[]{:S(2)}) copy-start(s32[1024]{0:T(1024)} %list_ref.1) | copy-start | bytes 12292
  6.1 0.7 %copy-start.5 = (s32[32]{0:T(128)S(1)}, s32[32]{0:T(128)}, u32[]{:S(2)}) copy-start(s32[32]{0:T(128)} %counts_ref.1) | copy-start | bytes 388
  6.8 7.0 %copy-start.1 = (bf16[4096,1024]{1,0:T(8,128)(2,1)S(1)}, bf16[4096,1024]{1,0:T(8,128)(2,1)}, u32[]{:S(2)}) copy-start(bf16[4096,1024]{1,0:T(8,128)(2,1)} %vec_ref.5) | copy-start | bytes 25165828
  6.8 36.9 %copy-start.6 = (bf16[512,1024]{1,0:T(8,128)(2,1)S(1)}, bf16[512,1024]{1,0:T(8,128)(2,1)}, u32[]{:S(2)}) copy-start(bf16[512,1024]{1,0:T(8,128)(2,1)} %refs_5_.1) | copy-start | bytes 3145732
  9.2 6.1 %collective-permute-start = (f32[16,128]{1,0:T(8,128)S(1)}, f32[16,128]{1,0:T(8,128)S(1)}, u32[]{:S(2)}, u32[]{:S(2)}) collective-permute-start(f32[16,128]{1,0:T(8,128)S(1)} %get-tuple-element.19), channel_id=1, source_target_pairs={{0,8},{8,0},{16,24},{24,16},{1,9},{9,1},{17,25},{25,17},{2,10},{10... | collective-permute-start | bytes 24584 | tf_op jit(solution)/shard_map/ppermute | solution.py:361
  12.2 3.7 %collective-permute-start.1 = (f32[16,128]{1,0:T(8,128)S(1)}, f32[16,128]{1,0:T(8,128)S(1)}, u32[]{:S(2)}, u32[]{:S(2)}) collective-permute-start(f32[16,128]{1,0:T(8,128)S(1)} %get-tuple-element.20), channel_id=1, source_target_pairs={{0,16},{8,24},{16,0},{24,8},{1,17},{9,25},{17,1},{25,9},{2,18},{10... | collective-permute-start | bytes 24584 | tf_op jit(solution)/shard_map/ppermute | solution.py:361
  13.8 4.5 %collective-permute-start.2 = (f32[16,128]{1,0:T(8,128)S(1)}, f32[16,128]{1,0:T(8,128)S(1)}, u32[]{:S(2)}, u32[]{:S(2)}) collective-permute-start(f32[16,128]{1,0:T(8,128)S(1)} %get-tuple-element.21), channel_id=1, source_target_pairs={{0,24},{8,16},{16,8},{24,0},{1,25},{9,17},{17,9},{25,1},{2,26},{10... | collective-permute-start | bytes 24584 | tf_op jit(solution)/shard_map/ppermute | solution.py:361
  18.5 4.6 %collective-permute-start.5 = (s16[40,1024]{1,0:T(8,128)(2,1)S(1)}, s16[40,1024]{1,0:T(8,128)(2,1)S(1)}, u32[]{:S(2)}, u32[]{:S(2)}) collective-permute-start(s16[40,1024]{1,0:T(8,128)(2,1)S(1)} %pack.1.refs_0_), channel_id=1, source_target_pairs={{0,2},{1,3},{2,0},{3,1},{4,6},{5,7},{6,4},{7,5},{8,10},{9,11},{10,... | collective-permute-start | bytes 245768 | tf_op jit(solution)/shard_map/ppermute | solution.py:369
  20.1 7.1 %collective-permute-start.4 = (s16[40,1024]{1,0:T(8,128)(2,1)S(1)}, s16[40,1024]{1,0:T(8,128)(2,1)S(1)}, u32[]{:S(2)}, u32[]{:S(2)}) collective-permute-start(s16[40,1024]{1,0:T(8,128)(2,1)S(1)} %pack.1.refs_0_), channel_id=1, source_target_pairs={{0,4},{1,5},{2,6},{3,7},{4,0},{5,1},{6,2},{7,3},{8,12},{9,13},{10,... | collective-permute-start | bytes 245768 | tf_op jit(solution)/shard_map/ppermute | solution.py:369
  22.7 6.3 %collective-permute-start.3 = (s16[40,1024]{1,0:T(8,128)(2,1)S(1)}, s16[40,1024]{1,0:T(8,128)(2,1)S(1)}, u32[]{:S(2)}, u32[]{:S(2)}) collective-permute-start(s16[40,1024]{1,0:T(8,128)(2,1)S(1)} %pack.1.refs_0_), channel_id=1, source_target_pairs={{0,6},{1,7},{2,4},{3,5},{4,2},{5,3},{6,0},{7,1},{8,14},{9,15},{10,... | collective-permute-start | bytes 245768 | tf_op jit(solution)/shard_map/ppermute | solution.py:369
  29.0 14.7 %collective-permute-start.6 = (s16[160,1024]{1,0:T(8,128)(2,1)S(1)}, s16[160,1024]{1,0:T(8,128)(2,1)S(1)}, u32[]{:S(2)}, u32[]{:S(2)}) collective-permute-start(s16[160,1024]{1,0:T(8,128)(2,1)S(1)} %pad_add_fusion), channel_id=1, source_target_pairs={{0,1},{1,0},{2,3},{3,2},{4,5},{5,4},{6,7},{7,6},{8,9},{9,8},{10,11... | collective-permute-start | bytes 983048 | tf_op jit(solution)/shard_map/ppermute | solution.py:370
  29.0 9.2 %collective-permute-start.7 = (bf16[128,1024]{1,0:T(8,128)(2,1)S(1)}, bf16[128,1024]{1,0:T(8,128)(2,1)S(1)}, u32[]{:S(2)}, u32[]{:S(2)}) collective-permute-start(bf16[128,1024]{1,0:T(8,128)(2,1)S(1)} %get-tuple-element.22), channel_id=1, source_target_pairs={{0,8},{8,0},{16,24},{24,16},{1,9},{9,1},{17,25},{25,17},{2,10},{10... | collective-permute-start | bytes 786440 | tf_op jit(solution)/shard_map/ppermute | solution.py:362
  29.6 14.0 %collective-permute-start.8 = (bf16[128,1024]{1,0:T(8,128)(2,1)S(1)}, bf16[128,1024]{1,0:T(8,128)(2,1)S(1)}, u32[]{:S(2)}, u32[]{:S(2)}) collective-permute-start(bf16[128,1024]{1,0:T(8,128)(2,1)S(1)} %get-tuple-element.23), channel_id=1, source_target_pairs={{0,16},{8,24},{16,0},{24,8},{1,17},{9,25},{17,1},{25,9},{2,18},{10... | collective-permute-start | bytes 786440 | tf_op jit(solution)/shard_map/ppermute | solution.py:362
  30.1 13.5 %collective-permute-start.9 = (bf16[128,1024]{1,0:T(8,128)(2,1)S(1)}, bf16[128,1024]{1,0:T(8,128)(2,1)S(1)}, u32[]{:S(2)}, u32[]{:S(2)}) collective-permute-start(bf16[128,1024]{1,0:T(8,128)(2,1)S(1)} %get-tuple-element.24), channel_id=1, source_target_pairs={{0,24},{8,16},{16,8},{24,0},{1,25},{9,17},{17,9},{25,1},{2,26},{10... | collective-permute-start | bytes 786440 | tf_op jit(solution)/shard_map/ppermute | solution.py:362
  47.2 16.6 %collective-permute-start.10 = (bf16[128,512]{1,0:T(8,128)(2,1)S(1)}, bf16[128,512]{1,0:T(8,128)(2,1)S(1)}, u32[]{:S(2)}, u32[]{:S(2)}) collective-permute-start(bf16[128,512]{1,0:T(8,128)(2,1)S(1)} %get-tuple-element.27), channel_id=1, source_target_pairs={{8,0},{0,8},{24,16},{16,24},{9,1},{1,9},{25,17},{17,25},{10,2},{2,... | collective-permute-start | bytes 393224 | tf_op jit(solution)/shard_map/ppermute | solution.py:372
  48.7 15.1 %collective-permute-start.11 = (bf16[128,512]{1,0:T(8,128)(2,1)S(1)}, bf16[128,512]{1,0:T(8,128)(2,1)S(1)}, u32[]{:S(2)}, u32[]{:S(2)}) collective-permute-start(bf16[128,512]{1,0:T(8,128)(2,1)S(1)} %get-tuple-element.28), channel_id=1, source_target_pairs={{16,0},{24,8},{0,16},{8,24},{17,1},{25,9},{1,17},{9,25},{18,2},{26... | collective-permute-start | bytes 393224 | tf_op jit(solution)/shard_map/ppermute | solution.py:372
  49.2 14.6 %collective-permute-start.12 = (bf16[128,512]{1,0:T(8,128)(2,1)S(1)}, bf16[128,512]{1,0:T(8,128)(2,1)S(1)}, u32[]{:S(2)}, u32[]{:S(2)}) collective-permute-start(bf16[128,512]{1,0:T(8,128)(2,1)S(1)} %get-tuple-element.29), channel_id=1, source_target_pairs={{24,0},{16,8},{8,16},{0,24},{25,1},{17,9},{9,17},{1,25},{26,2},{18... | collective-permute-start | bytes 393224 | tf_op jit(solution)/shard_map/ppermute | solution.py:372

commit v2 on v1

v2 whole, which is shorter than its diff:
```python
import functools
import math

import jax
import jax.numpy as jnp
from jax import lax
from jax.experimental import pallas as pl
from jax.experimental.pallas import tpu as pltpu
from jax.sharding import PartitionSpec as P

PRIOR = 16
MIB = 1 << 20
F32 = jnp.float32
BF16 = jnp.bfloat16
I16 = jnp.int16
I32 = jnp.int32
ROW_DIMS = (((1,), (1,)), ((), ()))
COL_DIMS = (((0,), (0,)), ((), ()))
VMEM = pl.BlockSpec(memory_space=pltpu.VMEM)
SMEM = pl.BlockSpec(memory_space=pltpu.SMEM)
HBM = pl.BlockSpec(memory_space=pltpu.HBM)


def peer(index, step, size):
    if size & (size - 1) == 0:
        return index ^ step
    return (index + step) % size


def power(exponent):
    return jnp.exp2(exponent).astype(BF16).astype(F32)


def iota(shape, dim):
    return lax.broadcasted_iota(I32, shape, dim)


def shaped(shape, dtype):
    return jax.ShapeDtypeStruct(shape, dtype)


def params(mib):
    return pltpu.CompilerParams(vmem_limit_bytes=mib * MIB)


def cost(flops, size):
    return pl.CostEstimate(flops=flops, bytes_accessed=size, transcendentals=0)


def in_hbm(array):
    return pltpu.with_memory_space_constraint(array, pltpu.HBM)


def as_lanes(column):
    rows = column.shape[0]
    wide = jnp.broadcast_to(column, (rows, 128))
    return jnp.transpose(jnp.concatenate([wide, jnp.zeros((128 - rows, 128), F32)], axis=0))[0:1, :]


def coded_rows(values):
    largest = jnp.maximum(jnp.max(jnp.abs(values), axis=1, keepdims=True), 2.0**-80)
    exponent = jnp.ceil(jnp.log2(largest) + 0.001) - 15.0
    return jnp.round(values * power(-exponent)).astype(I32), exponent


def turned_weights(weights):
    return jnp.transpose(jnp.broadcast_to(weights, (128, 128)))


def movers_kernel(n_groups, lists_group, list_ref, pos_ref, counts_ref, keep_ref, vec_ref, *refs):
    steps = n_groups - 1
    alive_ref, meta_ref, picks_ref = refs[:3]
    head_refs, row_refs = refs[3 : 3 + steps], refs[3 + steps : 3 + 2 * steps]
    lists, pos, fill, held, sems = refs[3 + 2 * steps :]
    loads = [
        pltpu.make_async_copy(src, dst, sems.at[steps + i])
        for i, (src, dst) in enumerate([(list_ref, lists), (pos_ref, pos), (counts_ref, fill), (keep_ref, held)])
    ]
    for load in loads:
        load.start()
    blocks, block = keep_ref.shape
    group = lax.axis_index("grp")
    base = (group * lax.axis_size("row") + lax.axis_index("row")) * blocks
    lane = iota((1, block), 1)
    row = iota((blocks, block), 0)
    slots = jnp.full((1, block), -1, I32)
    filled = jnp.zeros((blocks, block), I32)
    picks = [jnp.int32(-1)] * steps
    homes = [jnp.int32(-1)] * steps
    for load in loads:
        load.wait()
    for b in range(blocks):
        home = pos[lists[base + b]]
        home_group = home // lists_group
        slot = home - home_group * lists_group
        slots = jnp.where((lane == b) & (home_group == group), slot, slots)
        for k in range(steps):
            hit = home_group == peer(group, k + 1, n_groups)
            picks[k] = jnp.where(hit, b, picks[k])
            homes[k] = jnp.where(hit, slot, homes[k])
    fetches = []
    for k in range(steps):
        picks_ref[k] = picks[k]
        start = pl.multiple_of(jnp.maximum(picks[k], 0) * block, block)
        fetches.append(pltpu.make_async_copy(vec_ref.at[pl.ds(start, block), :], row_refs[k], sems.at[k]))
        fetches[k].start()
    for b in range(blocks):
        filled = jnp.where(row == b, fill[b], filled)
    alive = held[...].astype(F32) * (iota((blocks, block), 1) < filled).astype(F32)
    alive_ref[...] = alive
    ones = jnp.ones((8, block), BF16)
    block_counts = lax.dot_general(ones, alive.astype(BF16), ROW_DIMS, preferred_element_type=F32)
    meta_ref[...] = jnp.zeros_like(meta_ref)
    meta_ref[0:1, :] = slots.astype(F32)
    meta_ref[1:2, 0:blocks] = block_counts[0:1, :]
    for k in range(steps):
        fetches[k].wait()
        weights = alive_ref[pl.ds(jnp.maximum(picks[k], 0), 1), :]
        wide = jnp.broadcast_to(weights, (16, block)).astype(BF16)
        total = jnp.dot(wide, row_refs[k][...], preferred_element_type=F32)
        chunks = total.shape[1] // 128
        for j in range(chunks):
            head_refs[k][j : j + 1, :] = total[0:1, j * 128 : (j + 1) * 128]
        head_refs[k][chunks : chunks + 8, :] = jnp.concatenate(
            [
                jnp.broadcast_to(jnp.sum(weights, axis=1, keepdims=True), (1, 128)),
                jnp.broadcast_to(homes[k].astype(F32), (1, 128)),
                jnp.zeros((6, 128), F32),
            ],
            axis=0,
        )


def movers(n_groups, lists_group, block_list, home_pos, counts, keep, vectors):
    steps = n_groups - 1
    blocks, block = keep.shape
    width = vectors.shape[1]
    outs = pl.pallas_call(
        functools.partial(movers_kernel, n_groups, lists_group),
        out_shape=[shaped((blocks, block), F32), shaped((8, block), F32), shaped((steps,), I32)]
        + [shaped((width // 128 + 8, 128), F32)] * steps
        + [shaped((block, width), BF16)] * steps,
        in_specs=[HBM] * 5,
        out_specs=[VMEM, VMEM, SMEM] + [VMEM] * (2 * steps),
        scratch_shapes=[
            pltpu.SMEM(block_list.shape, I32),
            pltpu.SMEM(home_pos.shape, I32),
            pltpu.SMEM(counts.shape, I32),
            pltpu.VMEM(keep.shape, I32),
            pltpu.SemaphoreType.DMA((steps + 4,)),
        ],
        compiler_params=params(8),
        cost_estimate=cost(2 * steps * block * width, 6 * steps * block * width),
        name="movers",
    )(*map(in_hbm, (block_list, home_pos, counts, keep, vectors)))
    return outs[0], outs[1], outs[2], outs[3 : 3 + steps], outs[3 + steps :]


def sums_kernel(alive_ref, vec_ref, sums_ref):
    blocks, block = alive_ref.shape
    tile = 8
    row = iota((tile, block), 0)
    for t in range(blocks // tile):
        alive = alive_ref[t * tile : (t + 1) * tile, :]
        spread = jnp.concatenate([jnp.where(row == j, alive, 0.0) for j in range(tile)], axis=1)
        rows = vec_ref[t * tile * block : (t + 1) * tile * block, :]
        sums_ref[t * tile : (t + 1) * tile, :] = jnp.dot(spread.astype(BF16), rows, preferred_element_type=F32)


def block_sums(alive, vectors):
    blocks = alive.shape[0]
    rows, width = vectors.shape
    return pl.pallas_call(
        sums_kernel,
        out_shape=shaped((blocks, width), F32),
        in_specs=[VMEM] * 2,
        out_specs=VMEM,
        compiler_params=params(16),
        cost_estimate=cost(16 * rows * width, 2 * rows * width),
        name="block_sums",
    )(alive, vectors)


def pack_kernel(meta_ref, sums_ref, *refs):
    heads, out_ref = refs[:-1], refs[-1]
    blocks, width = sums_ref.shape
    rows = out_ref.shape[0]
    chunks = width // 128
    lane = iota((1, 128), 1)
    slots, counts = meta_ref[0:1, :], meta_ref[1:2, :]
    arrived = []
    for k, head in enumerate(heads):
        arrived.append(jnp.concatenate([head[j : j + 1, :] for j in range(chunks)], axis=1))
        slots = jnp.where(lane == blocks + k, head[chunks + 1 : chunks + 2, :], slots)
        counts = jnp.where(lane == blocks + k, head[chunks : chunks + 1, :], counts)
    spare = rows - blocks - len(heads)
    coded, exponent = coded_rows(
        jnp.concatenate([sums_ref[...]] + arrived + [jnp.zeros((spare, width), F32)], axis=0)
    )
    extra = jnp.concatenate([slots, counts, as_lanes(exponent)], axis=0).astype(I32)
    extra = jnp.concatenate([extra, jnp.zeros((3, width - 128), I32)], axis=1)
    out_ref[...] = jnp.concatenate([coded[: rows - 3], extra], axis=0).astype(I16)


def pack(meta, sums, heads):
    blocks, width = sums.shape
    rows = blocks + -(-(len(heads) + 3) // 8) * 8
    return pl.pallas_call(
        pack_kernel,
        out_shape=shaped((rows, width), I16),
        in_specs=[VMEM] * (2 + len(heads)),
        out_specs=VMEM,
        compiler_params=params(8),
        cost_estimate=cost(8 * rows * width, 6 * rows * width),
        name="pack",
    )(meta, sums, *heads)


def add_up(sources, blocks, lists):
    rows = sources[0].shape[0]

    def lanes(which, first, last):
        parts = [x[rows - 3 + which : rows - 2 + which, first:last].astype(F32) for x in sources]
        return jnp.concatenate(parts, axis=1)

    picks_high, picks_low, high, low, hits, counts = [], [], [], [], [], []
    for first, last in ((0, blocks), (blocks, rows)):
        values = jnp.concatenate([x[first:last] for x in sources], axis=0)
        hit = iota((lists, values.shape[0]), 0) == lanes(0, first, last).astype(I32)
        scale = power(lanes(2, first, last))
        hits.append(jnp.where(hit, 1.0, 0.0).astype(BF16))
        picks_high.append(jnp.where(hit, scale * 256.0, 0.0).astype(BF16))
        picks_low.append(jnp.where(hit, scale, 0.0).astype(BF16))
        counts.append(jnp.broadcast_to(lanes(1, first, last), (128, values.shape[0])).astype(BF16))
        high.append((values >> 8).astype(F32).astype(BF16))
        low.append((values & 255).astype(F32).astype(BF16))
    totals = lax.dot_general(
        jnp.concatenate(hits, axis=1), jnp.concatenate(counts, axis=1), ROW_DIMS, preferred_element_type=F32
    )
    sums = jnp.dot(
        jnp.concatenate(picks_high + picks_low, axis=1),
        jnp.concatenate(high + low, axis=0),
        preferred_element_type=F32,
    )
    return sums, totals


def prior_kernel(blocks, mine_ref, old_ref, sums_ref, totals_ref):
    lists = old_ref.shape[0]
    prior = 1.0 * PRIOR
    sums, totals = add_up([mine_ref[...].astype(I32)], blocks, lists)
    sums_ref[...] = sums + prior * old_ref[...].astype(F32)
    totals_ref[...] = totals + prior


def with_prior(blocks, mine, old):
    lists, width = old.shape
    return pl.pallas_call(
        functools.partial(prior_kernel, blocks),
        out_shape=[shaped((lists, width), F32), shaped((lists, 128), F32)],
        in_specs=[VMEM] * 2,
        out_specs=[VMEM] * 2,
        compiler_params=params(16),
        cost_estimate=cost(20000 * lists * width, 8 * lists * width),
        name="prior",
    )(mine, old)


def table_kernel(blocks, n_near, *refs):
    near, far = refs[:n_near], refs[n_near]
    sums_ref, totals_ref, table_ref, norms_ref, share_ref = refs[n_near + 1 :]
    lists, width = sums_ref.shape
    rows = near[0].shape[0]
    sources = [ref[...].astype(I32) for ref in near]
    sources += [far[j * rows : (j + 1) * rows, :].astype(I32) for j in range(n_near + 1)]
    sums, totals = add_up(sources, blocks, lists)
    totals = totals_ref[:, 0:1] + totals[:, 0:1]
    table = ((sums_ref[...] + sums) * (1.0 / totals)).astype(BF16)
    table_ref[...] = table
    share = share_ref.shape[0]
    start = pl.multiple_of(lax.axis_index("row") * share, share)
    share_ref[...] = table_ref[pl.ds(start, share), :]
    squares = jnp.square(table.astype(F32))
    partial = squares[:, 0:128]
    for j in range(1, width // 128):
        partial = partial + squares[:, j * 128 : (j + 1) * 128]
    ones = jnp.ones((16, 128), BF16)
    norms = jnp.zeros((16, lists), F32)
    for _ in range(3):
        piece = partial.astype(BF16)
        partial = partial - piece.astype(F32)
        norms = norms + lax.dot_general(ones, piece, ROW_DIMS, preferred_element_type=F32)
    norms_ref[...] = norms[0:8] * (1.0 / math.sqrt(width))


def make_table(n_rows, blocks, near, far, sums, totals):
    lists, width = sums.shape
    return pl.pallas_call(
        functools.partial(table_kernel, blocks, len(near)),
        out_shape=[shaped((lists, width), BF16), shaped((8, lists), F32), shaped((lists // n_rows, width), BF16)],
        in_specs=[VMEM] * (len(near) + 3),
        out_specs=[VMEM] * 3,
        compiler_params=params(24),
        cost_estimate=cost(2000 * lists * width, 8 * lists * width),
        name="table",
    )(*near, far, sums, totals)


def parts_kernel(norms_ref, table_ref, *refs):
    steps = len(refs) // 2
    factor = 1.0 / math.sqrt(table_ref.shape[1])
    norms = norms_ref[0:1, :]
    for row_ref, part_ref in zip(refs[:steps], refs[steps:]):
        dots = lax.dot_general(row_ref[...], table_ref[...], ROW_DIMS, preferred_element_type=F32)
        part_ref[...] = (dots * (2.0 * factor) - norms).astype(part_ref.dtype)


def parts_of(norms, table, rows):
    lists, width = table.shape
    block = rows[0].shape[0]
    return pl.pallas_call(
        parts_kernel,
        out_shape=[shaped((block, lists), BF16)] * len(rows),
        in_specs=[VMEM] * (2 + len(rows)),
        out_specs=[VMEM] * len(rows),
        compiler_params=params(16),
        cost_estimate=cost(2 * len(rows) * block * lists * width, 2 * lists * width),
        name="parts",
    )(norms, table, *rows)


def scores_kernel(alive_ref, norms_ref, table_ref, vec_ref, out_ref, held, sems):
    blocks, block = alive_ref.shape
    lists, width = table_ref.shape
    factor = 1.0 / math.sqrt(width)
    norms = norms_ref[0:1, :]
    table = table_ref[...]
    tile = 4
    stores = []
    for t in range(blocks // tile):
        span = slice(t * tile * block, (t + 1) * tile * block)
        dots = lax.dot_general(vec_ref[span, :], table, ROW_DIMS, preferred_element_type=F32)
        for j in range(tile):
            b = t * tile + j
            weights = jnp.concatenate([turned_weights(alive_ref[b : b + 1, :])] * (lists // 128), axis=1)
            part = dots[j * block : (j + 1) * block, :]
            held[b * block : (b + 1) * block, :] = (part * (2.0 * factor) - norms) * weights
        stores.append(pltpu.make_async_copy(held.at[span, :], out_ref.at[span, :], sems.at[t]))
        stores[t].start()
    for store in stores:
        store.wait()


def scores_of(alive, norms, table, vectors):
    blocks = alive.shape[0]
    rows, width = vectors.shape
    lists = table.shape[0]
    return pl.pallas_call(
        scores_kernel,
        out_shape=shaped((rows, lists), F32),
        in_specs=[VMEM] * 4,
        out_specs=HBM,
        scratch_shapes=[pltpu.VMEM((rows, lists), F32), pltpu.SemaphoreType.DMA((blocks // 4,))],
        compiler_params=params(24),
        cost_estimate=cost(2 * lists * rows * width, 4 * rows * lists),
        name="scores",
    )(alive, norms, table, vectors)


def merge_kernel(picks_ref, alive_ref, *refs):
    steps = picks_ref.shape[0]
    parts, out_ref, held, sems = refs[:steps], refs[steps + 1], refs[steps + 2], refs[steps + 3]
    block, lists = parts[0].shape

    def store(k):
        start = pl.multiple_of(picks_ref[k] * block, block)
        return pltpu.make_async_copy(held.at[k], out_ref.at[pl.ds(start, block), :], sems.at[k])

    for k in range(steps):

        @pl.when(picks_ref[k] >= 0)
        def _():
            weights = turned_weights(alive_ref[pl.ds(picks_ref[k], 1), :])
            weights = jnp.concatenate([weights] * (lists // 128), axis=1)
            held[k] = parts[k][...].astype(F32) * weights
            store(k).start()

    for k in range(steps):

        @pl.when(picks_ref[k] >= 0)
        def _():
            store(k).wait()


def merge(picks, alive, parts, scores):
    steps = len(parts)
    block, lists = parts[0].shape
    return pl.pallas_call(
        merge_kernel,
        out_shape=shaped(scores.shape, scores.dtype),
        in_specs=[SMEM, VMEM] + [VMEM] * steps + [HBM],
        out_specs=HBM,
        scratch_shapes=[pltpu.VMEM((steps, block, lists), F32), pltpu.SemaphoreType.DMA((steps,))],
        input_output_aliases={2 + steps: 0},
        compiler_params=params(8),
        cost_estimate=cost(2 * steps * block * lists, 6 * steps * block * lists),
        name="merge",
    )(picks, alive, *parts, scores)


def local(vectors, keep_bits, counts, block_list, home_pos, old_centroids):
    n_groups = lax.axis_size("grp")
    n_rows = lax.axis_size("row")
    blocks = counts.shape[0]
    block = vectors.shape[0] // blocks
    lists_group = old_centroids.shape[0]
    keep = keep_bits.reshape(blocks, block)
    there = [[(i, peer(i, k, n_groups)) for i in range(n_groups)] for k in range(1, n_groups)]
    back = [[(j, i) for i, j in pairs] for pairs in there]
    chips = n_rows // 2
    along = [[(i, 2 * peer(i // 2, k, chips) + i % 2) for i in range(n_rows)] for k in range(1, chips)]
    cores = [(i, i ^ 1) for i in range(n_rows)]

    alive, meta, picks, heads, rows = movers(n_groups, lists_group, block_list, home_pos, counts, keep, vectors)
    heads = [lax.ppermute(x, "grp", pairs) for x, pairs in zip(heads, there)]
    mine = pack(meta, block_sums(alive, vectors), heads)
    mine, *rows = lax.optimization_barrier((mine, *rows))
    rows = [lax.ppermute(x, "grp", pairs) for x, pairs in zip(rows, there)]
    near = [lax.ppermute(mine, "row", pairs) for pairs in along]
    sums, totals = with_prior(blocks, mine, old_centroids)
    far = lax.ppermute(jnp.concatenate([mine] + near, axis=0), "row", cores)
    table, norms, share = make_table(n_rows, blocks, near, far, sums, totals)
    parts = parts_of(norms, table, rows)
    parts = [lax.ppermute(x, "grp", pairs) for x, pairs in zip(parts, back)]
    scores = scores_of(alive, norms, table, vectors)
    scores = merge(picks, alive, parts, scores)
    return (share, scores)


def solution(mesh):
    in_specs = (
        P(("grp", "row"), None),
        P(("grp", "row")),
        P(("grp", "row")),
        P(),
        P(),
        P("grp", None),
    )
    out_specs = (P(("grp", "row"), None), P(("grp", "row"), None))
    return jax.shard_map(local, mesh=mesh, in_specs=in_specs, out_specs=out_specs, check_vma=False)
```

time: 65.6 us -> 41.7 us (0.64)
  waiting for transfers between devices: 20 us -> 9.65 us
  Pallas kernels: 22.3 us -> 16 us
  local copies, waits for them, and re-layouts: 6.14 us -> 0.01 us
  starting transfers between devices: 16.1 us -> 15 us
    ppermute x3, waiting for transfers between devices: 11 us -> 2.81 us  [local(): rows = [lax.ppermute(x, 'grp', pairs) for x, pairs in zip(rows, there)]]
    pallas_call x5 -> x7, Pallas kernels: 19.9 us -> 12.2 us  [the longest x1 5.59 us: scores_of(): pl.pallas_call(scores_kernel, out_shape=shaped((rows, lists), F32), in_sp...]
    unnamed x14 -> x4, local copies, waits for them, and re-layouts: 6.14 us -> 0.01 us
    ppermute x4, waiting for transfers between devices: 6.04 us -> 3.49 us  [the longest x3 2.42 us: local(): near = [lax.ppermute(mine, 'row', pairs) for pairs in along]]
    pallas_call x1, Pallas kernels: 2.45 us -> 3.83 us  [movers(): pl.pallas_call(functools.partial(movers_kernel, n_groups, lists_group), o...]
    ppermute x3, starting transfers between devices: 3.55 us -> 2.38 us  [local(): rows = [lax.ppermute(x, 'grp', pairs) for x, pairs in zip(rows, there)]]
  transfers between devices with their start and end apart: 13 -> 13, of which waited for: 7 -> 6; matrix products, arithmetic and copies ran while one was open for 0% -> 0% of each run, Pallas kernels for 22% -> 23%
where the time goes in v2:
time: 41.7 us; the launch traced here: 41.4 us
  Pallas kernels  16 us (38%)
  starting transfers between devices  15 us (36%)
  waiting for transfers between devices  9.65 us (23%)
  between operations  0.74 us (2%)
    pallas_call x1, Pallas kernels, scores_of(): pl.pallas_call(scores_kernel, out_shape=shaped((rows, lists), F32), in_sp...  5.59 us
    ppermute x3, starting transfers between devices, local(): heads = [lax.ppermute(x, 'grp', pairs) for x, pairs in zip(heads, there)]  4.54 us
    ppermute x3, starting transfers between devices, local(): near = [lax.ppermute(mine, 'row', pairs) for pairs in along]  4.42 us
    pallas_call x1, Pallas kernels, movers(): pl.pallas_call(functools.partial(movers_kernel, n_groups, lists_group), o...  3.83 us
    ppermute x3, starting transfers between devices, local(): parts = [lax.ppermute(x, 'grp', pairs) for x, pairs in zip(parts, back)]  3.55 us
    ppermute x3, waiting for transfers between devices, local(): heads = [lax.ppermute(x, 'grp', pairs) for x, pairs in zip(heads, there)]  3.33 us
    ppermute x3, waiting for transfers between devices, local(): rows = [lax.ppermute(x, 'grp', pairs) for x, pairs in zip(rows, there)]  2.81 us
    ppermute x3, waiting for transfers between devices, local(): near = [lax.ppermute(mine, 'row', pairs) for pairs in along]  2.42 us
  transfers between devices with their start and end apart: 13, of which 6 were waited for; matrix products, arithmetic and copies ran while one was open for 0% of the time, Pallas kernels for 23%

profile of v2, /device:TPU:0, one launch (start us, length us, event | category | flops | bytes accessed | tf_op | source)
XLA Modules:
  0.0 41.4 jit_solution(2985805960494127043)
XLA Ops:
  0.7 3.8 %movers.1 = (f32[32,128]{1,0:T(8,128)S(1)}, f32[8,128]{1,0:T(8,128)S(1)}, s32[3]{0:T(128)S(1)}, f32[16,128]{1,0:T(8,128)S(1)}, f32[16,128]{1,0:T(8,128)S(1)}, /*...) custom-call(s32[1024]{0:T(1024)} %list_ref.1, ...), custom_call_target="tpu_custom_call" | custom-call | flops 786432 | bytes 2359296 | tf_op jit(solution)/shard_map/movers/pallas_call | solution.py:138
  4.5 3.0 %collective-permute-start = (f32[16,128]{1,0:T(8,128)S(1)}, f32[16,128]{1,0:T(8,128)S(1)}, u32[]{:S(2)}, u32[]{:S(2)}) collective-permute-start(f32[16,128]{1,0:T(8,128)S(1)} %get-tuple-element.25), channel_id=1, source_target_pairs={{0,8},{8,0},{16,24},{24,16},{1,9},{9,1},{17,25},{25,17},{2,10},{10... | collective-permute-start | bytes 24584 | tf_op jit(solution)/shard_map/ppermute | solution.py:425
  7.5 1.5 %collective-permute-start.1 = (f32[16,128]{1,0:T(8,128)S(1)}, f32[16,128]{1,0:T(8,128)S(1)}, u32[]{:S(2)}, u32[]{:S(2)}) collective-permute-start(f32[16,128]{1,0:T(8,128)S(1)} %get-tuple-element.26), channel_id=1, source_target_pairs={{0,16},{8,24},{16,0},{24,8},{1,17},{9,25},{17,1},{25,9},{2,18},{10... | collective-permute-start | bytes 24584 | tf_op jit(solution)/shard_map/ppermute | solution.py:425
  9.0 0.0 collective-permute-start.2
  9.0 1.2 %block_sums.1.sums_ref = f32[32,1024]{1,0:T(8,128)S(1)} custom-call(f32[32,128]{1,0:T(8,128)S(1)} %get-tuple-element.24.alive_ref, bf16[4096,1024]{1,0:T(8,128)(2,1)S(1)} %copy-done), custom_call_target="tpu_custom_call" | custom-call | flops 67108864 | bytes 8388608 | tf_op jit(solution)/shard_map/block_sums/pallas_call | solution.py:173
  10.2 0.0 collective-permute-done.refs_0_
  10.2 0.9 %collective-permute-done.1.refs_1_ = f32[16,128]{1,0:T(8,128)S(1)} collective-permute-done((f32[16,128]{1,0:T(8,128)S(1)}, f32[16,128]{1,0:T(8,128)S(1)}, u32[]{:S(2)}, u32[]{:S(2)}) %collective-permute-start.1) | collective-permute-done | bytes 8224 | tf_op jit(solution)/shard_map/ppermute | solution.py:425
  11.1 2.4 %collective-permute-done.2.refs_2_ = f32[16,128]{1,0:T(8,128)S(1)} collective-permute-done((f32[16,128]{1,0:T(8,128)S(1)}, f32[16,128]{1,0:T(8,128)S(1)}, u32[]{:S(2)}, u32[]{:S(2)}) %collective-permute-start.2) | collective-permute-done | bytes 8224 | tf_op jit(solution)/shard_map/ppermute | solution.py:425
  13.6 0.2 pack.1.mine_ref
  13.7 3.6 %collective-permute-start.5 = (s16[40,1024]{1,0:T(8,128)(2,1)S(1)}, s16[40,1024]{1,0:T(8,128)(2,1)S(1)}, u32[]{:S(2)}, u32[]{:S(2)}) collective-permute-start(s16[40,1024]{1,0:T(8,128)(2,1)S(1)} %pack.1.mine_ref), channel_id=1, source_target_pairs={{0,6},{1,7},{2,4},{3,5},{4,2},{5,3},{6,0},{7,1},{8,14},{9,15},{10,... | collective-permute-start | bytes 245768 | tf_op jit(solution)/shard_map/ppermute | solution.py:429
  17.4 0.0 collective-permute-start.4
  17.4 0.8 %collective-permute-start.3 = (s16[40,1024]{1,0:T(8,128)(2,1)S(1)}, s16[40,1024]{1,0:T(8,128)(2,1)S(1)}, u32[]{:S(2)}, u32[]{:S(2)}) collective-permute-start(s16[40,1024]{1,0:T(8,128)(2,1)S(1)} %pack.1.mine_ref), channel_id=1, source_target_pairs={{0,2},{1,3},{2,0},{3,1},{4,6},{5,7},{6,4},{7,5},{8,10},{9,11},{10,... | collective-permute-start | bytes 245768 | tf_op jit(solution)/shard_map/ppermute | solution.py:429
  18.1 0.5 %collective-permute-start.7 = (bf16[128,1024]{1,0:T(8,128)(2,1)S(1)}, bf16[128,1024]{1,0:T(8,128)(2,1)S(1)}, u32[]{:S(2)}, u32[]{:S(2)}) collective-permute-start(bf16[128,1024]{1,0:T(8,128)(2,1)S(1)} %get-tuple-element.38), channel_id=1, source_target_pairs={{0,8},{8,0},{16,24},{24,16},{1,9},{9,1},{17,25},{25,17},{2,10},{10... | collective-permute-start | bytes 786440 | tf_op jit(solution)/shard_map/ppermute | solution.py:428
  18.7 0.4 collective-permute-start.8
  19.0 1.1 %collective-permute-done.5.refs_2_ = s16[40,1024]{1,0:T(8,128)(2,1)S(1)} collective-permute-done((s16[40,1024]{1,0:T(8,128)(2,1)S(1)}, s16[40,1024]{1,0:T(8,128)(2,1)S(1)}, u32[]{:S(2)}, u32[]{:S(2)}) %collective-permute-start.5) | collective-permute-done | bytes 81952 | tf_op jit(solution)/shard_map/ppermute | solution.py:429
  20.2 1.5 %collective-permute-start.9 = (bf16[128,1024]{1,0:T(8,128)(2,1)S(1)}, bf16[128,1024]{1,0:T(8,128)(2,1)S(1)}, u32[]{:S(2)}, u32[]{:S(2)}) collective-permute-start(bf16[128,1024]{1,0:T(8,128)(2,1)S(1)} %get-tuple-element.40), channel_id=1, source_target_pairs={{0,24},{8,16},{16,8},{24,0},{1,25},{9,17},{17,9},{25,1},{2,26},{10... | collective-permute-start | bytes 786440 | tf_op jit(solution)/shard_map/ppermute | solution.py:428
  21.6 1.3 %collective-permute-done.4.refs_1_ = s16[40,1024]{1,0:T(8,128)(2,1)S(1)} collective-permute-done((s16[40,1024]{1,0:T(8,128)(2,1)S(1)}, s16[40,1024]{1,0:T(8,128)(2,1)S(1)}, u32[]{:S(2)}, u32[]{:S(2)}) %collective-permute-start.4) | collective-permute-done | bytes 81952 | tf_op jit(solution)/shard_map/ppermute | solution.py:429
  23.0 0.0 collective-permute-done.3.refs_0_
  23.0 0.1 collective-permute-start.6
  23.1 0.5 %prior.1 = (f32[512,1024]{1,0:T(8,128)S(1)}, f32[512,128]{1,0:T(8,128)S(1)}) custom-call(s16[40,1024]{1,0:T(8,128)(2,1)S(1)} %pack.1.mine_ref, bf16[512,1024]{1,0:T(8,128)(2,1)S(1)} %copy-done.1), custom_call_target="tpu_custom_call" | custom-call | flops 10485760000 | bytes 4194304 | tf_op jit(solution)/shard_map/prior/pallas_call | solution.py:258
  23.6 1.1 %collective-permute-done.6.refs_3_ = s16[160,1024]{1,0:T(8,128)(2,1)S(1)} collective-permute-done((s16[160,1024]{1,0:T(8,128)(2,1)S(1)}, s16[160,1024]{1,0:T(8,128)(2,1)S(1)}, u32[]{:S(2)}, u32[]{:S(2)}) %collective-permute-start.6) | collective-permute-done | bytes 327712 | tf_op jit(solution)/shard_map/ppermute | solution.py:431
  24.7 2.2 %table.1 = (bf16[512,1024]{1,0:T(8,128)(2,1)S(1)}, f32[8,512]{1,0:T(8,128)S(1)}, bf16[64,1024]{1,0:T(8,128)(2,1)}) custom-call(s16[40,1024]{1,0:T(8,128)(2,1)S(1)} %collective-permute-done.3.refs_0_, s16[40,1024]{1,0:T(8,128)(2,1)S(1)} %collective-permute-done.4.refs_1_, s16[40,1024]{1,0:T(8,128)(2,1)S(1)} %collective-permute-done.5.refs_2_, ...), custom_call_target="tpu_custom_call" | custom-call | flops 1048576000 | bytes 4194304 | tf_op jit(solution)/shard_map/table/pallas_call | solution.py:298
  26.8 0.0 collective-permute-done.7.refs_0_
  26.8 2.8 %collective-permute-done.8.refs_1_ = bf16[128,1024]{1,0:T(8,128)(2,1)S(1)} collective-permute-done((bf16[128,1024]{1,0:T(8,128)(2,1)S(1)}, bf16[128,1024]{1,0:T(8,128)(2,1)S(1)}, u32[]{:S(2)}, u32[]{:S(2)}) %collective-permute-start.8) | collective-permute-done | bytes 262176 | tf_op jit(solution)/shard_map/ppermute | solution.py:428
  29.7 1.2 %parts.1 = (bf16[128,512]{1,0:T(8,128)(2,1)S(1)}, bf16[128,512]{1,0:T(8,128)(2,1)S(1)}, bf16[128,512]{1,0:T(8,128)(2,1)S(1)}) custom-call(f32[8,512]{1,0:T(8,128)S(1)} %get-tuple-element.36.norms_ref, bf16[512,1024]{1,0:T(8,128)(2,1)S(1)} %get-tuple-element.37.table_ref, bf16[128,1024]{1,0:T(8,128)(2,1)S(1)} %collective-permute-done.7.refs_0_, ...), custom_call_target="tpu_custom_call" | custom-call | flops 402653184 | bytes 1048576 | tf_op jit(solution)/shard_map/parts/pallas_call | solution.py:321
  30.8 1.6 %collective-permute-start.10 = (bf16[128,512]{1,0:T(8,128)(2,1)S(1)}, bf16[128,512]{1,0:T(8,128)(2,1)S(1)}, u32[]{:S(2)}, u32[]{:S(2)}) collective-permute-start(bf16[128,512]{1,0:T(8,128)(2,1)S(1)} %get-tuple-element.41), channel_id=1, source_target_pairs={{8,0},{0,8},{24,16},{16,24},{9,1},{1,9},{25,17},{17,25},{10,2},{2,... | collective-permute-start | bytes 393224 | tf_op jit(solution)/shard_map/ppermute | solution.py:434
  32.4 0.5 %collective-permute-start.11 = (bf16[128,512]{1,0:T(8,128)(2,1)S(1)}, bf16[128,512]{1,0:T(8,128)(2,1)S(1)}, u32[]{:S(2)}, u32[]{:S(2)}) collective-permute-start(bf16[128,512]{1,0:T(8,128)(2,1)S(1)} %get-tuple-element.42), channel_id=1, source_target_pairs={{16,0},{24,8},{0,16},{8,24},{17,1},{25,9},{1,17},{9,25},{18,2},{26... | collective-permute-start | bytes 393224 | tf_op jit(solution)/shard_map/ppermute | solution.py:434
  32.9 1.5 %collective-permute-start.12 = (bf16[128,512]{1,0:T(8,128)(2,1)S(1)}, bf16[128,512]{1,0:T(8,128)(2,1)S(1)}, u32[]{:S(2)}, u32[]{:S(2)}) collective-permute-start(bf16[128,512]{1,0:T(8,128)(2,1)S(1)} %get-tuple-element.43), channel_id=1, source_target_pairs={{24,0},{16,8},{8,16},{0,24},{25,1},{17,9},{9,17},{1,25},{26,2},{18... | collective-permute-start | bytes 393224 | tf_op jit(solution)/shard_map/ppermute | solution.py:434
  34.4 5.6 %scores.1.refs_3_ = f32[4096,512]{1,0:T(8,128)} custom-call(f32[32,128]{1,0:T(8,128)S(1)} %get-tuple-element.24.alive_ref, f32[8,512]{1,0:T(8,128)S(1)} %get-tuple-element.36.norms_ref, bf16[512,1024]{1,0:T(8,128)(2,1)S(1)} %get-tuple-element.37.table_ref, bf16[4096,1024]{1,0:T(8,128)(2,1)S(1)} %copy-done), custom_call_target="tpu_custom_call" | custom-call | flops 4294967296 | bytes 8388608 | tf_op jit(solution)/shard_map/scores/pallas_call | solution.py:358
  40.0 0.0 collective-permute-done.11.refs_1_
  40.0 0.0 collective-permute-done.12.refs_2_
  40.0 1.4 %merge.1 = f32[4096,512]{1,0:T(8,128)} custom-call(s32[3]{0:T(128)S(1)} %get-tuple-element.35.picks_ref, f32[32,128]{1,0:T(8,128)S(1)} %get-tuple-element.24.alive_ref, bf16[128,512]{1,0:T(8,128)(2,1)S(1)} %collective-permute-done.10.refs_0_, bf16[128,512]{1,0:T(8,128)(2,1)S(1)} %collective-permute-done.11.refs_1_, ...), custom_call_target="tpu_custom_call", output_to_operand_aliasing={{}: (5, {})} | custom-call | flops 393216 | bytes 1179648 | tf_op jit(solution)/shard_map/merge/pallas_call | solution.py:398
  (7 shorter events, 0.0 us)
Async XLA Ops:
  0.6 8.4 %copy-start = (bf16[4096,1024]{1,0:T(8,128)(2,1)S(1)}, bf16[4096,1024]{1,0:T(8,128)(2,1)}, u32[]{:S(2)}) copy-start(bf16[4096,1024]{1,0:T(8,128)(2,1)} %vec_ref.5) | copy-start | bytes 25165828
  0.6 22.4 %copy-start.1 = (bf16[512,1024]{1,0:T(8,128)(2,1)S(1)}, bf16[512,1024]{1,0:T(8,128)(2,1)}, u32[]{:S(2)}) copy-start(bf16[512,1024]{1,0:T(8,128)(2,1)} %old_ref.1) | copy-start | bytes 3145732
  4.5 5.7 %collective-permute-start = (f32[16,128]{1,0:T(8,128)S(1)}, f32[16,128]{1,0:T(8,128)S(1)}, u32[]{:S(2)}, u32[]{:S(2)}) collective-permute-start(f32[16,128]{1,0:T(8,128)S(1)} %get-tuple-element.25), channel_id=1, source_target_pairs={{0,8},{8,0},{16,24},{24,16},{1,9},{9,1},{17,25},{25,17},{2,10},{10... | collective-permute-start | bytes 24584 | tf_op jit(solution)/shard_map/ppermute | solution.py:425
  7.5 3.7 %collective-permute-start.1 = (f32[16,128]{1,0:T(8,128)S(1)}, f32[16,128]{1,0:T(8,128)S(1)}, u32[]{:S(2)}, u32[]{:S(2)}) collective-permute-start(f32[16,128]{1,0:T(8,128)S(1)} %get-tuple-element.26), channel_id=1, source_target_pairs={{0,16},{8,24},{16,0},{24,8},{1,17},{9,25},{17,1},{25,9},{2,18},{10... | collective-permute-start | bytes 24584 | tf_op jit(solution)/shard_map/ppermute | solution.py:425
  9.0 4.5 %collective-permute-start.2 = (f32[16,128]{1,0:T(8,128)S(1)}, f32[16,128]{1,0:T(8,128)S(1)}, u32[]{:S(2)}, u32[]{:S(2)}) collective-permute-start(f32[16,128]{1,0:T(8,128)S(1)} %get-tuple-element.27), channel_id=1, source_target_pairs={{0,24},{8,16},{16,8},{24,0},{1,25},{9,17},{17,9},{25,1},{2,26},{10... | collective-permute-start | bytes 24584 | tf_op jit(solution)/shard_map/ppermute | solution.py:425
  13.7 6.4 %collective-permute-start.5 = (s16[40,1024]{1,0:T(8,128)(2,1)S(1)}, s16[40,1024]{1,0:T(8,128)(2,1)S(1)}, u32[]{:S(2)}, u32[]{:S(2)}) collective-permute-start(s16[40,1024]{1,0:T(8,128)(2,1)S(1)} %pack.1.mine_ref), channel_id=1, source_target_pairs={{0,6},{1,7},{2,4},{3,5},{4,2},{5,3},{6,0},{7,1},{8,14},{9,15},{10,... | collective-permute-start | bytes 245768 | tf_op jit(solution)/shard_map/ppermute | solution.py:429
  17.4 5.6 %collective-permute-start.4 = (s16[40,1024]{1,0:T(8,128)(2,1)S(1)}, s16[40,1024]{1,0:T(8,128)(2,1)S(1)}, u32[]{:S(2)}, u32[]{:S(2)}) collective-permute-start(s16[40,1024]{1,0:T(8,128)(2,1)S(1)} %pack.1.mine_ref), channel_id=1, source_target_pairs={{0,4},{1,5},{2,6},{3,7},{4,0},{5,1},{6,2},{7,3},{8,12},{9,13},{10,... | collective-permute-start | bytes 245768 | tf_op jit(solution)/shard_map/ppermute | solution.py:429
  17.4 5.6 %collective-permute-start.3 = (s16[40,1024]{1,0:T(8,128)(2,1)S(1)}, s16[40,1024]{1,0:T(8,128)(2,1)S(1)}, u32[]{:S(2)}, u32[]{:S(2)}) collective-permute-start(s16[40,1024]{1,0:T(8,128)(2,1)S(1)} %pack.1.mine_ref), channel_id=1, source_target_pairs={{0,2},{1,3},{2,0},{3,1},{4,6},{5,7},{6,4},{7,5},{8,10},{9,11},{10,... | collective-permute-start | bytes 245768 | tf_op jit(solution)/shard_map/ppermute | solution.py:429
  18.1 8.7 %collective-permute-start.7 = (bf16[128,1024]{1,0:T(8,128)(2,1)S(1)}, bf16[128,1024]{1,0:T(8,128)(2,1)S(1)}, u32[]{:S(2)}, u32[]{:S(2)}) collective-permute-start(bf16[128,1024]{1,0:T(8,128)(2,1)S(1)} %get-tuple-element.38), channel_id=1, source_target_pairs={{0,8},{8,0},{16,24},{24,16},{1,9},{9,1},{17,25},{25,17},{2,10},{10... | collective-permute-start | bytes 786440 | tf_op jit(solution)/shard_map/ppermute | solution.py:428
  18.7 11.0 %collective-permute-start.8 = (bf16[128,1024]{1,0:T(8,128)(2,1)S(1)}, bf16[128,1024]{1,0:T(8,128)(2,1)S(1)}, u32[]{:S(2)}, u32[]{:S(2)}) collective-permute-start(bf16[128,1024]{1,0:T(8,128)(2,1)S(1)} %get-tuple-element.39), channel_id=1, source_target_pairs={{0,16},{8,24},{16,0},{24,8},{1,17},{9,25},{17,1},{25,9},{2,18},{10... | collective-permute-start | bytes 786440 | tf_op jit(solution)/shard_map/ppermute | solution.py:428
  20.2 9.5 %collective-permute-start.9 = (bf16[128,1024]{1,0:T(8,128)(2,1)S(1)}, bf16[128,1024]{1,0:T(8,128)(2,1)S(1)}, u32[]{:S(2)}, u32[]{:S(2)}) collective-permute-start(bf16[128,1024]{1,0:T(8,128)(2,1)S(1)} %get-tuple-element.40), channel_id=1, source_target_pairs={{0,24},{8,16},{16,8},{24,0},{1,25},{9,17},{17,9},{25,1},{2,26},{10... | collective-permute-start | bytes 786440 | tf_op jit(solution)/shard_map/ppermute | solution.py:428
  23.0 1.7 %collective-permute-start.6 = (s16[160,1024]{1,0:T(8,128)(2,1)S(1)}, s16[160,1024]{1,0:T(8,128)(2,1)S(1)}, u32[]{:S(2)}, u32[]{:S(2)}) collective-permute-start(s16[160,1024]{1,0:T(8,128)(2,1)S(1)} %pad_add_fusion), channel_id=1, source_target_pairs={{0,1},{1,0},{2,3},{3,2},{4,5},{5,4},{6,7},{7,6},{8,9},{9,8},{10,11... | collective-permute-start | bytes 983048 | tf_op jit(solution)/shard_map/ppermute | solution.py:431
  30.8 9.2 %collective-permute-start.10 = (bf16[128,512]{1,0:T(8,128)(2,1)S(1)}, bf16[128,512]{1,0:T(8,128)(2,1)S(1)}, u32[]{:S(2)}, u32[]{:S(2)}) collective-permute-start(bf16[128,512]{1,0:T(8,128)(2,1)S(1)} %get-tuple-element.41), channel_id=1, source_target_pairs={{8,0},{0,8},{24,16},{16,24},{9,1},{1,9},{25,17},{17,25},{10,2},{2,... | collective-permute-start | bytes 393224 | tf_op jit(solution)/shard_map/ppermute | solution.py:434
  32.4 7.6 %collective-permute-start.11 = (bf16[128,512]{1,0:T(8,128)(2,1)S(1)}, bf16[128,512]{1,0:T(8,128)(2,1)S(1)}, u32[]{:S(2)}, u32[]{:S(2)}) collective-permute-start(bf16[128,512]{1,0:T(8,128)(2,1)S(1)} %get-tuple-element.42), channel_id=1, source_target_pairs={{16,0},{24,8},{0,16},{8,24},{17,1},{25,9},{1,17},{9,25},{18,2},{26... | collective-permute-start | bytes 393224 | tf_op jit(solution)/shard_map/ppermute | solution.py:434
  32.9 7.1 %collective-permute-start.12 = (bf16[128,512]{1,0:T(8,128)(2,1)S(1)}, bf16[128,512]{1,0:T(8,128)(2,1)S(1)}, u32[]{:S(2)}, u32[]{:S(2)}) collective-permute-start(bf16[128,512]{1,0:T(8,128)(2,1)S(1)} %get-tuple-element.43), channel_id=1, source_target_pairs={{24,0},{16,8},{8,16},{0,24},{25,1},{17,9},{9,17},{1,25},{26,2},{18... | collective-permute-start | bytes 393224 | tf_op jit(solution)/shard_map/ppermute | solution.py:434

commit v3 on v2

--- a/solution.py
+++ b/solution.py
@@ -423,12 +423,18 @@
 
     alive, meta, picks, heads, rows = movers(n_groups, lists_group, block_list, home_pos, counts, keep, vectors)
     heads = [lax.ppermute(x, "grp", pairs) for x, pairs in zip(heads, there)]
-    mine = pack(meta, block_sums(alive, vectors), heads)
-    mine, *rows = lax.optimization_barrier((mine, *rows))
+    sums = block_sums(alive, vectors)
+    last, sums, *heads = lax.optimization_barrier((rows[-1], sums, *heads))
+    last = lax.ppermute(last, "grp", there[-1])
+    mine = pack(meta, sums, heads)
+    mine, *rows = lax.optimization_barrier((mine, *rows[:-1]))
     rows = [lax.ppermute(x, "grp", pairs) for x, pairs in zip(rows, there)]
     near = [lax.ppermute(mine, "row", pairs) for pairs in along]
     sums, totals = with_prior(blocks, mine, old_centroids)
-    far = lax.ppermute(jnp.concatenate([mine] + near, axis=0), "row", cores)
+    both = jnp.concatenate([mine] + near, axis=0)
+    both, last = lax.optimization_barrier((both, last))
+    rows.append(last)
+    far = lax.ppermute(both, "row", cores)
     table, norms, share = make_table(n_rows, blocks, near, far, sums, totals)
     parts = parts_of(norms, table, rows)
     parts = [lax.ppermute(x, "grp", pairs) for x, pairs in zip(parts, back)]

time: 41.7 us -> 39.6 us (0.950)
  waiting for transfers between devices: 9.65 us -> 5.96 us
  starting transfers between devices: 15 us -> 16.6 us
    ppermute x3 -> x2, waiting for transfers between devices: 2.81 us -> 0.01 us  [local(): rows = [lax.ppermute(x, 'grp', pairs) for x, pairs in zip(rows, there)]]
    ppermute x3, waiting for transfers between devices: 2.42 us -> 1.06 us  [local(): near = [lax.ppermute(mine, 'row', pairs) for pairs in along]]
    ppermute x3 -> x2, starting transfers between devices: 2.38 us -> 3.68 us  [local(): rows = [lax.ppermute(x, 'grp', pairs) for x, pairs in zip(rows, there)]]
    ppermute x3, waiting for transfers between devices: 0.01 us -> 0.49 us  [local(): parts = [lax.ppermute(x, 'grp', pairs) for x, pairs in zip(parts, back)]]
    ppermute x1 -> x2, waiting for transfers between devices: 1.07 us -> 1.07 us  [the longest x1 1.06 us: local(): far = lax.ppermute(both, 'row', cores)]
  transfers between devices with their start and end apart: 13 -> 13, of which waited for: 6 -> 6; matrix products, arithmetic and copies ran while one was open for 0% -> 0% of each run, Pallas kernels for 23% -> 24%
where the time goes in v3:
time: 39.6 us; the launch traced here: 39.4 us
  starting transfers between devices  16.6 us (42%)
  Pallas kernels  16.1 us (41%)
  waiting for transfers between devices  5.96 us (15%)
  between operations  0.73 us (2%)
    pallas_call x1, Pallas kernels, scores_of(): pl.pallas_call(scores_kernel, out_shape=shaped((rows, lists), F32), in_sp...  5.59 us
    ppermute x3, starting transfers between devices, local(): near = [lax.ppermute(mine, 'row', pairs) for pairs in along]  4.73 us
    ppermute x3, starting transfers between devices, local(): heads = [lax.ppermute(x, 'grp', pairs) for x, pairs in zip(heads, there)]  4.54 us
    pallas_call x1, Pallas kernels, movers(): pl.pallas_call(functools.partial(movers_kernel, n_groups, lists_group), o...  3.83 us
    ppermute x2, starting transfers between devices, local(): rows = [lax.ppermute(x, 'grp', pairs) for x, pairs in zip(rows, there)]  3.68 us
    ppermute x3, starting transfers between devices, local(): parts = [lax.ppermute(x, 'grp', pairs) for x, pairs in zip(parts, back)]  3.55 us
    ppermute x3, waiting for transfers between devices, local(): heads = [lax.ppermute(x, 'grp', pairs) for x, pairs in zip(heads, there)]  3.33 us
    pallas_call x1, Pallas kernels, make_table(): pl.pallas_call(functools.partial(table_kernel, blocks, len(near)), out_sh...  2.17 us
  transfers between devices with their start and end apart: 13, of which 6 were waited for; matrix products, arithmetic and copies ran while one was open for 0% of the time, Pallas kernels for 24%

profile of v3, /device:TPU:0, one launch (start us, length us, event | category | flops | bytes accessed | tf_op | source)
XLA Modules:
  0.0 39.4 jit_solution(17856273989563443763)
XLA Ops:
  0.7 3.8 %movers.1 = (f32[32,128]{1,0:T(8,128)S(1)}, f32[8,128]{1,0:T(8,128)S(1)}, s32[3]{0:T(128)S(1)}, f32[16,128]{1,0:T(8,128)S(1)}, f32[16,128]{1,0:T(8,128)S(1)}, /*...) custom-call(s32[1024]{0:T(1024)} %list_ref.1, ...), custom_call_target="tpu_custom_call" | custom-call | flops 786432 | bytes 2359296 | tf_op jit(solution)/shard_map/movers/pallas_call | solution.py:138
  4.5 3.0 %collective-permute-start = (f32[16,128]{1,0:T(8,128)S(1)}, f32[16,128]{1,0:T(8,128)S(1)}, u32[]{:S(2)}, u32[]{:S(2)}) collective-permute-start(f32[16,128]{1,0:T(8,128)S(1)} %get-tuple-element.32), channel_id=1, source_target_pairs={{0,8},{8,0},{16,24},{24,16},{1,9},{9,1},{17,25},{25,17},{2,10},{10... | collective-permute-start | bytes 24584 | tf_op jit(solution)/shard_map/ppermute | solution.py:425
  7.5 1.5 %collective-permute-start.1 = (f32[16,128]{1,0:T(8,128)S(1)}, f32[16,128]{1,0:T(8,128)S(1)}, u32[]{:S(2)}, u32[]{:S(2)}) collective-permute-start(f32[16,128]{1,0:T(8,128)S(1)} %get-tuple-element.33), channel_id=1, source_target_pairs={{0,16},{8,24},{16,0},{24,8},{1,17},{9,25},{17,1},{25,9},{2,18},{10... | collective-permute-start | bytes 24584 | tf_op jit(solution)/shard_map/ppermute | solution.py:425
  9.0 0.0 collective-permute-start.2
  9.0 1.2 %block_sums.1.sums_ref = f32[32,1024]{1,0:T(8,128)S(1)} custom-call(f32[32,128]{1,0:T(8,128)S(1)} %get-tuple-element.31.alive_ref, bf16[4096,1024]{1,0:T(8,128)(2,1)S(1)} %copy-done), custom_call_target="tpu_custom_call" | custom-call | flops 67108864 | bytes 8388608 | tf_op jit(solution)/shard_map/block_sums/pallas_call | solution.py:173
  10.2 0.0 collective-permute-done.refs_0_
  10.2 0.9 %collective-permute-done.1.refs_1_ = f32[16,128]{1,0:T(8,128)S(1)} collective-permute-done((f32[16,128]{1,0:T(8,128)S(1)}, f32[16,128]{1,0:T(8,128)S(1)}, u32[]{:S(2)}, u32[]{:S(2)}) %collective-permute-start.1) | collective-permute-done | bytes 8224 | tf_op jit(solution)/shard_map/ppermute | solution.py:425
  11.1 2.4 %collective-permute-done.2.refs_2_ = f32[16,128]{1,0:T(8,128)S(1)} collective-permute-done((f32[16,128]{1,0:T(8,128)S(1)}, f32[16,128]{1,0:T(8,128)S(1)}, u32[]{:S(2)}, u32[]{:S(2)}) %collective-permute-start.2) | collective-permute-done | bytes 8224 | tf_op jit(solution)/shard_map/ppermute | solution.py:425
  13.6 0.0 collective-permute-start.6
  13.6 0.2 pack.1.mine_ref
  13.7 4.1 %collective-permute-start.5 = (s16[40,1024]{1,0:T(8,128)(2,1)S(1)}, s16[40,1024]{1,0:T(8,128)(2,1)S(1)}, u32[]{:S(2)}, u32[]{:S(2)}) collective-permute-start(s16[40,1024]{1,0:T(8,128)(2,1)S(1)} %pack.1.mine_ref), channel_id=1, source_target_pairs={{0,6},{1,7},{2,4},{3,5},{4,2},{5,3},{6,0},{7,1},{8,14},{9,15},{10,... | collective-permute-start | bytes 245768 | tf_op jit(solution)/shard_map/ppermute | solution.py:432
  17.8 0.0 collective-permute-start.4
  17.8 0.6 %collective-permute-start.3 = (s16[40,1024]{1,0:T(8,128)(2,1)S(1)}, s16[40,1024]{1,0:T(8,128)(2,1)S(1)}, u32[]{:S(2)}, u32[]{:S(2)}) collective-permute-start(s16[40,1024]{1,0:T(8,128)(2,1)S(1)} %pack.1.mine_ref), channel_id=1, source_target_pairs={{0,2},{1,3},{2,0},{3,1},{4,6},{5,7},{6,4},{7,5},{8,10},{9,11},{10,... | collective-permute-start | bytes 245768 | tf_op jit(solution)/shard_map/ppermute | solution.py:432
  18.5 1.6 %collective-permute-start.8 = (bf16[128,1024]{1,0:T(8,128)(2,1)S(1)}, bf16[128,1024]{1,0:T(8,128)(2,1)S(1)}, u32[]{:S(2)}, u32[]{:S(2)}) collective-permute-start(bf16[128,1024]{1,0:T(8,128)(2,1)S(1)} %get-tuple-element.50), channel_id=1, source_target_pairs={{0,8},{8,0},{16,24},{24,16},{1,9},{9,1},{17,25},{25,17},{2,10},{10... | collective-permute-start | bytes 786440 | tf_op jit(solution)/shard_map/ppermute | solution.py:431
  20.1 0.3 collective-permute-done.5.refs_2_
  20.4 2.0 %collective-permute-start.9 = (bf16[128,1024]{1,0:T(8,128)(2,1)S(1)}, bf16[128,1024]{1,0:T(8,128)(2,1)S(1)}, u32[]{:S(2)}, u32[]{:S(2)}) collective-permute-start(bf16[128,1024]{1,0:T(8,128)(2,1)S(1)} %get-tuple-element.51), channel_id=1, source_target_pairs={{0,16},{8,24},{16,0},{24,8},{1,17},{9,25},{17,1},{25,9},{2,18},{10... | collective-permute-start | bytes 786440 | tf_op jit(solution)/shard_map/ppermute | solution.py:431
  22.5 0.7 %collective-permute-done.4.refs_1_ = s16[40,1024]{1,0:T(8,128)(2,1)S(1)} collective-permute-done((s16[40,1024]{1,0:T(8,128)(2,1)S(1)}, s16[40,1024]{1,0:T(8,128)(2,1)S(1)}, u32[]{:S(2)}, u32[]{:S(2)}) %collective-permute-start.4) | collective-permute-done | bytes 81952 | tf_op jit(solution)/shard_map/ppermute | solution.py:432
  23.2 0.0 collective-permute-done.3.refs_0_
  23.2 0.0 collective-permute-done.6.refs_2_
  23.3 0.1 collective-permute-start.7
  23.3 0.5 %prior.1 = (f32[512,1024]{1,0:T(8,128)S(1)}, f32[512,128]{1,0:T(8,128)S(1)}) custom-call(s16[40,1024]{1,0:T(8,128)(2,1)S(1)} %pack.1.mine_ref, bf16[512,1024]{1,0:T(8,128)(2,1)S(1)} %copy-done.1), custom_call_target="tpu_custom_call" | custom-call | flops 10485760000 | bytes 4194304 | tf_op jit(solution)/shard_map/prior/pallas_call | solution.py:258
  23.9 1.1 %collective-permute-done.7.refs_3_ = s16[160,1024]{1,0:T(8,128)(2,1)S(1)} collective-permute-done((s16[160,1024]{1,0:T(8,128)(2,1)S(1)}, s16[160,1024]{1,0:T(8,128)(2,1)S(1)}, u32[]{:S(2)}, u32[]{:S(2)}) %collective-permute-start.7) | collective-permute-done | bytes 327712 | tf_op jit(solution)/shard_map/ppermute | solution.py:437
  25.0 2.2 %table.1 = (bf16[512,1024]{1,0:T(8,128)(2,1)S(1)}, f32[8,512]{1,0:T(8,128)S(1)}, bf16[64,1024]{1,0:T(8,128)(2,1)}) custom-call(s16[40,1024]{1,0:T(8,128)(2,1)S(1)} %collective-permute-done.3.refs_0_, s16[40,1024]{1,0:T(8,128)(2,1)S(1)} %collective-permute-done.4.refs_1_, s16[40,1024]{1,0:T(8,128)(2,1)S(1)} %collective-permute-done.5.refs_2_, ...), custom_call_target="tpu_custom_call" | custom-call | flops 1048576000 | bytes 4194304 | tf_op jit(solution)/shard_map/table/pallas_call | solution.py:298
  27.1 1.2 %parts.1 = (bf16[128,512]{1,0:T(8,128)(2,1)S(1)}, bf16[128,512]{1,0:T(8,128)(2,1)S(1)}, bf16[128,512]{1,0:T(8,128)(2,1)S(1)}) custom-call(f32[8,512]{1,0:T(8,128)S(1)} %get-tuple-element.48.norms_ref, bf16[512,1024]{1,0:T(8,128)(2,1)S(1)} %get-tuple-element.49.table_ref, bf16[128,1024]{1,0:T(8,128)(2,1)S(1)} %collective-permute-done.8.refs_0_, ...), custom_call_target="tpu_custom_call" | custom-call | flops 402653184 | bytes 1048576 | tf_op jit(solution)/shard_map/parts/pallas_call | solution.py:321
  28.3 1.8 %collective-permute-start.10 = (bf16[128,512]{1,0:T(8,128)(2,1)S(1)}, bf16[128,512]{1,0:T(8,128)(2,1)S(1)}, u32[]{:S(2)}, u32[]{:S(2)}) collective-permute-start(bf16[128,512]{1,0:T(8,128)(2,1)S(1)} %get-tuple-element.53), channel_id=1, source_target_pairs={{8,0},{0,8},{24,16},{16,24},{9,1},{1,9},{25,17},{17,25},{10,2},{2,... | collective-permute-start | bytes 393224 | tf_op jit(solution)/shard_map/ppermute | solution.py:440
  30.1 1.5 %collective-permute-start.11 = (bf16[128,512]{1,0:T(8,128)(2,1)S(1)}, bf16[128,512]{1,0:T(8,128)(2,1)S(1)}, u32[]{:S(2)}, u32[]{:S(2)}) collective-permute-start(bf16[128,512]{1,0:T(8,128)(2,1)S(1)} %get-tuple-element.54), channel_id=1, source_target_pairs={{16,0},{24,8},{0,16},{8,24},{17,1},{25,9},{1,17},{9,25},{18,2},{26... | collective-permute-start | bytes 393224 | tf_op jit(solution)/shard_map/ppermute | solution.py:440
  31.6 0.3 collective-permute-start.12
  31.8 5.6 %scores.1.refs_3_ = f32[4096,512]{1,0:T(8,128)} custom-call(f32[32,128]{1,0:T(8,128)S(1)} %get-tuple-element.31.alive_ref, f32[8,512]{1,0:T(8,128)S(1)} %get-tuple-element.48.norms_ref, bf16[512,1024]{1,0:T(8,128)(2,1)S(1)} %get-tuple-element.49.table_ref, bf16[4096,1024]{1,0:T(8,128)(2,1)S(1)} %copy-done), custom_call_target="tpu_custom_call" | custom-call | flops 4294967296 | bytes 8388608 | tf_op jit(solution)/shard_map/scores/pallas_call | solution.py:358
  37.4 0.0 collective-permute-done.10.refs_0_
  37.5 0.5 %collective-permute-done.11.refs_1_ = bf16[128,512]{1,0:T(8,128)(2,1)S(1)} collective-permute-done((bf16[128,512]{1,0:T(8,128)(2,1)S(1)}, bf16[128,512]{1,0:T(8,128)(2,1)S(1)}, u32[]{:S(2)}, u32[]{:S(2)}) %collective-permute-start.11) | collective-permute-done | bytes 131104 | tf_op jit(solution)/shard_map/ppermute | solution.py:440
  37.9 0.0 collective-permute-done.12.refs_2_
  37.9 1.5 %merge.1 = f32[4096,512]{1,0:T(8,128)} custom-call(s32[3]{0:T(128)S(1)} %get-tuple-element.47.picks_ref, f32[32,128]{1,0:T(8,128)S(1)} %get-tuple-element.31.alive_ref, bf16[128,512]{1,0:T(8,128)(2,1)S(1)} %collective-permute-done.10.refs_0_, bf16[128,512]{1,0:T(8,128)(2,1)S(1)} %collective-permute-done.11.refs_1_, ...), custom_call_target="tpu_custom_call", output_to_operand_aliasing={{}: (5, {})} | custom-call | flops 393216 | bytes 1179648 | tf_op jit(solution)/shard_map/merge/pallas_call | solution.py:398
  (7 shorter events, 0.0 us)
Async XLA Ops:
  0.6 8.4 %copy-start = (bf16[4096,1024]{1,0:T(8,128)(2,1)S(1)}, bf16[4096,1024]{1,0:T(8,128)(2,1)}, u32[]{:S(2)}) copy-start(bf16[4096,1024]{1,0:T(8,128)(2,1)} %vec_ref.5) | copy-start | bytes 25165828
  0.6 22.7 %copy-start.1 = (bf16[512,1024]{1,0:T(8,128)(2,1)S(1)}, bf16[512,1024]{1,0:T(8,128)(2,1)}, u32[]{:S(2)}) copy-start(bf16[512,1024]{1,0:T(8,128)(2,1)} %old_ref.1) | copy-start | bytes 3145732
  4.5 5.7 %collective-permute-start = (f32[16,128]{1,0:T(8,128)S(1)}, f32[16,128]{1,0:T(8,128)S(1)}, u32[]{:S(2)}, u32[]{:S(2)}) collective-permute-start(f32[16,128]{1,0:T(8,128)S(1)} %get-tuple-element.32), channel_id=1, source_target_pairs={{0,8},{8,0},{16,24},{24,16},{1,9},{9,1},{17,25},{25,17},{2,10},{10... | collective-permute-start | bytes 24584 | tf_op jit(solution)/shard_map/ppermute | solution.py:425
  7.5 3.7 %collective-permute-start.1 = (f32[16,128]{1,0:T(8,128)S(1)}, f32[16,128]{1,0:T(8,128)S(1)}, u32[]{:S(2)}, u32[]{:S(2)}) collective-permute-start(f32[16,128]{1,0:T(8,128)S(1)} %get-tuple-element.33), channel_id=1, source_target_pairs={{0,16},{8,24},{16,0},{24,8},{1,17},{9,25},{17,1},{25,9},{2,18},{10... | collective-permute-start | bytes 24584 | tf_op jit(solution)/shard_map/ppermute | solution.py:425
  9.0 4.5 %collective-permute-start.2 = (f32[16,128]{1,0:T(8,128)S(1)}, f32[16,128]{1,0:T(8,128)S(1)}, u32[]{:S(2)}, u32[]{:S(2)}) collective-permute-start(f32[16,128]{1,0:T(8,128)S(1)} %get-tuple-element.34), channel_id=1, source_target_pairs={{0,24},{8,16},{16,8},{24,0},{1,25},{9,17},{17,9},{25,1},{2,26},{10... | collective-permute-start | bytes 24584 | tf_op jit(solution)/shard_map/ppermute | solution.py:425
  13.6 9.7 %collective-permute-start.6 = (bf16[128,1024]{1,0:T(8,128)(2,1)S(1)}, bf16[128,1024]{1,0:T(8,128)(2,1)S(1)}, u32[]{:S(2)}, u32[]{:S(2)}) collective-permute-start(bf16[128,1024]{1,0:T(8,128)(2,1)S(1)} %get-tuple-element.42), channel_id=1, source_target_pairs={{0,24},{8,16},{16,8},{24,0},{1,25},{9,17},{17,9},{25,1},{2,26},{10... | collective-permute-start | bytes 786440 | tf_op jit(solution)/shard_map/ppermute | solution.py:428
  13.7 6.7 %collective-permute-start.5 = (s16[40,1024]{1,0:T(8,128)(2,1)S(1)}, s16[40,1024]{1,0:T(8,128)(2,1)S(1)}, u32[]{:S(2)}, u32[]{:S(2)}) collective-permute-start(s16[40,1024]{1,0:T(8,128)(2,1)S(1)} %pack.1.mine_ref), channel_id=1, source_target_pairs={{0,6},{1,7},{2,4},{3,5},{4,2},{5,3},{6,0},{7,1},{8,14},{9,15},{10,... | collective-permute-start | bytes 245768 | tf_op jit(solution)/shard_map/ppermute | solution.py:432
  17.8 5.4 %collective-permute-start.4 = (s16[40,1024]{1,0:T(8,128)(2,1)S(1)}, s16[40,1024]{1,0:T(8,128)(2,1)S(1)}, u32[]{:S(2)}, u32[]{:S(2)}) collective-permute-start(s16[40,1024]{1,0:T(8,128)(2,1)S(1)} %pack.1.mine_ref), channel_id=1, source_target_pairs={{0,4},{1,5},{2,6},{3,7},{4,0},{5,1},{6,2},{7,3},{8,12},{9,13},{10,... | collective-permute-start | bytes 245768 | tf_op jit(solution)/shard_map/ppermute | solution.py:432
  17.8 5.4 %collective-permute-start.3 = (s16[40,1024]{1,0:T(8,128)(2,1)S(1)}, s16[40,1024]{1,0:T(8,128)(2,1)S(1)}, u32[]{:S(2)}, u32[]{:S(2)}) collective-permute-start(s16[40,1024]{1,0:T(8,128)(2,1)S(1)} %pack.1.mine_ref), channel_id=1, source_target_pairs={{0,2},{1,3},{2,0},{3,1},{4,6},{5,7},{6,4},{7,5},{8,10},{9,11},{10,... | collective-permute-start | bytes 245768 | tf_op jit(solution)/shard_map/ppermute | solution.py:432
  18.5 8.6 %collective-permute-start.8 = (bf16[128,1024]{1,0:T(8,128)(2,1)S(1)}, bf16[128,1024]{1,0:T(8,128)(2,1)S(1)}, u32[]{:S(2)}, u32[]{:S(2)}) collective-permute-start(bf16[128,1024]{1,0:T(8,128)(2,1)S(1)} %get-tuple-element.50), channel_id=1, source_target_pairs={{0,8},{8,0},{16,24},{24,16},{1,9},{9,1},{17,25},{25,17},{2,10},{10... | collective-permute-start | bytes 786440 | tf_op jit(solution)/shard_map/ppermute | solution.py:431
  20.4 6.7 %collective-permute-start.9 = (bf16[128,1024]{1,0:T(8,128)(2,1)S(1)}, bf16[128,1024]{1,0:T(8,128)(2,1)S(1)}, u32[]{:S(2)}, u32[]{:S(2)}) collective-permute-start(bf16[128,1024]{1,0:T(8,128)(2,1)S(1)} %get-tuple-element.51), channel_id=1, source_target_pairs={{0,16},{8,24},{16,0},{24,8},{1,17},{9,25},{17,1},{25,9},{2,18},{10... | collective-permute-start | bytes 786440 | tf_op jit(solution)/shard_map/ppermute | solution.py:431
  23.3 1.7 %collective-permute-start.7 = (s16[160,1024]{1,0:T(8,128)(2,1)S(1)}, s16[160,1024]{1,0:T(8,128)(2,1)S(1)}, u32[]{:S(2)}, u32[]{:S(2)}) collective-permute-start(s16[160,1024]{1,0:T(8,128)(2,1)S(1)} %pad_add_fusion), channel_id=1, source_target_pairs={{0,1},{1,0},{2,3},{3,2},{4,5},{5,4},{6,7},{7,6},{8,9},{9,8},{10,11... | collective-permute-start | bytes 983048 | tf_op jit(solution)/shard_map/ppermute | solution.py:437
  28.3 9.2 %collective-permute-start.10 = (bf16[128,512]{1,0:T(8,128)(2,1)S(1)}, bf16[128,512]{1,0:T(8,128)(2,1)S(1)}, u32[]{:S(2)}, u32[]{:S(2)}) collective-permute-start(bf16[128,512]{1,0:T(8,128)(2,1)S(1)} %get-tuple-element.53), channel_id=1, source_target_pairs={{8,0},{0,8},{24,16},{16,24},{9,1},{1,9},{25,17},{17,25},{10,2},{2,... | collective-permute-start | bytes 393224 | tf_op jit(solution)/shard_map/ppermute | solution.py:440
  30.1 7.9 %collective-permute-start.11 = (bf16[128,512]{1,0:T(8,128)(2,1)S(1)}, bf16[128,512]{1,0:T(8,128)(2,1)S(1)}, u32[]{:S(2)}, u32[]{:S(2)}) collective-permute-start(bf16[128,512]{1,0:T(8,128)(2,1)S(1)} %get-tuple-element.54), channel_id=1, source_target_pairs={{16,0},{24,8},{0,16},{8,24},{17,1},{25,9},{1,17},{9,25},{18,2},{26... | collective-permute-start | bytes 393224 | tf_op jit(solution)/shard_map/ppermute | solution.py:440
  31.6 6.4 %collective-permute-start.12 = (bf16[128,512]{1,0:T(8,128)(2,1)S(1)}, bf16[128,512]{1,0:T(8,128)(2,1)S(1)}, u32[]{:S(2)}, u32[]{:S(2)}) collective-permute-start(bf16[128,512]{1,0:T(8,128)(2,1)S(1)} %get-tuple-element.55), channel_id=1, source_target_pairs={{24,0},{16,8},{8,16},{0,24},{25,1},{17,9},{9,17},{1,25},{26,2},{18... | collective-permute-start | bytes 393224 | tf_op jit(solution)/shard_map/ppermute | solution.py:440

commit v4 on v3

--- a/solution.py
+++ b/solution.py
@@ -211,36 +211,38 @@
         in_specs=[VMEM] * (2 + len(heads)),
         out_specs=VMEM,
         compiler_params=params(8),
-        cost_estimate=cost(8 * rows * width, 6 * rows * width),
+        cost_estimate=cost(6 * 10**9, 6 * rows * width),
         name="pack",
     )(meta, sums, *heads)
 
 
 def add_up(sources, blocks, lists):
-    rows = sources[0].shape[0]
-
-    def lanes(which, first, last):
-        parts = [x[rows - 3 + which : rows - 2 + which, first:last].astype(F32) for x in sources]
-        return jnp.concatenate(parts, axis=1)
-
-    picks_high, picks_low, high, low, hits, counts = [], [], [], [], [], []
-    for first, last in ((0, blocks), (blocks, rows)):
-        values = jnp.concatenate([x[first:last] for x in sources], axis=0)
-        hit = iota((lists, values.shape[0]), 0) == lanes(0, first, last).astype(I32)
-        scale = power(lanes(2, first, last))
-        hits.append(jnp.where(hit, 1.0, 0.0).astype(BF16))
-        picks_high.append(jnp.where(hit, scale * 256.0, 0.0).astype(BF16))
-        picks_low.append(jnp.where(hit, scale, 0.0).astype(BF16))
-        counts.append(jnp.broadcast_to(lanes(1, first, last), (128, values.shape[0])).astype(BF16))
-        high.append((values >> 8).astype(F32).astype(BF16))
-        low.append((values & 255).astype(F32).astype(BF16))
-    totals = lax.dot_general(
-        jnp.concatenate(hits, axis=1), jnp.concatenate(counts, axis=1), ROW_DIMS, preferred_element_type=F32
-    )
+    rows, width = sources[0].shape
+    span = 4 if rows - blocks == 8 else rows - blocks
+    fill = -len(sources) % (8 // span) if span < 8 else 0
+    big = jnp.concatenate([x[:blocks] for x in sources], axis=0)
+    small = [x[blocks : blocks + span] for x in sources] + [jnp.zeros((span, width), I32)] * fill
+    small = jnp.concatenate(small, axis=0)
+
+    def lanes(which, spare):
+        facts = [x[rows - 3 + which : rows - 2 + which, 0:128].astype(F32) for x in sources]
+        wide = jnp.concatenate([x[:, 0:blocks] for x in facts], axis=1)
+        tail = [x[:, blocks : blocks + span] for x in facts] + [jnp.full((1, span), spare, F32)] * fill
+        return wide, jnp.concatenate(tail, axis=1)
+
+    def four(pair, low=True):
+        wide, tail = pair
+        return jnp.concatenate([wide, wide * low, tail, tail * low], axis=1)
+
+    slots = four(lanes(0, -1.0))
+    counts = four(lanes(1, 0.0), low=False)
+    scale, scale_small = map(power, lanes(2, 0.0))
+    scale = jnp.concatenate([256.0 * scale, scale, 256.0 * scale_small, scale_small], axis=1)
+    hit = iota((lists, slots.shape[1]), 0) == slots.astype(I32)
+    totals = jnp.sum(jnp.where(hit, counts, 0.0), axis=1, keepdims=True)
+    values = jnp.concatenate([big >> 8, big & 255, small >> 8, small & 255], axis=0)
     sums = jnp.dot(
-        jnp.concatenate(picks_high + picks_low, axis=1),
-        jnp.concatenate(high + low, axis=0),
-        preferred_element_type=F32,
+        jnp.where(hit, scale, 0.0).astype(BF16), values.astype(F32).astype(BF16), preferred_element_type=F32
     )
     return sums, totals
 
@@ -250,7 +252,7 @@
     prior = 1.0 * PRIOR
     sums, totals = add_up([mine_ref[...].astype(I32)], blocks, lists)
     sums_ref[...] = sums + prior * old_ref[...].astype(F32)
-    totals_ref[...] = totals + prior
+    totals_ref[...] = jnp.broadcast_to(totals + prior, totals_ref.shape)
 
 
 def with_prior(blocks, mine, old):
@@ -274,7 +276,7 @@
     sources = [ref[...].astype(I32) for ref in near]
     sources += [far[j * rows : (j + 1) * rows, :].astype(I32) for j in range(n_near + 1)]
     sums, totals = add_up(sources, blocks, lists)
-    totals = totals_ref[:, 0:1] + totals[:, 0:1]
+    totals = totals_ref[:, 0:1] + totals
     table = ((sums_ref[...] + sums) * (1.0 / totals)).astype(BF16)
     table_ref[...] = table
     share = share_ref.shape[0]
@@ -424,8 +426,7 @@
     alive, meta, picks, heads, rows = movers(n_groups, lists_group, block_list, home_pos, counts, keep, vectors)
     heads = [lax.ppermute(x, "grp", pairs) for x, pairs in zip(heads, there)]
     sums = block_sums(alive, vectors)
-    last, sums, *heads = lax.optimization_barrier((rows[-1], sums, *heads))
-    last = lax.ppermute(last, "grp", there[-1])
+    last = lax.ppermute(rows[-1], "grp", there[-1])
     mine = pack(meta, sums, heads)
     mine, *rows = lax.optimization_barrier((mine, *rows[:-1]))
     rows = [lax.ppermute(x, "grp", pairs) for x, pairs in zip(rows, there)]

time: 39.6 us -> 38.5 us (0.972)
  Pallas kernels: 16.1 us -> 15.5 us
  starting transfers between devices: 16.6 us -> 16.1 us
    ppermute x3, waiting for transfers between devices: 1.06 us -> 4.19 us  [local(): near = [lax.ppermute(mine, 'row', pairs) for pairs in along]]
    ppermute x2, starting transfers between devices: 3.68 us -> 0.66 us  [local(): rows = [lax.ppermute(x, 'grp', pairs) for x, pairs in zip(rows, there)]]
    ppermute x1, starting transfers between devices: 0.02 us -> 2.9 us  [local(): last = lax.ppermute(rows[-1], 'grp', there[-1])]
    ppermute x3, waiting for transfers between devices: 3.33 us -> 0.58 us  [local(): heads = [lax.ppermute(x, 'grp', pairs) for x, pairs in zip(heads, there)]]
    ppermute x3, waiting for transfers between devices: 0.49 us -> 0.01 us  [local(): parts = [lax.ppermute(x, 'grp', pairs) for x, pairs in zip(parts, back)]]
  transfers between devices with their start and end apart: 13 -> 13, of which waited for: 6 -> 4; matrix products, arithmetic and copies ran while one was open for 0% -> 0% of each run, Pallas kernels for 24% -> 24%
where the time goes in v4:
time: 38.5 us; the launch traced here: 38.2 us
  starting transfers between devices  16.1 us (42%)
  Pallas kernels  15.5 us (40%)
  waiting for transfers between devices  5.82 us (15%)
  between operations  0.74 us (2%)
    pallas_call x1, Pallas kernels, scores_of(): pl.pallas_call(scores_kernel, out_shape=shaped((rows, lists), F32), in_sp...  5.59 us
    ppermute x3, starting transfers between devices, local(): heads = [lax.ppermute(x, 'grp', pairs) for x, pairs in zip(heads, there)]  4.54 us
    ppermute x3, starting transfers between devices, local(): near = [lax.ppermute(mine, 'row', pairs) for pairs in along]  4.42 us
    ppermute x3, waiting for transfers between devices, local(): near = [lax.ppermute(mine, 'row', pairs) for pairs in along]  4.19 us
    pallas_call x1, Pallas kernels, movers(): pl.pallas_call(functools.partial(movers_kernel, n_groups, lists_group), o...  3.6 us
    ppermute x3, starting transfers between devices, local(): parts = [lax.ppermute(x, 'grp', pairs) for x, pairs in zip(parts, back)]  3.55 us
    ppermute x1, starting transfers between devices, local(): last = lax.ppermute(rows[-1], 'grp', there[-1])  2.9 us
    pallas_call x1, Pallas kernels, make_table(): pl.pallas_call(functools.partial(table_kernel, blocks, len(near)), out_sh...  1.79 us
  transfers between devices with their start and end apart: 13, of which 4 were waited for; matrix products, arithmetic and copies ran while one was open for 0% of the time, Pallas kernels for 24%

profile of v4, /device:TPU:0, one launch (start us, length us, event | category | flops | bytes accessed | tf_op | source)
XLA Modules:
  0.0 38.2 jit_solution(2811295934920552230)
XLA Ops:
  0.6 3.6 %movers.1 = (f32[32,128]{1,0:T(8,128)S(1)}, f32[8,128]{1,0:T(8,128)S(1)}, s32[3]{0:T(128)S(1)}, f32[16,128]{1,0:T(8,128)S(1)}, f32[16,128]{1,0:T(8,128)S(1)}, /*...) custom-call(s32[1024]{0:T(1024)} %list_ref.1, ...), custom_call_target="tpu_custom_call" | custom-call | flops 786432 | bytes 2359296 | tf_op jit(solution)/shard_map/movers/pallas_call | solution.py:138
  4.2 3.0 %collective-permute-start = (f32[16,128]{1,0:T(8,128)S(1)}, f32[16,128]{1,0:T(8,128)S(1)}, u32[]{:S(2)}, u32[]{:S(2)}) collective-permute-start(f32[16,128]{1,0:T(8,128)S(1)} %get-tuple-element.26), channel_id=1, source_target_pairs={{0,8},{8,0},{16,24},{24,16},{1,9},{9,1},{17,25},{25,17},{2,10},{10... | collective-permute-start | bytes 24584 | tf_op jit(solution)/shard_map/ppermute | solution.py:427
  7.2 1.5 %collective-permute-start.1 = (f32[16,128]{1,0:T(8,128)S(1)}, f32[16,128]{1,0:T(8,128)S(1)}, u32[]{:S(2)}, u32[]{:S(2)}) collective-permute-start(f32[16,128]{1,0:T(8,128)S(1)} %get-tuple-element.27), channel_id=1, source_target_pairs={{0,16},{8,24},{16,0},{24,8},{1,17},{9,25},{17,1},{25,9},{2,18},{10... | collective-permute-start | bytes 24584 | tf_op jit(solution)/shard_map/ppermute | solution.py:427
  8.8 0.0 collective-permute-start.2
  8.8 2.9 %collective-permute-start.6 = (bf16[128,1024]{1,0:T(8,128)(2,1)S(1)}, bf16[128,1024]{1,0:T(8,128)(2,1)S(1)}, u32[]{:S(2)}, u32[]{:S(2)}) collective-permute-start(bf16[128,1024]{1,0:T(8,128)(2,1)S(1)} %get-tuple-element.32), channel_id=1, source_target_pairs={{0,24},{8,16},{16,8},{24,0},{1,25},{9,17},{17,9},{25,1},{2,26},{10... | collective-permute-start | bytes 786440 | tf_op jit(solution)/shard_map/ppermute | solution.py:429
  11.7 1.2 %block_sums.1.sums_ref = f32[32,1024]{1,0:T(8,128)S(1)} custom-call(f32[32,128]{1,0:T(8,128)S(1)} %get-tuple-element.25.alive_ref, bf16[4096,1024]{1,0:T(8,128)(2,1)S(1)} %copy-done), custom_call_target="tpu_custom_call" | custom-call | flops 67108864 | bytes 8388608 | tf_op jit(solution)/shard_map/block_sums/pallas_call | solution.py:173
  12.9 0.0 collective-permute-done.refs_0_
  12.9 0.0 collective-permute-done.1.refs_1_
  12.9 0.6 %collective-permute-done.2.refs_2_ = f32[16,128]{1,0:T(8,128)S(1)} collective-permute-done((f32[16,128]{1,0:T(8,128)S(1)}, f32[16,128]{1,0:T(8,128)S(1)}, u32[]{:S(2)}, u32[]{:S(2)}) %collective-permute-start.2) | collective-permute-done | bytes 8224 | tf_op jit(solution)/shard_map/ppermute | solution.py:427
  13.5 0.2 pack.1.mine_ref
  13.6 3.6 %collective-permute-start.5 = (s16[40,1024]{1,0:T(8,128)(2,1)S(1)}, s16[40,1024]{1,0:T(8,128)(2,1)S(1)}, u32[]{:S(2)}, u32[]{:S(2)}) collective-permute-start(s16[40,1024]{1,0:T(8,128)(2,1)S(1)} %pack.1.mine_ref), channel_id=1, source_target_pairs={{0,6},{1,7},{2,4},{3,5},{4,2},{5,3},{6,0},{7,1},{8,14},{9,15},{10,... | collective-permute-start | bytes 245768 | tf_op jit(solution)/shard_map/ppermute | solution.py:433
  17.3 0.0 collective-permute-start.4
  17.3 0.8 %collective-permute-start.3 = (s16[40,1024]{1,0:T(8,128)(2,1)S(1)}, s16[40,1024]{1,0:T(8,128)(2,1)S(1)}, u32[]{:S(2)}, u32[]{:S(2)}) collective-permute-start(s16[40,1024]{1,0:T(8,128)(2,1)S(1)} %pack.1.mine_ref), channel_id=1, source_target_pairs={{0,2},{1,3},{2,0},{3,1},{4,6},{5,7},{6,4},{7,5},{8,10},{9,11},{10,... | collective-permute-start | bytes 245768 | tf_op jit(solution)/shard_map/ppermute | solution.py:433
  18.1 0.4 %collective-permute-start.8 = (bf16[128,1024]{1,0:T(8,128)(2,1)S(1)}, bf16[128,1024]{1,0:T(8,128)(2,1)S(1)}, u32[]{:S(2)}, u32[]{:S(2)}) collective-permute-start(bf16[128,1024]{1,0:T(8,128)(2,1)S(1)} %get-tuple-element.40), channel_id=1, source_target_pairs={{0,8},{8,0},{16,24},{24,16},{1,9},{9,1},{17,25},{25,17},{2,10},{10... | collective-permute-start | bytes 786440 | tf_op jit(solution)/shard_map/ppermute | solution.py:432
  18.5 1.6 %collective-permute-done.5.refs_2_ = s16[40,1024]{1,0:T(8,128)(2,1)S(1)} collective-permute-done((s16[40,1024]{1,0:T(8,128)(2,1)S(1)}, s16[40,1024]{1,0:T(8,128)(2,1)S(1)}, u32[]{:S(2)}, u32[]{:S(2)}) %collective-permute-start.5) | collective-permute-done | bytes 81952 | tf_op jit(solution)/shard_map/ppermute | solution.py:433
  20.0 0.3 collective-permute-start.9
  20.3 2.6 %collective-permute-done.4.refs_1_ = s16[40,1024]{1,0:T(8,128)(2,1)S(1)} collective-permute-done((s16[40,1024]{1,0:T(8,128)(2,1)S(1)}, s16[40,1024]{1,0:T(8,128)(2,1)S(1)}, u32[]{:S(2)}, u32[]{:S(2)}) %collective-permute-start.4) | collective-permute-done | bytes 81952 | tf_op jit(solution)/shard_map/ppermute | solution.py:433
  22.9 0.0 collective-permute-done.3.refs_0_
  22.9 0.0 collective-permute-done.6.refs_2_
  23.0 0.1 collective-permute-start.7
  23.0 0.6 %prior.1 = (f32[512,1024]{1,0:T(8,128)S(1)}, f32[512,128]{1,0:T(8,128)S(1)}) custom-call(s16[40,1024]{1,0:T(8,128)(2,1)S(1)} %pack.1.mine_ref, bf16[512,1024]{1,0:T(8,128)(2,1)S(1)} %copy-done.1), custom_call_target="tpu_custom_call" | custom-call | flops 10485760000 | bytes 4194304 | tf_op jit(solution)/shard_map/prior/pallas_call | solution.py:260
  23.6 1.0 %collective-permute-done.7.refs_3_ = s16[160,1024]{1,0:T(8,128)(2,1)S(1)} collective-permute-done((s16[160,1024]{1,0:T(8,128)(2,1)S(1)}, s16[160,1024]{1,0:T(8,128)(2,1)S(1)}, u32[]{:S(2)}, u32[]{:S(2)}) %collective-permute-start.7) | collective-permute-done | bytes 327712 | tf_op jit(solution)/shard_map/ppermute | solution.py:438
  24.6 1.8 %table.1 = (bf16[512,1024]{1,0:T(8,128)(2,1)S(1)}, f32[8,512]{1,0:T(8,128)S(1)}, bf16[64,1024]{1,0:T(8,128)(2,1)}) custom-call(s16[40,1024]{1,0:T(8,128)(2,1)S(1)} %collective-permute-done.3.refs_0_, s16[40,1024]{1,0:T(8,128)(2,1)S(1)} %collective-permute-done.4.refs_1_, s16[40,1024]{1,0:T(8,128)(2,1)S(1)} %collective-permute-done.5.refs_2_, ...), custom_call_target="tpu_custom_call" | custom-call | flops 1048576000 | bytes 4194304 | tf_op jit(solution)/shard_map/table/pallas_call | solution.py:300
  26.4 0.0 collective-permute-done.8.refs_0_
  26.4 1.2 %parts.1 = (bf16[128,512]{1,0:T(8,128)(2,1)S(1)}, bf16[128,512]{1,0:T(8,128)(2,1)S(1)}, bf16[128,512]{1,0:T(8,128)(2,1)S(1)}) custom-call(f32[8,512]{1,0:T(8,128)S(1)} %get-tuple-element.38.norms_ref, bf16[512,1024]{1,0:T(8,128)(2,1)S(1)} %get-tuple-element.39.table_ref, bf16[128,1024]{1,0:T(8,128)(2,1)S(1)} %collective-permute-done.8.refs_0_, ...), custom_call_target="tpu_custom_call" | custom-call | flops 402653184 | bytes 1048576 | tf_op jit(solution)/shard_map/parts/pallas_call | solution.py:323
  27.6 0.6 %collective-permute-start.10 = (bf16[128,512]{1,0:T(8,128)(2,1)S(1)}, bf16[128,512]{1,0:T(8,128)(2,1)S(1)}, u32[]{:S(2)}, u32[]{:S(2)}) collective-permute-start(bf16[128,512]{1,0:T(8,128)(2,1)S(1)} %get-tuple-element.43), channel_id=1, source_target_pairs={{8,0},{0,8},{24,16},{16,24},{9,1},{1,9},{25,17},{17,25},{10,2},{2,... | collective-permute-start | bytes 393224 | tf_op jit(solution)/shard_map/ppermute | solution.py:441
  28.2 0.5 %collective-permute-start.11 = (bf16[128,512]{1,0:T(8,128)(2,1)S(1)}, bf16[128,512]{1,0:T(8,128)(2,1)S(1)}, u32[]{:S(2)}, u32[]{:S(2)}) collective-permute-start(bf16[128,512]{1,0:T(8,128)(2,1)S(1)} %get-tuple-element.44), channel_id=1, source_target_pairs={{16,0},{24,8},{0,16},{8,24},{17,1},{25,9},{1,17},{9,25},{18,2},{26... | collective-permute-start | bytes 393224 | tf_op jit(solution)/shard_map/ppermute | solution.py:441
  28.7 2.5 %collective-permute-start.12 = (bf16[128,512]{1,0:T(8,128)(2,1)S(1)}, bf16[128,512]{1,0:T(8,128)(2,1)S(1)}, u32[]{:S(2)}, u32[]{:S(2)}) collective-permute-start(bf16[128,512]{1,0:T(8,128)(2,1)S(1)} %get-tuple-element.45), channel_id=1, source_target_pairs={{24,0},{16,8},{8,16},{0,24},{25,1},{17,9},{9,17},{1,25},{26,2},{18... | collective-permute-start | bytes 393224 | tf_op jit(solution)/shard_map/ppermute | solution.py:441
  31.2 5.6 %scores.1.refs_3_ = f32[4096,512]{1,0:T(8,128)} custom-call(f32[32,128]{1,0:T(8,128)S(1)} %get-tuple-element.25.alive_ref, f32[8,512]{1,0:T(8,128)S(1)} %get-tuple-element.38.norms_ref, bf16[512,1024]{1,0:T(8,128)(2,1)S(1)} %get-tuple-element.39.table_ref, bf16[4096,1024]{1,0:T(8,128)(2,1)S(1)} %copy-done), custom_call_target="tpu_custom_call" | custom-call | flops 4294967296 | bytes 8388608 | tf_op jit(solution)/shard_map/scores/pallas_call | solution.py:360
  36.8 0.0 collective-permute-done.10.refs_0_
  36.8 0.0 collective-permute-done.11.refs_1_
  36.8 1.4 %merge.1 = f32[4096,512]{1,0:T(8,128)} custom-call(s32[3]{0:T(128)S(1)} %get-tuple-element.37.picks_ref, f32[32,128]{1,0:T(8,128)S(1)} %get-tuple-element.25.alive_ref, bf16[128,512]{1,0:T(8,128)(2,1)S(1)} %collective-permute-done.10.refs_0_, bf16[128,512]{1,0:T(8,128)(2,1)S(1)} %collective-permute-done.11.refs_1_, ...), custom_call_target="tpu_custom_call", output_to_operand_aliasing={{}: (5, {})} | custom-call | flops 393216 | bytes 1179648 | tf_op jit(solution)/shard_map/merge/pallas_call | solution.py:400
  (7 shorter events, 0.0 us)
Async XLA Ops:
  0.6 11.1 %copy-start = (bf16[4096,1024]{1,0:T(8,128)(2,1)S(1)}, bf16[4096,1024]{1,0:T(8,128)(2,1)}, u32[]{:S(2)}) copy-start(bf16[4096,1024]{1,0:T(8,128)(2,1)} %vec_ref.5) | copy-start | bytes 25165828
  4.2 8.6 %collective-permute-start = (f32[16,128]{1,0:T(8,128)S(1)}, f32[16,128]{1,0:T(8,128)S(1)}, u32[]{:S(2)}, u32[]{:S(2)}) collective-permute-start(f32[16,128]{1,0:T(8,128)S(1)} %get-tuple-element.26), channel_id=1, source_target_pairs={{0,8},{8,0},{16,24},{24,16},{1,9},{9,1},{17,25},{25,17},{2,10},{10... | collective-permute-start | bytes 24584 | tf_op jit(solution)/shard_map/ppermute | solution.py:427
  7.2 5.6 %collective-permute-start.1 = (f32[16,128]{1,0:T(8,128)S(1)}, f32[16,128]{1,0:T(8,128)S(1)}, u32[]{:S(2)}, u32[]{:S(2)}) collective-permute-start(f32[16,128]{1,0:T(8,128)S(1)} %get-tuple-element.27), channel_id=1, source_target_pairs={{0,16},{8,24},{16,0},{24,8},{1,17},{9,25},{17,1},{25,9},{2,18},{10... | collective-permute-start | bytes 24584 | tf_op jit(solution)/shard_map/ppermute | solution.py:427
  8.8 4.7 %collective-permute-start.2 = (f32[16,128]{1,0:T(8,128)S(1)}, f32[16,128]{1,0:T(8,128)S(1)}, u32[]{:S(2)}, u32[]{:S(2)}) collective-permute-start(f32[16,128]{1,0:T(8,128)S(1)} %get-tuple-element.28), channel_id=1, source_target_pairs={{0,24},{8,16},{16,8},{24,0},{1,25},{9,17},{17,9},{25,1},{2,26},{10... | collective-permute-start | bytes 24584 | tf_op jit(solution)/shard_map/ppermute | solution.py:427
  8.8 14.2 %collective-permute-start.6 = (bf16[128,1024]{1,0:T(8,128)(2,1)S(1)}, bf16[128,1024]{1,0:T(8,128)(2,1)S(1)}, u32[]{:S(2)}, u32[]{:S(2)}) collective-permute-start(bf16[128,1024]{1,0:T(8,128)(2,1)S(1)} %get-tuple-element.32), channel_id=1, source_target_pairs={{0,24},{8,16},{16,8},{24,0},{1,25},{9,17},{17,9},{25,1},{2,26},{10... | collective-permute-start | bytes 786440 | tf_op jit(solution)/shard_map/ppermute | solution.py:429
  13.5 9.6 %copy-start.1 = (bf16[512,1024]{1,0:T(8,128)(2,1)S(1)}, bf16[512,1024]{1,0:T(8,128)(2,1)}, u32[]{:S(2)}) copy-start(bf16[512,1024]{1,0:T(8,128)(2,1)} %old_ref.1) | copy-start | bytes 3145732
  13.6 6.4 %collective-permute-start.5 = (s16[40,1024]{1,0:T(8,128)(2,1)S(1)}, s16[40,1024]{1,0:T(8,128)(2,1)S(1)}, u32[]{:S(2)}, u32[]{:S(2)}) collective-permute-start(s16[40,1024]{1,0:T(8,128)(2,1)S(1)} %pack.1.mine_ref), channel_id=1, source_target_pairs={{0,6},{1,7},{2,4},{3,5},{4,2},{5,3},{6,0},{7,1},{8,14},{9,15},{10,... | collective-permute-start | bytes 245768 | tf_op jit(solution)/shard_map/ppermute | solution.py:433
  17.3 5.6 %collective-permute-start.4 = (s16[40,1024]{1,0:T(8,128)(2,1)S(1)}, s16[40,1024]{1,0:T(8,128)(2,1)S(1)}, u32[]{:S(2)}, u32[]{:S(2)}) collective-permute-start(s16[40,1024]{1,0:T(8,128)(2,1)S(1)} %pack.1.mine_ref), channel_id=1, source_target_pairs={{0,4},{1,5},{2,6},{3,7},{4,0},{5,1},{6,2},{7,3},{8,12},{9,13},{10,... | collective-permute-start | bytes 245768 | tf_op jit(solution)/shard_map/ppermute | solution.py:433
  17.3 5.6 %collective-permute-start.3 = (s16[40,1024]{1,0:T(8,128)(2,1)S(1)}, s16[40,1024]{1,0:T(8,128)(2,1)S(1)}, u32[]{:S(2)}, u32[]{:S(2)}) collective-permute-start(s16[40,1024]{1,0:T(8,128)(2,1)S(1)} %pack.1.mine_ref), channel_id=1, source_target_pairs={{0,2},{1,3},{2,0},{3,1},{4,6},{5,7},{6,4},{7,5},{8,10},{9,11},{10,... | collective-permute-start | bytes 245768 | tf_op jit(solution)/shard_map/ppermute | solution.py:433
  18.1 8.4 %collective-permute-start.8 = (bf16[128,1024]{1,0:T(8,128)(2,1)S(1)}, bf16[128,1024]{1,0:T(8,128)(2,1)S(1)}, u32[]{:S(2)}, u32[]{:S(2)}) collective-permute-start(bf16[128,1024]{1,0:T(8,128)(2,1)S(1)} %get-tuple-element.40), channel_id=1, source_target_pairs={{0,8},{8,0},{16,24},{24,16},{1,9},{9,1},{17,25},{25,17},{2,10},{10... | collective-permute-start | bytes 786440 | tf_op jit(solution)/shard_map/ppermute | solution.py:432
  20.0 6.4 %collective-permute-start.9 = (bf16[128,1024]{1,0:T(8,128)(2,1)S(1)}, bf16[128,1024]{1,0:T(8,128)(2,1)S(1)}, u32[]{:S(2)}, u32[]{:S(2)}) collective-permute-start(bf16[128,1024]{1,0:T(8,128)(2,1)S(1)} %get-tuple-element.41), channel_id=1, source_target_pairs={{0,16},{8,24},{16,0},{24,8},{1,17},{9,25},{17,1},{25,9},{2,18},{10... | collective-permute-start | bytes 786440 | tf_op jit(solution)/shard_map/ppermute | solution.py:432
  23.0 1.7 %collective-permute-start.7 = (s16[160,1024]{1,0:T(8,128)(2,1)S(1)}, s16[160,1024]{1,0:T(8,128)(2,1)S(1)}, u32[]{:S(2)}, u32[]{:S(2)}) collective-permute-start(s16[160,1024]{1,0:T(8,128)(2,1)S(1)} %pad_add_fusion), channel_id=1, source_target_pairs={{0,1},{1,0},{2,3},{3,2},{4,5},{5,4},{6,7},{7,6},{8,9},{9,8},{10,11... | collective-permute-start | bytes 983048 | tf_op jit(solution)/shard_map/ppermute | solution.py:438
  27.6 9.2 %collective-permute-start.10 = (bf16[128,512]{1,0:T(8,128)(2,1)S(1)}, bf16[128,512]{1,0:T(8,128)(2,1)S(1)}, u32[]{:S(2)}, u32[]{:S(2)}) collective-permute-start(bf16[128,512]{1,0:T(8,128)(2,1)S(1)} %get-tuple-element.43), channel_id=1, source_target_pairs={{8,0},{0,8},{24,16},{16,24},{9,1},{1,9},{25,17},{17,25},{10,2},{2,... | collective-permute-start | bytes 393224 | tf_op jit(solution)/shard_map/ppermute | solution.py:441
  28.2 8.6 %collective-permute-start.11 = (bf16[128,512]{1,0:T(8,128)(2,1)S(1)}, bf16[128,512]{1,0:T(8,128)(2,1)S(1)}, u32[]{:S(2)}, u32[]{:S(2)}) collective-permute-start(bf16[128,512]{1,0:T(8,128)(2,1)S(1)} %get-tuple-element.44), channel_id=1, source_target_pairs={{16,0},{24,8},{0,16},{8,24},{17,1},{25,9},{1,17},{9,25},{18,2},{26... | collective-permute-start | bytes 393224 | tf_op jit(solution)/shard_map/ppermute | solution.py:441
  28.7 8.1 %collective-permute-start.12 = (bf16[128,512]{1,0:T(8,128)(2,1)S(1)}, bf16[128,512]{1,0:T(8,128)(2,1)S(1)}, u32[]{:S(2)}, u32[]{:S(2)}) collective-permute-start(bf16[128,512]{1,0:T(8,128)(2,1)S(1)} %get-tuple-element.45), channel_id=1, source_target_pairs={{24,0},{16,8},{8,16},{0,24},{25,1},{17,9},{9,17},{1,25},{26,2},{18... | collective-permute-start | bytes 393224 | tf_op jit(solution)/shard_map/ppermute | solution.py:441

commit v5 on v4

--- a/solution.py
+++ b/solution.py
@@ -9,6 +9,7 @@
 from jax.sharding import PartitionSpec as P
 
 PRIOR = 16
+TAIL = 4
 MIB = 1 << 20
 F32 = jnp.float32
 BF16 = jnp.bfloat16
@@ -182,9 +183,8 @@
 
 
 def pack_kernel(meta_ref, sums_ref, *refs):
-    heads, out_ref = refs[:-1], refs[-1]
+    heads, out_ref = refs[:-1][::-1], refs[-1]
     blocks, width = sums_ref.shape
-    rows = out_ref.shape[0]
     chunks = width // 128
     lane = iota((1, 128), 1)
     slots, counts = meta_ref[0:1, :], meta_ref[1:2, :]
@@ -193,41 +193,45 @@
         arrived.append(jnp.concatenate([head[j : j + 1, :] for j in range(chunks)], axis=1))
         slots = jnp.where(lane == blocks + k, head[chunks + 1 : chunks + 2, :], slots)
         counts = jnp.where(lane == blocks + k, head[chunks : chunks + 1, :], counts)
-    spare = rows - blocks - len(heads)
-    coded, exponent = coded_rows(
-        jnp.concatenate([sums_ref[...]] + arrived + [jnp.zeros((spare, width), F32)], axis=0)
-    )
-    extra = jnp.concatenate([slots, counts, as_lanes(exponent)], axis=0).astype(I32)
-    extra = jnp.concatenate([extra, jnp.zeros((3, width - 128), I32)], axis=1)
-    out_ref[...] = jnp.concatenate([coded[: rows - 3], extra], axis=0).astype(I16)
+    coded, exponent = coded_rows(jnp.concatenate([sums_ref[...]] + arrived, axis=0))
+    facts = jnp.concatenate([slots, counts, as_lanes(exponent)], axis=1).astype(I32)
+    facts = jnp.concatenate([facts, jnp.zeros((1, width - 384), I32)], axis=1)
+    tail = jnp.concatenate([coded[blocks:]] + [jnp.zeros((1, width), I32)] * (TAIL - 1 - len(heads)) + [facts], axis=0)
+    parts = [coded[j : j + 8] for j in range(0, blocks, 8)]
+    parts.append(jnp.concatenate([tail[:, : width // 2], tail[:, width // 2 :]], axis=0))
+    out_ref[...] = jnp.concatenate(parts, axis=1).astype(I16)
 
 
 def pack(meta, sums, heads):
     blocks, width = sums.shape
-    rows = blocks + -(-(len(heads) + 3) // 8) * 8
+    size = blocks // 8 * width + width // 2
     return pl.pallas_call(
         pack_kernel,
-        out_shape=shaped((rows, width), I16),
+        out_shape=shaped((8, size), I16),
         in_specs=[VMEM] * (2 + len(heads)),
         out_specs=VMEM,
         compiler_params=params(8),
-        cost_estimate=cost(6 * 10**9, 6 * rows * width),
+        cost_estimate=cost(6 * 10**9, 48 * size),
         name="pack",
-    )(meta, sums, *heads)
-
-
-def add_up(sources, blocks, lists):
-    rows, width = sources[0].shape
-    span = 4 if rows - blocks == 8 else rows - blocks
-    fill = -len(sources) % (8 // span) if span < 8 else 0
-    big = jnp.concatenate([x[:blocks] for x in sources], axis=0)
-    small = [x[blocks : blocks + span] for x in sources] + [jnp.zeros((span, width), I32)] * fill
-    small = jnp.concatenate(small, axis=0)
+    )(meta, sums, *heads[::-1])
+
+
+def unpacked(packed, blocks, width):
+    big = jnp.concatenate([packed[:, j * width : (j + 1) * width] for j in range(blocks // 8)], axis=0)
+    tail = packed[:, blocks // 8 * width :]
+    return big, jnp.concatenate([tail[:TAIL], tail[TAIL:]], axis=1)
+
+
+def add_up(sources, blocks, lists, width):
+    sources = [unpacked(x, blocks, width) for x in sources]
+    fill = len(sources) % 2
+    big = jnp.concatenate([x for x, _ in sources], axis=0)
+    small = jnp.concatenate([x for _, x in sources] + [jnp.zeros((TAIL, width), I32)] * fill, axis=0)
 
     def lanes(which, spare):
-        facts = [x[rows - 3 + which : rows - 2 + which, 0:128].astype(F32) for x in sources]
+        facts = [x[TAIL - 1 :, 128 * which : 128 * which + 128].astype(F32) for _, x in sources]
         wide = jnp.concatenate([x[:, 0:blocks] for x in facts], axis=1)
-        tail = [x[:, blocks : blocks + span] for x in facts] + [jnp.full((1, span), spare, F32)] * fill
+        tail = [x[:, blocks : blocks + TAIL] for x in facts] + [jnp.full((1, TAIL), spare, F32)] * fill
         return wide, jnp.concatenate(tail, axis=1)
 
     def four(pair, low=True):
@@ -250,7 +254,7 @@
 def prior_kernel(blocks, mine_ref, old_ref, sums_ref, totals_ref):
     lists = old_ref.shape[0]
     prior = 1.0 * PRIOR
-    sums, totals = add_up([mine_ref[...].astype(I32)], blocks, lists)
+    sums, totals = add_up([mine_ref[...].astype(I32)], blocks, lists, old_ref.shape[1])
     sums_ref[...] = sums + prior * old_ref[...].astype(F32)
     totals_ref[...] = jnp.broadcast_to(totals + prior, totals_ref.shape)
 
@@ -274,8 +278,9 @@
     lists, width = sums_ref.shape
     rows = near[0].shape[0]
     sources = [ref[...].astype(I32) for ref in near]
-    sources += [far[j * rows : (j + 1) * rows, :].astype(I32) for j in range(n_near + 1)]
-    sums, totals = add_up(sources, blocks, lists)
+    far_all = far[...].astype(I32)
+    sources += [far_all[j * rows : (j + 1) * rows] for j in range(n_near + 1)]
+    sums, totals = add_up(sources, blocks, lists, width)
     totals = totals_ref[:, 0:1] + totals
     table = ((sums_ref[...] + sums) * (1.0 / totals)).astype(BF16)
     table_ref[...] = table
@@ -424,7 +429,7 @@
     cores = [(i, i ^ 1) for i in range(n_rows)]
 
     alive, meta, picks, heads, rows = movers(n_groups, lists_group, block_list, home_pos, counts, keep, vectors)
-    heads = [lax.ppermute(x, "grp", pairs) for x, pairs in zip(heads, there)]
+    heads = [lax.ppermute(x, "grp", pairs) for x, pairs in zip(heads[::-1], there[::-1])][::-1]
     sums = block_sums(alive, vectors)
     last = lax.ppermute(rows[-1], "grp", there[-1])
     mine = pack(meta, sums, heads)
@@ -432,8 +437,8 @@
     rows = [lax.ppermute(x, "grp", pairs) for x, pairs in zip(rows, there)]
     near = [lax.ppermute(mine, "row", pairs) for pairs in along]
     sums, totals = with_prior(blocks, mine, old_centroids)
+    near, last = lax.optimization_barrier((near, last))
     both = jnp.concatenate([mine] + near, axis=0)
-    both, last = lax.optimization_barrier((both, last))
     rows.append(last)
     far = lax.ppermute(both, "row", cores)
     table, norms, share = make_table(n_rows, blocks, near, far, sums, totals)

time: 38.5 us -> 38 us (0.987)
  waiting for transfers between devices: 5.82 us -> 4.22 us
  starting transfers between devices: 16.1 us -> 17.2 us
    ppermute x2, starting transfers between devices: 0.66 us -> 1.68 us  [local(): rows = [lax.ppermute(x, 'grp', pairs) for x, pairs in zip(rows, there)]]
    ppermute x3, waiting for transfers between devices: 4.19 us -> 3.19 us  [local(): near = [lax.ppermute(mine, 'row', pairs) for pairs in along]]
    ppermute x3, waiting for transfers between devices: 0.58 us -> 0.02 us  [local(): lax.ppermute(x, 'grp', pairs)]
  transfers between devices with their start and end apart: 13 -> 13, of which waited for: 4 -> 3; matrix products, arithmetic and copies ran while one was open for 0% -> 0% of each run, Pallas kernels for 24% -> 25%
where the time goes in v5:
time: 38 us; the launch traced here: 37.9 us
  starting transfers between devices  17.2 us (45%)
  Pallas kernels  15.7 us (41%)
  waiting for transfers between devices  4.22 us (11%)
  between operations  0.74 us (2%)
    pallas_call x1, Pallas kernels, scores_of(): pl.pallas_call(scores_kernel, out_shape=shaped((rows, lists), F32), in_sp...  5.59 us
    ppermute x3, starting transfers between devices, local(): lax.ppermute(x, 'grp', pairs)  4.6 us
    ppermute x3, starting transfers between devices, local(): near = [lax.ppermute(mine, 'row', pairs) for pairs in along]  4.42 us
    pallas_call x1, Pallas kernels, movers(): pl.pallas_call(functools.partial(movers_kernel, n_groups, lists_group), o...  3.6 us
    ppermute x3, starting transfers between devices, local(): parts = [lax.ppermute(x, 'grp', pairs) for x, pairs in zip(parts, back)]  3.55 us
    ppermute x3, waiting for transfers between devices, local(): near = [lax.ppermute(mine, 'row', pairs) for pairs in along]  3.19 us
    ppermute x1, starting transfers between devices, local(): last = lax.ppermute(rows[-1], 'grp', there[-1])  2.85 us
    pallas_call x1, Pallas kernels, make_table(): pl.pallas_call(functools.partial(table_kernel, blocks, len(near)), out_sh...  1.83 us
  transfers between devices with their start and end apart: 13, of which 3 were waited for; matrix products, arithmetic and copies ran while one was open for 0% of the time, Pallas kernels for 25%

profile of v5, /device:TPU:0, one launch (start us, length us, event | category | flops | bytes accessed | tf_op | source)
XLA Modules:
  0.0 37.9 jit_solution(17187560093140474673)
XLA Ops:
  0.6 3.6 %movers.1 = (f32[32,128]{1,0:T(8,128)S(1)}, f32[8,128]{1,0:T(8,128)S(1)}, s32[3]{0:T(128)S(1)}, f32[16,128]{1,0:T(8,128)S(1)}, f32[16,128]{1,0:T(8,128)S(1)}, /*...) custom-call(s32[1024]{0:T(1024)} %list_ref.1, ...), custom_call_target="tpu_custom_call" | custom-call | flops 786432 | bytes 2359296 | tf_op jit(solution)/shard_map/movers/pallas_call | solution.py:139
  4.2 4.0 %collective-permute-start = (f32[16,128]{1,0:T(8,128)S(1)}, f32[16,128]{1,0:T(8,128)S(1)}, u32[]{:S(2)}, u32[]{:S(2)}) collective-permute-start(f32[16,128]{1,0:T(8,128)S(1)} %get-tuple-element.28), channel_id=1, source_target_pairs={{0,24},{8,16},{16,8},{24,0},{1,25},{9,17},{17,9},{25,1},{2,26},{10... | collective-permute-start | bytes 24584 | tf_op jit(solution)/shard_map/ppermute | solution.py:432
  8.2 0.5 %collective-permute-start.1 = (f32[16,128]{1,0:T(8,128)S(1)}, f32[16,128]{1,0:T(8,128)S(1)}, u32[]{:S(2)}, u32[]{:S(2)}) collective-permute-start(f32[16,128]{1,0:T(8,128)S(1)} %get-tuple-element.29), channel_id=1, source_target_pairs={{0,16},{8,24},{16,0},{24,8},{1,17},{9,25},{17,1},{25,9},{2,18},{10... | collective-permute-start | bytes 24584 | tf_op jit(solution)/shard_map/ppermute | solution.py:432
  8.7 0.1 collective-permute-start.2
  8.8 2.8 %collective-permute-start.6 = (bf16[128,1024]{1,0:T(8,128)(2,1)S(1)}, bf16[128,1024]{1,0:T(8,128)(2,1)S(1)}, u32[]{:S(2)}, u32[]{:S(2)}) collective-permute-start(bf16[128,1024]{1,0:T(8,128)(2,1)S(1)} %get-tuple-element.34), channel_id=1, source_target_pairs={{0,24},{8,16},{16,8},{24,0},{1,25},{9,17},{17,9},{25,1},{2,26},{10... | collective-permute-start | bytes 786440 | tf_op jit(solution)/shard_map/ppermute | solution.py:434
  11.7 1.2 %block_sums.1.sums_ref = f32[32,1024]{1,0:T(8,128)S(1)} custom-call(f32[32,128]{1,0:T(8,128)S(1)} %get-tuple-element.27.alive_ref, bf16[4096,1024]{1,0:T(8,128)(2,1)S(1)} %copy-done), custom_call_target="tpu_custom_call" | custom-call | flops 67108864 | bytes 8388608 | tf_op jit(solution)/shard_map/block_sums/pallas_call | solution.py:174
  12.9 0.0 collective-permute-done.refs_0_
  12.9 0.0 collective-permute-done.1.refs_1_
  12.9 0.0 collective-permute-done.2.refs_2_
  12.9 0.0 copy-start.1
  12.9 0.2 pack.1.mine_ref
  13.1 3.6 %collective-permute-start.5 = (s16[8,4608]{1,0:T(8,128)(2,1)S(1)}, s16[8,4608]{1,0:T(8,128)(2,1)S(1)}, u32[]{:S(2)}, u32[]{:S(2)}) collective-permute-start(s16[8,4608]{1,0:T(8,128)(2,1)S(1)} %pack.1.mine_ref), channel_id=1, source_target_pairs={{0,6},{1,7},{2,4},{3,5},{4,2},{5,3},{6,0},{7,1},{8,14},{9,15},{10,... | collective-permute-start | bytes 221192 | tf_op jit(solution)/shard_map/ppermute | solution.py:438
  16.7 0.0 collective-permute-start.4
  16.7 0.8 %collective-permute-start.3 = (s16[8,4608]{1,0:T(8,128)(2,1)S(1)}, s16[8,4608]{1,0:T(8,128)(2,1)S(1)}, u32[]{:S(2)}, u32[]{:S(2)}) collective-permute-start(s16[8,4608]{1,0:T(8,128)(2,1)S(1)} %pack.1.mine_ref), channel_id=1, source_target_pairs={{0,2},{1,3},{2,0},{3,1},{4,6},{5,7},{6,4},{7,5},{8,10},{9,11},{10,... | collective-permute-start | bytes 221192 | tf_op jit(solution)/shard_map/ppermute | solution.py:438
  17.5 0.5 %collective-permute-start.8 = (bf16[128,1024]{1,0:T(8,128)(2,1)S(1)}, bf16[128,1024]{1,0:T(8,128)(2,1)S(1)}, u32[]{:S(2)}, u32[]{:S(2)}) collective-permute-start(bf16[128,1024]{1,0:T(8,128)(2,1)S(1)} %get-tuple-element.44), channel_id=1, source_target_pairs={{0,8},{8,0},{16,24},{24,16},{1,9},{9,1},{17,25},{25,17},{2,10},{10... | collective-permute-start | bytes 786440 | tf_op jit(solution)/shard_map/ppermute | solution.py:437
  18.1 1.3 %collective-permute-done.5.refs_2_ = s16[8,4608]{1,0:T(8,128)(2,1)S(1)} collective-permute-done((s16[8,4608]{1,0:T(8,128)(2,1)S(1)}, s16[8,4608]{1,0:T(8,128)(2,1)S(1)}, u32[]{:S(2)}, u32[]{:S(2)}) %collective-permute-start.5) | collective-permute-done | bytes 73760 | tf_op jit(solution)/shard_map/ppermute | solution.py:438
  19.4 1.1 %collective-permute-start.9 = (bf16[128,1024]{1,0:T(8,128)(2,1)S(1)}, bf16[128,1024]{1,0:T(8,128)(2,1)S(1)}, u32[]{:S(2)}, u32[]{:S(2)}) collective-permute-start(bf16[128,1024]{1,0:T(8,128)(2,1)S(1)} %get-tuple-element.45), channel_id=1, source_target_pairs={{0,16},{8,24},{16,0},{24,8},{1,17},{9,25},{17,1},{25,9},{2,18},{10... | collective-permute-start | bytes 786440 | tf_op jit(solution)/shard_map/ppermute | solution.py:437
  20.5 1.9 %collective-permute-done.4.refs_1_ = s16[8,4608]{1,0:T(8,128)(2,1)S(1)} collective-permute-done((s16[8,4608]{1,0:T(8,128)(2,1)S(1)}, s16[8,4608]{1,0:T(8,128)(2,1)S(1)}, u32[]{:S(2)}, u32[]{:S(2)}) %collective-permute-start.4) | collective-permute-done | bytes 73760 | tf_op jit(solution)/shard_map/ppermute | solution.py:438
  22.4 0.0 collective-permute-done.3.refs_0_
  22.4 0.0 collective-permute-done.6.refs_2_
  22.4 0.1 collective-permute-start.7
  22.5 0.6 %prior.1 = (f32[512,1024]{1,0:T(8,128)S(1)}, f32[512,128]{1,0:T(8,128)S(1)}) custom-call(s16[8,4608]{1,0:T(8,128)(2,1)S(1)} %pack.1.mine_ref, bf16[512,1024]{1,0:T(8,128)(2,1)S(1)} %copy-done.1), custom_call_target="tpu_custom_call" | custom-call | flops 10485760000 | bytes 4194304 | tf_op jit(solution)/shard_map/prior/pallas_call | solution.py:264
  23.1 1.0 %collective-permute-done.7.refs_3_ = s16[32,4608]{1,0:T(8,128)(2,1)S(1)} collective-permute-done((s16[32,4608]{1,0:T(8,128)(2,1)S(1)}, s16[32,4608]{1,0:T(8,128)(2,1)S(1)}, u32[]{:S(2)}, u32[]{:S(2)}) %collective-permute-start.7) | collective-permute-done | bytes 294944 | tf_op jit(solution)/shard_map/ppermute | solution.py:443
  24.1 1.8 %table.1 = (bf16[512,1024]{1,0:T(8,128)(2,1)S(1)}, f32[8,512]{1,0:T(8,128)S(1)}, bf16[64,1024]{1,0:T(8,128)(2,1)}) custom-call(s16[8,4608]{1,0:T(8,128)(2,1)S(1)} %collective-permute-done.3.refs_0_, s16[8,4608]{1,0:T(8,128)(2,1)S(1)} %collective-permute-done.4.refs_1_, s16[8,4608]{1,0:T(8,128)(2,1)S(1)} %collective-permute-done.5.refs_2_, ...), custom_call_target="tpu_custom_call" | custom-call | flops 1048576000 | bytes 4194304 | tf_op jit(solution)/shard_map/table/pallas_call | solution.py:305
  25.9 0.0 collective-permute-done.8.refs_0_
  25.9 1.2 %parts.1 = (bf16[128,512]{1,0:T(8,128)(2,1)S(1)}, bf16[128,512]{1,0:T(8,128)(2,1)S(1)}, bf16[128,512]{1,0:T(8,128)(2,1)S(1)}) custom-call(f32[8,512]{1,0:T(8,128)S(1)} %get-tuple-element.42.norms_ref, bf16[512,1024]{1,0:T(8,128)(2,1)S(1)} %get-tuple-element.43.table_ref, bf16[128,1024]{1,0:T(8,128)(2,1)S(1)} %collective-permute-done.8.refs_0_, ...), custom_call_target="tpu_custom_call" | custom-call | flops 402653184 | bytes 1048576 | tf_op jit(solution)/shard_map/parts/pallas_call | solution.py:328
  27.1 0.6 %collective-permute-start.10 = (bf16[128,512]{1,0:T(8,128)(2,1)S(1)}, bf16[128,512]{1,0:T(8,128)(2,1)S(1)}, u32[]{:S(2)}, u32[]{:S(2)}) collective-permute-start(bf16[128,512]{1,0:T(8,128)(2,1)S(1)} %get-tuple-element.47), channel_id=1, source_target_pairs={{8,0},{0,8},{24,16},{16,24},{9,1},{1,9},{25,17},{17,25},{10,2},{2,... | collective-permute-start | bytes 393224 | tf_op jit(solution)/shard_map/ppermute | solution.py:446
  27.7 0.8 %collective-permute-start.11 = (bf16[128,512]{1,0:T(8,128)(2,1)S(1)}, bf16[128,512]{1,0:T(8,128)(2,1)S(1)}, u32[]{:S(2)}, u32[]{:S(2)}) collective-permute-start(bf16[128,512]{1,0:T(8,128)(2,1)S(1)} %get-tuple-element.48), channel_id=1, source_target_pairs={{16,0},{24,8},{0,16},{8,24},{17,1},{25,9},{1,17},{9,25},{18,2},{26... | collective-permute-start | bytes 393224 | tf_op jit(solution)/shard_map/ppermute | solution.py:446
  28.5 2.1 %collective-permute-start.12 = (bf16[128,512]{1,0:T(8,128)(2,1)S(1)}, bf16[128,512]{1,0:T(8,128)(2,1)S(1)}, u32[]{:S(2)}, u32[]{:S(2)}) collective-permute-start(bf16[128,512]{1,0:T(8,128)(2,1)S(1)} %get-tuple-element.49), channel_id=1, source_target_pairs={{24,0},{16,8},{8,16},{0,24},{25,1},{17,9},{9,17},{1,25},{26,2},{18... | collective-permute-start | bytes 393224 | tf_op jit(solution)/shard_map/ppermute | solution.py:446
  30.6 5.6 %scores.1.refs_3_ = f32[4096,512]{1,0:T(8,128)} custom-call(f32[32,128]{1,0:T(8,128)S(1)} %get-tuple-element.27.alive_ref, f32[8,512]{1,0:T(8,128)S(1)} %get-tuple-element.42.norms_ref, bf16[512,1024]{1,0:T(8,128)(2,1)S(1)} %get-tuple-element.43.table_ref, bf16[4096,1024]{1,0:T(8,128)(2,1)S(1)} %copy-done), custom_call_target="tpu_custom_call" | custom-call | flops 4294967296 | bytes 8388608 | tf_op jit(solution)/shard_map/scores/pallas_call | solution.py:365
  36.2 0.0 collective-permute-done.11.refs_1_
  36.3 1.6 %merge.1 = f32[4096,512]{1,0:T(8,128)} custom-call(s32[3]{0:T(128)S(1)} %get-tuple-element.41.picks_ref, f32[32,128]{1,0:T(8,128)S(1)} %get-tuple-element.27.alive_ref, bf16[128,512]{1,0:T(8,128)(2,1)S(1)} %collective-permute-done.10.refs_0_, bf16[128,512]{1,0:T(8,128)(2,1)S(1)} %collective-permute-done.11.refs_1_, ...), custom_call_target="tpu_custom_call", output_to_operand_aliasing={{}: (5, {})} | custom-call | flops 393216 | bytes 1179648 | tf_op jit(solution)/shard_map/merge/pallas_call | solution.py:405
  (7 shorter events, 0.0 us)
Async XLA Ops:
  0.6 11.1 %copy-start = (bf16[4096,1024]{1,0:T(8,128)(2,1)S(1)}, bf16[4096,1024]{1,0:T(8,128)(2,1)}, u32[]{:S(2)}) copy-start(bf16[4096,1024]{1,0:T(8,128)(2,1)} %vec_ref.5) | copy-start | bytes 25165828
  4.2 8.6 %collective-permute-start = (f32[16,128]{1,0:T(8,128)S(1)}, f32[16,128]{1,0:T(8,128)S(1)}, u32[]{:S(2)}, u32[]{:S(2)}) collective-permute-start(f32[16,128]{1,0:T(8,128)S(1)} %get-tuple-element.28), channel_id=1, source_target_pairs={{0,24},{8,16},{16,8},{24,0},{1,25},{9,17},{17,9},{25,1},{2,26},{10... | collective-permute-start | bytes 24584 | tf_op jit(solution)/shard_map/ppermute | solution.py:432
  8.2 4.7 %collective-permute-start.1 = (f32[16,128]{1,0:T(8,128)S(1)}, f32[16,128]{1,0:T(8,128)S(1)}, u32[]{:S(2)}, u32[]{:S(2)}) collective-permute-start(f32[16,128]{1,0:T(8,128)S(1)} %get-tuple-element.29), channel_id=1, source_target_pairs={{0,16},{8,24},{16,0},{24,8},{1,17},{9,25},{17,1},{25,9},{2,18},{10... | collective-permute-start | bytes 24584 | tf_op jit(solution)/shard_map/ppermute | solution.py:432
  8.7 4.2 %collective-permute-start.2 = (f32[16,128]{1,0:T(8,128)S(1)}, f32[16,128]{1,0:T(8,128)S(1)}, u32[]{:S(2)}, u32[]{:S(2)}) collective-permute-start(f32[16,128]{1,0:T(8,128)S(1)} %get-tuple-element.30), channel_id=1, source_target_pairs={{0,8},{8,0},{16,24},{24,16},{1,9},{9,1},{17,25},{25,17},{2,10},{10... | collective-permute-start | bytes 24584 | tf_op jit(solution)/shard_map/ppermute | solution.py:432
  8.8 13.5 %collective-permute-start.6 = (bf16[128,1024]{1,0:T(8,128)(2,1)S(1)}, bf16[128,1024]{1,0:T(8,128)(2,1)S(1)}, u32[]{:S(2)}, u32[]{:S(2)}) collective-permute-start(bf16[128,1024]{1,0:T(8,128)(2,1)S(1)} %get-tuple-element.34), channel_id=1, source_target_pairs={{0,24},{8,16},{16,8},{24,0},{1,25},{9,17},{17,9},{25,1},{2,26},{10... | collective-permute-start | bytes 786440 | tf_op jit(solution)/shard_map/ppermute | solution.py:434
  12.9 9.6 %copy-start.1 = (bf16[512,1024]{1,0:T(8,128)(2,1)S(1)}, bf16[512,1024]{1,0:T(8,128)(2,1)}, u32[]{:S(2)}) copy-start(bf16[512,1024]{1,0:T(8,128)(2,1)} %old_ref.1) | copy-start | bytes 3145732
  13.1 6.2 %collective-permute-start.5 = (s16[8,4608]{1,0:T(8,128)(2,1)S(1)}, s16[8,4608]{1,0:T(8,128)(2,1)S(1)}, u32[]{:S(2)}, u32[]{:S(2)}) collective-permute-start(s16[8,4608]{1,0:T(8,128)(2,1)S(1)} %pack.1.mine_ref), channel_id=1, source_target_pairs={{0,6},{1,7},{2,4},{3,5},{4,2},{5,3},{6,0},{7,1},{8,14},{9,15},{10,... | collective-permute-start | bytes 221192 | tf_op jit(solution)/shard_map/ppermute | solution.py:438
  16.7 5.7 %collective-permute-start.4 = (s16[8,4608]{1,0:T(8,128)(2,1)S(1)}, s16[8,4608]{1,0:T(8,128)(2,1)S(1)}, u32[]{:S(2)}, u32[]{:S(2)}) collective-permute-start(s16[8,4608]{1,0:T(8,128)(2,1)S(1)} %pack.1.mine_ref), channel_id=1, source_target_pairs={{0,4},{1,5},{2,6},{3,7},{4,0},{5,1},{6,2},{7,3},{8,12},{9,13},{10,... | collective-permute-start | bytes 221192 | tf_op jit(solution)/shard_map/ppermute | solution.py:438
  16.7 5.7 %collective-permute-start.3 = (s16[8,4608]{1,0:T(8,128)(2,1)S(1)}, s16[8,4608]{1,0:T(8,128)(2,1)S(1)}, u32[]{:S(2)}, u32[]{:S(2)}) collective-permute-start(s16[8,4608]{1,0:T(8,128)(2,1)S(1)} %pack.1.mine_ref), channel_id=1, source_target_pairs={{0,2},{1,3},{2,0},{3,1},{4,6},{5,7},{6,4},{7,5},{8,10},{9,11},{10,... | collective-permute-start | bytes 221192 | tf_op jit(solution)/shard_map/ppermute | solution.py:438
  17.5 8.4 %collective-permute-start.8 = (bf16[128,1024]{1,0:T(8,128)(2,1)S(1)}, bf16[128,1024]{1,0:T(8,128)(2,1)S(1)}, u32[]{:S(2)}, u32[]{:S(2)}) collective-permute-start(bf16[128,1024]{1,0:T(8,128)(2,1)S(1)} %get-tuple-element.44), channel_id=1, source_target_pairs={{0,8},{8,0},{16,24},{24,16},{1,9},{9,1},{17,25},{25,17},{2,10},{10... | collective-permute-start | bytes 786440 | tf_op jit(solution)/shard_map/ppermute | solution.py:437
  19.4 6.6 %collective-permute-start.9 = (bf16[128,1024]{1,0:T(8,128)(2,1)S(1)}, bf16[128,1024]{1,0:T(8,128)(2,1)S(1)}, u32[]{:S(2)}, u32[]{:S(2)}) collective-permute-start(bf16[128,1024]{1,0:T(8,128)(2,1)S(1)} %get-tuple-element.45), channel_id=1, source_target_pairs={{0,16},{8,24},{16,0},{24,8},{1,17},{9,25},{17,1},{25,9},{2,18},{10... | collective-permute-start | bytes 786440 | tf_op jit(solution)/shard_map/ppermute | solution.py:437
  22.4 1.6 %collective-permute-start.7 = (s16[32,4608]{1,0:T(8,128)(2,1)S(1)}, s16[32,4608]{1,0:T(8,128)(2,1)S(1)}, u32[]{:S(2)}, u32[]{:S(2)}) collective-permute-start(s16[32,4608]{1,0:T(8,128)(2,1)S(1)} %pad_add_fusion), channel_id=1, source_target_pairs={{0,1},{1,0},{2,3},{3,2},{4,5},{5,4},{6,7},{7,6},{8,9},{9,8},{10,11... | collective-permute-start | bytes 884744 | tf_op jit(solution)/shard_map/ppermute | solution.py:443
  27.1 9.2 %collective-permute-start.10 = (bf16[128,512]{1,0:T(8,128)(2,1)S(1)}, bf16[128,512]{1,0:T(8,128)(2,1)S(1)}, u32[]{:S(2)}, u32[]{:S(2)}) collective-permute-start(bf16[128,512]{1,0:T(8,128)(2,1)S(1)} %get-tuple-element.47), channel_id=1, source_target_pairs={{8,0},{0,8},{24,16},{16,24},{9,1},{1,9},{25,17},{17,25},{10,2},{2,... | collective-permute-start | bytes 393224 | tf_op jit(solution)/shard_map/ppermute | solution.py:446
  27.7 8.6 %collective-permute-start.11 = (bf16[128,512]{1,0:T(8,128)(2,1)S(1)}, bf16[128,512]{1,0:T(8,128)(2,1)S(1)}, u32[]{:S(2)}, u32[]{:S(2)}) collective-permute-start(bf16[128,512]{1,0:T(8,128)(2,1)S(1)} %get-tuple-element.48), channel_id=1, source_target_pairs={{16,0},{24,8},{0,16},{8,24},{17,1},{25,9},{1,17},{9,25},{18,2},{26... | collective-permute-start | bytes 393224 | tf_op jit(solution)/shard_map/ppermute | solution.py:446
  28.5 7.8 %collective-permute-start.12 = (bf16[128,512]{1,0:T(8,128)(2,1)S(1)}, bf16[128,512]{1,0:T(8,128)(2,1)S(1)}, u32[]{:S(2)}, u32[]{:S(2)}) collective-permute-start(bf16[128,512]{1,0:T(8,128)(2,1)S(1)} %get-tuple-element.49), channel_id=1, source_target_pairs={{24,0},{16,8},{8,16},{0,24},{25,1},{17,9},{9,17},{1,25},{26,2},{18... | collective-permute-start | bytes 393224 | tf_op jit(solution)/shard_map/ppermute | solution.py:446

commit v6 on v5

--- a/solution.py
+++ b/solution.py
@@ -82,17 +82,18 @@
     blocks, block = keep_ref.shape
     group = lax.axis_index("grp")
     base = (group * lax.axis_size("row") + lax.axis_index("row")) * blocks
+    shift = lists_group.bit_length() - 1
     lane = iota((1, block), 1)
     row = iota((blocks, block), 0)
     slots = jnp.full((1, block), -1, I32)
     filled = jnp.zeros((blocks, block), I32)
     picks = [jnp.int32(-1)] * steps
     homes = [jnp.int32(-1)] * steps
-    for load in loads:
+    for load in loads[:2]:
         load.wait()
     for b in range(blocks):
         home = pos[lists[base + b]]
-        home_group = home // lists_group
+        home_group = home >> shift if lists_group == 1 << shift else home // lists_group
         slot = home - home_group * lists_group
         slots = jnp.where((lane == b) & (home_group == group), slot, slots)
         for k in range(steps):
@@ -105,6 +106,8 @@
         start = pl.multiple_of(jnp.maximum(picks[k], 0) * block, block)
         fetches.append(pltpu.make_async_copy(vec_ref.at[pl.ds(start, block), :], row_refs[k], sems.at[k]))
         fetches[k].start()
+    for load in loads[2:]:
+        load.wait()
     for b in range(blocks):
         filled = jnp.where(row == b, fill[b], filled)
     alive = held[...].astype(F32) * (iota((blocks, block), 1) < filled).astype(F32)
@@ -251,35 +254,32 @@
     return sums, totals
 
 
-def prior_kernel(blocks, mine_ref, old_ref, sums_ref, totals_ref):
+def prior_kernel(blocks, *refs):
+    near, (old_ref, sums_ref, totals_ref) = refs[:-3], refs[-3:]
     lists = old_ref.shape[0]
     prior = 1.0 * PRIOR
-    sums, totals = add_up([mine_ref[...].astype(I32)], blocks, lists, old_ref.shape[1])
+    sums, totals = add_up([ref[...].astype(I32) for ref in near], blocks, lists, old_ref.shape[1])
     sums_ref[...] = sums + prior * old_ref[...].astype(F32)
     totals_ref[...] = jnp.broadcast_to(totals + prior, totals_ref.shape)
 
 
-def with_prior(blocks, mine, old):
+def with_prior(blocks, near, old):
     lists, width = old.shape
     return pl.pallas_call(
         functools.partial(prior_kernel, blocks),
         out_shape=[shaped((lists, width), F32), shaped((lists, 128), F32)],
-        in_specs=[VMEM] * 2,
+        in_specs=[VMEM] * (1 + len(near)),
         out_specs=[VMEM] * 2,
         compiler_params=params(16),
         cost_estimate=cost(20000 * lists * width, 8 * lists * width),
         name="prior",
-    )(mine, old)
-
-
-def table_kernel(blocks, n_near, *refs):
-    near, far = refs[:n_near], refs[n_near]
-    sums_ref, totals_ref, table_ref, norms_ref, share_ref = refs[n_near + 1 :]
+    )(*near, old)
+
+
+def table_kernel(blocks, far, sums_ref, totals_ref, table_ref, norms_ref, share_ref):
     lists, width = sums_ref.shape
-    rows = near[0].shape[0]
-    sources = [ref[...].astype(I32) for ref in near]
     far_all = far[...].astype(I32)
-    sources += [far_all[j * rows : (j + 1) * rows] for j in range(n_near + 1)]
+    sources = [far_all[j : j + 8] for j in range(0, far.shape[0], 8)]
     sums, totals = add_up(sources, blocks, lists, width)
     totals = totals_ref[:, 0:1] + totals
     table = ((sums_ref[...] + sums) * (1.0 / totals)).astype(BF16)
@@ -300,17 +300,17 @@
     norms_ref[...] = norms[0:8] * (1.0 / math.sqrt(width))
 
 
-def make_table(n_rows, blocks, near, far, sums, totals):
+def make_table(n_rows, blocks, far, sums, totals):
     lists, width = sums.shape
     return pl.pallas_call(
-        functools.partial(table_kernel, blocks, len(near)),
+        functools.partial(table_kernel, blocks),
         out_shape=[shaped((lists, width), BF16), shaped((8, lists), F32), shaped((lists // n_rows, width), BF16)],
-        in_specs=[VMEM] * (len(near) + 3),
+        in_specs=[VMEM] * 3,
         out_specs=[VMEM] * 3,
         compiler_params=params(24),
         cost_estimate=cost(2000 * lists * width, 8 * lists * width),
         name="table",
-    )(*near, far, sums, totals)
+    )(far, sums, totals)
 
 
 def parts_kernel(norms_ref, table_ref, *refs):
@@ -435,13 +435,14 @@
     mine = pack(meta, sums, heads)
     mine, *rows = lax.optimization_barrier((mine, *rows[:-1]))
     rows = [lax.ppermute(x, "grp", pairs) for x, pairs in zip(rows, there)]
-    near = [lax.ppermute(mine, "row", pairs) for pairs in along]
-    sums, totals = with_prior(blocks, mine, old_centroids)
+    order = sorted(range(chips - 1), key=lambda i: (i + 1 == chips - 1, i == 0))
+    near = [lax.ppermute(mine, "row", along[i]) for i in order]
+    sums, totals = with_prior(blocks, [mine] + near, old_centroids)
     near, last = lax.optimization_barrier((near, last))
     both = jnp.concatenate([mine] + near, axis=0)
     rows.append(last)
     far = lax.ppermute(both, "row", cores)
-    table, norms, share = make_table(n_rows, blocks, near, far, sums, totals)
+    table, norms, share = make_table(n_rows, blocks, far, sums, totals)
     parts = parts_of(norms, table, rows)
     parts = [lax.ppermute(x, "grp", pairs) for x, pairs in zip(parts, back)]
     scores = scores_of(alive, norms, table, vectors)

time: 38 us -> 37.5 us (0.987)
  Pallas kernels: 15.7 us -> 15.3 us
    ppermute x2, waiting for transfers between devices: 0.01 us -> 0.51 us  [local(): rows = [lax.ppermute(x, 'grp', pairs) for x, pairs in zip(rows, there)]]
    ppermute x3, waiting for transfers between devices: 3.19 us -> 2.76 us  [local(): near = [lax.ppermute(mine, 'row', along[i]) for i in order]]
  transfers between devices with their start and end apart: 13 -> 13, of which waited for: 3 -> 5; matrix products, arithmetic and copies ran while one was open for 0% -> 0% of each run, Pallas kernels for 25% -> 25%
where the time goes in v6:
time: 37.5 us; the launch traced here: 37.3 us
  starting transfers between devices  17.2 us (46%)
  Pallas kernels  15.3 us (41%)
  waiting for transfers between devices  4.04 us (11%)
  between operations  0.74 us (2%)
    pallas_call x1, Pallas kernels, scores_of(): pl.pallas_call(scores_kernel, out_shape=shaped((rows, lists), F32), in_sp...  5.59 us
    ppermute x3, starting transfers between devices, local(): lax.ppermute(x, 'grp', pairs)  4.6 us
    ppermute x3, starting transfers between devices, local(): near = [lax.ppermute(mine, 'row', along[i]) for i in order]  4.42 us
    ppermute x3, starting transfers between devices, local(): parts = [lax.ppermute(x, 'grp', pairs) for x, pairs in zip(parts, back)]  3.55 us
    pallas_call x1, Pallas kernels, movers(): pl.pallas_call(functools.partial(movers_kernel, n_groups, lists_group), o...  3.31 us
    ppermute x1, starting transfers between devices, local(): last = lax.ppermute(rows[-1], 'grp', there[-1])  2.85 us
    ppermute x3, waiting for transfers between devices, local(): near = [lax.ppermute(mine, 'row', along[i]) for i in order]  2.76 us
    ppermute x2, starting transfers between devices, local(): rows = [lax.ppermute(x, 'grp', pairs) for x, pairs in zip(rows, there)]  1.7 us
  transfers between devices with their start and end apart: 13, of which 5 were waited for; matrix products, arithmetic and copies ran while one was open for 0% of the time, Pallas kernels for 25%

profile of v6, /device:TPU:0, one launch (start us, length us, event | category | flops | bytes accessed | tf_op | source)
XLA Modules:
  0.0 37.3 jit_solution(16868776797343451208)
XLA Ops:
  0.6 3.3 %movers.1 = (f32[32,128]{1,0:T(8,128)S(1)}, f32[8,128]{1,0:T(8,128)S(1)}, s32[3]{0:T(128)S(1)}, f32[16,128]{1,0:T(8,128)S(1)}, f32[16,128]{1,0:T(8,128)S(1)}, /*...) custom-call(s32[1024]{0:T(1024)} %list_ref.1, ...), custom_call_target="tpu_custom_call" | custom-call | flops 786432 | bytes 2359296 | tf_op jit(solution)/shard_map/movers/pallas_call | solution.py:142
  4.0 4.0 %collective-permute-start = (f32[16,128]{1,0:T(8,128)S(1)}, f32[16,128]{1,0:T(8,128)S(1)}, u32[]{:S(2)}, u32[]{:S(2)}) collective-permute-start(f32[16,128]{1,0:T(8,128)S(1)} %get-tuple-element.28), channel_id=1, source_target_pairs={{0,24},{8,16},{16,8},{24,0},{1,25},{9,17},{17,9},{25,1},{2,26},{10... | collective-permute-start | bytes 24584 | tf_op jit(solution)/shard_map/ppermute | solution.py:432
  7.9 0.5 %collective-permute-start.1 = (f32[16,128]{1,0:T(8,128)S(1)}, f32[16,128]{1,0:T(8,128)S(1)}, u32[]{:S(2)}, u32[]{:S(2)}) collective-permute-start(f32[16,128]{1,0:T(8,128)S(1)} %get-tuple-element.29), channel_id=1, source_target_pairs={{0,16},{8,24},{16,0},{24,8},{1,17},{9,25},{17,1},{25,9},{2,18},{10... | collective-permute-start | bytes 24584 | tf_op jit(solution)/shard_map/ppermute | solution.py:432
  8.4 0.1 collective-permute-start.2
  8.6 2.8 %collective-permute-start.6 = (bf16[128,1024]{1,0:T(8,128)(2,1)S(1)}, bf16[128,1024]{1,0:T(8,128)(2,1)S(1)}, u32[]{:S(2)}, u32[]{:S(2)}) collective-permute-start(bf16[128,1024]{1,0:T(8,128)(2,1)S(1)} %get-tuple-element.34), channel_id=1, source_target_pairs={{0,24},{8,16},{16,8},{24,0},{1,25},{9,17},{17,9},{25,1},{2,26},{10... | collective-permute-start | bytes 786440 | tf_op jit(solution)/shard_map/ppermute | solution.py:434
  11.4 1.2 %block_sums.1.sums_ref = f32[32,1024]{1,0:T(8,128)S(1)} custom-call(f32[32,128]{1,0:T(8,128)S(1)} %get-tuple-element.27.alive_ref, bf16[4096,1024]{1,0:T(8,128)(2,1)S(1)} %copy-done), custom_call_target="tpu_custom_call" | custom-call | flops 67108864 | bytes 8388608 | tf_op jit(solution)/shard_map/block_sums/pallas_call | solution.py:177
  12.6 0.0 collective-permute-done.refs_0_
  12.6 0.0 collective-permute-done.1.refs_1_
  12.6 0.0 collective-permute-done.2.refs_2_
  12.6 0.0 copy-start.1
  12.6 0.2 pack.1.refs_0_
  12.8 3.6 %collective-permute-start.5 = (s16[8,4608]{1,0:T(8,128)(2,1)S(1)}, s16[8,4608]{1,0:T(8,128)(2,1)S(1)}, u32[]{:S(2)}, u32[]{:S(2)}) collective-permute-start(s16[8,4608]{1,0:T(8,128)(2,1)S(1)} %pack.1.refs_0_), channel_id=1, source_target_pairs={{0,6},{1,7},{2,4},{3,5},{4,2},{5,3},{6,0},{7,1},{8,14},{9,15},{10,... | collective-permute-start | bytes 221192 | tf_op jit(solution)/shard_map/ppermute | solution.py:439
  16.4 0.0 collective-permute-start.4
  16.4 0.8 %collective-permute-start.3 = (s16[8,4608]{1,0:T(8,128)(2,1)S(1)}, s16[8,4608]{1,0:T(8,128)(2,1)S(1)}, u32[]{:S(2)}, u32[]{:S(2)}) collective-permute-start(s16[8,4608]{1,0:T(8,128)(2,1)S(1)} %pack.1.refs_0_), channel_id=1, source_target_pairs={{0,4},{1,5},{2,6},{3,7},{4,0},{5,1},{6,2},{7,3},{8,12},{9,13},{10,... | collective-permute-start | bytes 221192 | tf_op jit(solution)/shard_map/ppermute | solution.py:439
  17.2 0.5 %collective-permute-start.8 = (bf16[128,1024]{1,0:T(8,128)(2,1)S(1)}, bf16[128,1024]{1,0:T(8,128)(2,1)S(1)}, u32[]{:S(2)}, u32[]{:S(2)}) collective-permute-start(bf16[128,1024]{1,0:T(8,128)(2,1)S(1)} %get-tuple-element.44), channel_id=1, source_target_pairs={{0,8},{8,0},{16,24},{24,16},{1,9},{9,1},{17,25},{25,17},{2,10},{10... | collective-permute-start | bytes 786440 | tf_op jit(solution)/shard_map/ppermute | solution.py:437
  17.8 1.4 %collective-permute-done.5.refs_3_ = s16[8,4608]{1,0:T(8,128)(2,1)S(1)} collective-permute-done((s16[8,4608]{1,0:T(8,128)(2,1)S(1)}, s16[8,4608]{1,0:T(8,128)(2,1)S(1)}, u32[]{:S(2)}, u32[]{:S(2)}) %collective-permute-start.5) | collective-permute-done | bytes 73760 | tf_op jit(solution)/shard_map/ppermute | solution.py:439
  19.1 1.2 %collective-permute-start.9 = (bf16[128,1024]{1,0:T(8,128)(2,1)S(1)}, bf16[128,1024]{1,0:T(8,128)(2,1)S(1)}, u32[]{:S(2)}, u32[]{:S(2)}) collective-permute-start(bf16[128,1024]{1,0:T(8,128)(2,1)S(1)} %get-tuple-element.45), channel_id=1, source_target_pairs={{0,16},{8,24},{16,0},{24,8},{1,17},{9,25},{17,1},{25,9},{2,18},{10... | collective-permute-start | bytes 786440 | tf_op jit(solution)/shard_map/ppermute | solution.py:437
  20.3 0.5 %collective-permute-done.4.refs_2_ = s16[8,4608]{1,0:T(8,128)(2,1)S(1)} collective-permute-done((s16[8,4608]{1,0:T(8,128)(2,1)S(1)}, s16[8,4608]{1,0:T(8,128)(2,1)S(1)}, u32[]{:S(2)}, u32[]{:S(2)}) %collective-permute-start.4) | collective-permute-done | bytes 73760 | tf_op jit(solution)/shard_map/ppermute | solution.py:439
  20.8 0.9 %collective-permute-done.3.refs_1_ = s16[8,4608]{1,0:T(8,128)(2,1)S(1)} collective-permute-done((s16[8,4608]{1,0:T(8,128)(2,1)S(1)}, s16[8,4608]{1,0:T(8,128)(2,1)S(1)}, u32[]{:S(2)}, u32[]{:S(2)}) %collective-permute-start.3) | collective-permute-done | bytes 73760 | tf_op jit(solution)/shard_map/ppermute | solution.py:439
  21.7 0.1 collective-permute-start.7
  21.8 0.8 %prior.1 = (f32[512,1024]{1,0:T(8,128)S(1)}, f32[512,128]{1,0:T(8,128)S(1)}) custom-call(s16[8,4608]{1,0:T(8,128)(2,1)S(1)} %pack.1.refs_0_, s16[8,4608]{1,0:T(8,128)(2,1)S(1)} %collective-permute-done.3.refs_1_, s16[8,4608]{1,0:T(8,128)(2,1)S(1)} %collective-permute-done.4.refs_2_, s16[8,4608]{1,0:T(8,128)(2,1)S(1)} %collective-permute-done.5.refs_3_, ...), custom_call_target="tpu_custom_call" | custom-call | flops 10485760000 | bytes 4194304 | tf_op jit(solution)/shard_map/prior/pallas_call | solution.py:268
  22.6 0.7 %collective-permute-done.7.far = s16[32,4608]{1,0:T(8,128)(2,1)S(1)} collective-permute-done((s16[32,4608]{1,0:T(8,128)(2,1)S(1)}, s16[32,4608]{1,0:T(8,128)(2,1)S(1)}, u32[]{:S(2)}, u32[]{:S(2)}) %collective-permute-start.7) | collective-permute-done | bytes 294944 | tf_op jit(solution)/shard_map/ppermute | solution.py:444
  23.4 1.6 %table.1 = (bf16[512,1024]{1,0:T(8,128)(2,1)S(1)}, f32[8,512]{1,0:T(8,128)S(1)}, bf16[64,1024]{1,0:T(8,128)(2,1)}) custom-call(s16[32,4608]{1,0:T(8,128)(2,1)S(1)} %collective-permute-done.7.far, f32[512,1024]{1,0:T(8,128)S(1)} %get-tuple-element.38.sums_ref, f32[512,128]{1,0:T(8,128)S(1)} %get-tuple-element.39.totals_ref), custom_call_target="tpu_custom_call" | custom-call | flops 1048576000 | bytes 4194304 | tf_op jit(solution)/shard_map/table/pallas_call | solution.py:305
  25.0 0.5 %collective-permute-done.9.refs_1_ = bf16[128,1024]{1,0:T(8,128)(2,1)S(1)} collective-permute-done((bf16[128,1024]{1,0:T(8,128)(2,1)S(1)}, bf16[128,1024]{1,0:T(8,128)(2,1)S(1)}, u32[]{:S(2)}, u32[]{:S(2)}) %collective-permute-start.9) | collective-permute-done | bytes 262176 | tf_op jit(solution)/shard_map/ppermute | solution.py:437
  25.5 1.2 %parts.1 = (bf16[128,512]{1,0:T(8,128)(2,1)S(1)}, bf16[128,512]{1,0:T(8,128)(2,1)S(1)}, bf16[128,512]{1,0:T(8,128)(2,1)S(1)}) custom-call(f32[8,512]{1,0:T(8,128)S(1)} %get-tuple-element.42.norms_ref, bf16[512,1024]{1,0:T(8,128)(2,1)S(1)} %get-tuple-element.43.table_ref, bf16[128,1024]{1,0:T(8,128)(2,1)S(1)} %collective-permute-done.8.refs_0_, ...), custom_call_target="tpu_custom_call" | custom-call | flops 402653184 | bytes 1048576 | tf_op jit(solution)/shard_map/parts/pallas_call | solution.py:328
  26.7 0.6 %collective-permute-start.10 = (bf16[128,512]{1,0:T(8,128)(2,1)S(1)}, bf16[128,512]{1,0:T(8,128)(2,1)S(1)}, u32[]{:S(2)}, u32[]{:S(2)}) collective-permute-start(bf16[128,512]{1,0:T(8,128)(2,1)S(1)} %get-tuple-element.47), channel_id=1, source_target_pairs={{8,0},{0,8},{24,16},{16,24},{9,1},{1,9},{25,17},{17,25},{10,2},{2,... | collective-permute-start | bytes 393224 | tf_op jit(solution)/shard_map/ppermute | solution.py:447
  27.3 0.9 %collective-permute-start.11 = (bf16[128,512]{1,0:T(8,128)(2,1)S(1)}, bf16[128,512]{1,0:T(8,128)(2,1)S(1)}, u32[]{:S(2)}, u32[]{:S(2)}) collective-permute-start(bf16[128,512]{1,0:T(8,128)(2,1)S(1)} %get-tuple-element.48), channel_id=1, source_target_pairs={{16,0},{24,8},{0,16},{8,24},{17,1},{25,9},{1,17},{9,25},{18,2},{26... | collective-permute-start | bytes 393224 | tf_op jit(solution)/shard_map/ppermute | solution.py:447
  28.2 2.0 %collective-permute-start.12 = (bf16[128,512]{1,0:T(8,128)(2,1)S(1)}, bf16[128,512]{1,0:T(8,128)(2,1)S(1)}, u32[]{:S(2)}, u32[]{:S(2)}) collective-permute-start(bf16[128,512]{1,0:T(8,128)(2,1)S(1)} %get-tuple-element.49), channel_id=1, source_target_pairs={{24,0},{16,8},{8,16},{0,24},{25,1},{17,9},{9,17},{1,25},{26,2},{18... | collective-permute-start | bytes 393224 | tf_op jit(solution)/shard_map/ppermute | solution.py:447
  30.2 5.6 %scores.1.refs_3_ = f32[4096,512]{1,0:T(8,128)} custom-call(f32[32,128]{1,0:T(8,128)S(1)} %get-tuple-element.27.alive_ref, f32[8,512]{1,0:T(8,128)S(1)} %get-tuple-element.42.norms_ref, bf16[512,1024]{1,0:T(8,128)(2,1)S(1)} %get-tuple-element.43.table_ref, bf16[4096,1024]{1,0:T(8,128)(2,1)S(1)} %copy-done), custom_call_target="tpu_custom_call" | custom-call | flops 4294967296 | bytes 8388608 | tf_op jit(solution)/shard_map/scores/pallas_call | solution.py:365
  35.8 0.0 collective-permute-done.11.refs_1_
  35.8 0.0 collective-permute-done.12.refs_2_
  35.8 1.5 %merge.1 = f32[4096,512]{1,0:T(8,128)} custom-call(s32[3]{0:T(128)S(1)} %get-tuple-element.41.picks_ref, f32[32,128]{1,0:T(8,128)S(1)} %get-tuple-element.27.alive_ref, bf16[128,512]{1,0:T(8,128)(2,1)S(1)} %collective-permute-done.10.refs_0_, bf16[128,512]{1,0:T(8,128)(2,1)S(1)} %collective-permute-done.11.refs_1_, ...), custom_call_target="tpu_custom_call", output_to_operand_aliasing={{}: (5, {})} | custom-call | flops 393216 | bytes 1179648 | tf_op jit(solution)/shard_map/merge/pallas_call | solution.py:405
  (7 shorter events, 0.0 us)
Async XLA Ops:
  0.6 10.8 %copy-start = (bf16[4096,1024]{1,0:T(8,128)(2,1)S(1)}, bf16[4096,1024]{1,0:T(8,128)(2,1)}, u32[]{:S(2)}) copy-start(bf16[4096,1024]{1,0:T(8,128)(2,1)} %vec_ref.5) | copy-start | bytes 25165828
  4.0 8.6 %collective-permute-start = (f32[16,128]{1,0:T(8,128)S(1)}, f32[16,128]{1,0:T(8,128)S(1)}, u32[]{:S(2)}, u32[]{:S(2)}) collective-permute-start(f32[16,128]{1,0:T(8,128)S(1)} %get-tuple-element.28), channel_id=1, source_target_pairs={{0,24},{8,16},{16,8},{24,0},{1,25},{9,17},{17,9},{25,1},{2,26},{10... | collective-permute-start | bytes 24584 | tf_op jit(solution)/shard_map/ppermute | solution.py:432
  7.9 4.7 %collective-permute-start.1 = (f32[16,128]{1,0:T(8,128)S(1)}, f32[16,128]{1,0:T(8,128)S(1)}, u32[]{:S(2)}, u32[]{:S(2)}) collective-permute-start(f32[16,128]{1,0:T(8,128)S(1)} %get-tuple-element.29), channel_id=1, source_target_pairs={{0,16},{8,24},{16,0},{24,8},{1,17},{9,25},{17,1},{25,9},{2,18},{10... | collective-permute-start | bytes 24584 | tf_op jit(solution)/shard_map/ppermute | solution.py:432
  8.4 4.2 %collective-permute-start.2 = (f32[16,128]{1,0:T(8,128)S(1)}, f32[16,128]{1,0:T(8,128)S(1)}, u32[]{:S(2)}, u32[]{:S(2)}) collective-permute-start(f32[16,128]{1,0:T(8,128)S(1)} %get-tuple-element.30), channel_id=1, source_target_pairs={{0,8},{8,0},{16,24},{24,16},{1,9},{9,1},{17,25},{25,17},{2,10},{10... | collective-permute-start | bytes 24584 | tf_op jit(solution)/shard_map/ppermute | solution.py:432
  8.6 13.1 %collective-permute-start.6 = (bf16[128,1024]{1,0:T(8,128)(2,1)S(1)}, bf16[128,1024]{1,0:T(8,128)(2,1)S(1)}, u32[]{:S(2)}, u32[]{:S(2)}) collective-permute-start(bf16[128,1024]{1,0:T(8,128)(2,1)S(1)} %get-tuple-element.34), channel_id=1, source_target_pairs={{0,24},{8,16},{16,8},{24,0},{1,25},{9,17},{17,9},{25,1},{2,26},{10... | collective-permute-start | bytes 786440 | tf_op jit(solution)/shard_map/ppermute | solution.py:434
  12.6 9.2 %copy-start.1 = (bf16[512,1024]{1,0:T(8,128)(2,1)S(1)}, bf16[512,1024]{1,0:T(8,128)(2,1)}, u32[]{:S(2)}) copy-start(bf16[512,1024]{1,0:T(8,128)(2,1)} %refs_4_.1) | copy-start | bytes 3145732
  12.8 6.3 %collective-permute-start.5 = (s16[8,4608]{1,0:T(8,128)(2,1)S(1)}, s16[8,4608]{1,0:T(8,128)(2,1)S(1)}, u32[]{:S(2)}, u32[]{:S(2)}) collective-permute-start(s16[8,4608]{1,0:T(8,128)(2,1)S(1)} %pack.1.refs_0_), channel_id=1, source_target_pairs={{0,6},{1,7},{2,4},{3,5},{4,2},{5,3},{6,0},{7,1},{8,14},{9,15},{10,... | collective-permute-start | bytes 221192 | tf_op jit(solution)/shard_map/ppermute | solution.py:439
  16.4 4.4 %collective-permute-start.4 = (s16[8,4608]{1,0:T(8,128)(2,1)S(1)}, s16[8,4608]{1,0:T(8,128)(2,1)S(1)}, u32[]{:S(2)}, u32[]{:S(2)}) collective-permute-start(s16[8,4608]{1,0:T(8,128)(2,1)S(1)} %pack.1.refs_0_), channel_id=1, source_target_pairs={{0,2},{1,3},{2,0},{3,1},{4,6},{5,7},{6,4},{7,5},{8,10},{9,11},{10,... | collective-permute-start | bytes 221192 | tf_op jit(solution)/shard_map/ppermute | solution.py:439
  16.4 5.3 %collective-permute-start.3 = (s16[8,4608]{1,0:T(8,128)(2,1)S(1)}, s16[8,4608]{1,0:T(8,128)(2,1)S(1)}, u32[]{:S(2)}, u32[]{:S(2)}) collective-permute-start(s16[8,4608]{1,0:T(8,128)(2,1)S(1)} %pack.1.refs_0_), channel_id=1, source_target_pairs={{0,4},{1,5},{2,6},{3,7},{4,0},{5,1},{6,2},{7,3},{8,12},{9,13},{10,... | collective-permute-start | bytes 221192 | tf_op jit(solution)/shard_map/ppermute | solution.py:439
  17.2 7.7 %collective-permute-start.8 = (bf16[128,1024]{1,0:T(8,128)(2,1)S(1)}, bf16[128,1024]{1,0:T(8,128)(2,1)S(1)}, u32[]{:S(2)}, u32[]{:S(2)}) collective-permute-start(bf16[128,1024]{1,0:T(8,128)(2,1)S(1)} %get-tuple-element.44), channel_id=1, source_target_pairs={{0,8},{8,0},{16,24},{24,16},{1,9},{9,1},{17,25},{25,17},{2,10},{10... | collective-permute-start | bytes 786440 | tf_op jit(solution)/shard_map/ppermute | solution.py:437
  19.1 6.4 %collective-permute-start.9 = (bf16[128,1024]{1,0:T(8,128)(2,1)S(1)}, bf16[128,1024]{1,0:T(8,128)(2,1)S(1)}, u32[]{:S(2)}, u32[]{:S(2)}) collective-permute-start(bf16[128,1024]{1,0:T(8,128)(2,1)S(1)} %get-tuple-element.45), channel_id=1, source_target_pairs={{0,16},{8,24},{16,0},{24,8},{1,17},{9,25},{17,1},{25,9},{2,18},{10... | collective-permute-start | bytes 786440 | tf_op jit(solution)/shard_map/ppermute | solution.py:437
  21.7 1.6 %collective-permute-start.7 = (s16[32,4608]{1,0:T(8,128)(2,1)S(1)}, s16[32,4608]{1,0:T(8,128)(2,1)S(1)}, u32[]{:S(2)}, u32[]{:S(2)}) collective-permute-start(s16[32,4608]{1,0:T(8,128)(2,1)S(1)} %pad_add_fusion), channel_id=1, source_target_pairs={{0,1},{1,0},{2,3},{3,2},{4,5},{5,4},{6,7},{7,6},{8,9},{9,8},{10,11... | collective-permute-start | bytes 884744 | tf_op jit(solution)/shard_map/ppermute | solution.py:444
  26.7 9.2 %collective-permute-start.10 = (bf16[128,512]{1,0:T(8,128)(2,1)S(1)}, bf16[128,512]{1,0:T(8,128)(2,1)S(1)}, u32[]{:S(2)}, u32[]{:S(2)}) collective-permute-start(bf16[128,512]{1,0:T(8,128)(2,1)S(1)} %get-tuple-element.47), channel_id=1, source_target_pairs={{8,0},{0,8},{24,16},{16,24},{9,1},{1,9},{25,17},{17,25},{10,2},{2,... | collective-permute-start | bytes 393224 | tf_op jit(solution)/shard_map/ppermute | solution.py:447
  27.3 8.6 %collective-permute-start.11 = (bf16[128,512]{1,0:T(8,128)(2,1)S(1)}, bf16[128,512]{1,0:T(8,128)(2,1)S(1)}, u32[]{:S(2)}, u32[]{:S(2)}) collective-permute-start(bf16[128,512]{1,0:T(8,128)(2,1)S(1)} %get-tuple-element.48), channel_id=1, source_target_pairs={{16,0},{24,8},{0,16},{8,24},{17,1},{25,9},{1,17},{9,25},{18,2},{26... | collective-permute-start | bytes 393224 | tf_op jit(solution)/shard_map/ppermute | solution.py:447
  28.2 7.6 %collective-permute-start.12 = (bf16[128,512]{1,0:T(8,128)(2,1)S(1)}, bf16[128,512]{1,0:T(8,128)(2,1)S(1)}, u32[]{:S(2)}, u32[]{:S(2)}) collective-permute-start(bf16[128,512]{1,0:T(8,128)(2,1)S(1)} %get-tuple-element.49), channel_id=1, source_target_pairs={{24,0},{16,8},{8,16},{0,24},{25,1},{17,9},{9,17},{1,25},{26,2},{18... | collective-permute-start | bytes 393224 | tf_op jit(solution)/shard_map/ppermute | solution.py:447

commit v7 on v6

--- a/solution.py
+++ b/solution.py
@@ -276,7 +276,7 @@
     )(*near, old)
 
 
-def table_kernel(blocks, far, sums_ref, totals_ref, table_ref, norms_ref, share_ref):
+def table_kernel(blocks, far, sums_ref, totals_ref, row_ref, table_ref, norms_ref, share_ref, part_ref):
     lists, width = sums_ref.shape
     far_all = far[...].astype(I32)
     sources = [far_all[j : j + 8] for j in range(0, far.shape[0], 8)]
@@ -297,20 +297,29 @@
         piece = partial.astype(BF16)
         partial = partial - piece.astype(F32)
         norms = norms + lax.dot_general(ones, piece, ROW_DIMS, preferred_element_type=F32)
-    norms_ref[...] = norms[0:8] * (1.0 / math.sqrt(width))
-
-
-def make_table(n_rows, blocks, far, sums, totals):
+    factor = 1.0 / math.sqrt(width)
+    norms = norms * factor
+    norms_ref[...] = norms[0:8]
+    dots = lax.dot_general(row_ref[...], table, ROW_DIMS, preferred_element_type=F32)
+    part_ref[...] = (dots * (2.0 * factor) - norms[0:1, :]).astype(part_ref.dtype)
+
+
+def make_table(n_rows, blocks, far, sums, totals, rows):
     lists, width = sums.shape
     return pl.pallas_call(
         functools.partial(table_kernel, blocks),
-        out_shape=[shaped((lists, width), BF16), shaped((8, lists), F32), shaped((lists // n_rows, width), BF16)],
-        in_specs=[VMEM] * 3,
-        out_specs=[VMEM] * 3,
+        out_shape=[
+            shaped((lists, width), BF16),
+            shaped((8, lists), F32),
+            shaped((lists // n_rows, width), BF16),
+            shaped((rows.shape[0], lists), BF16),
+        ],
+        in_specs=[VMEM] * 4,
+        out_specs=[VMEM] * 4,
         compiler_params=params(24),
         cost_estimate=cost(2000 * lists * width, 8 * lists * width),
         name="table",
-    )(far, sums, totals)
+    )(far, sums, totals, rows)
 
 
 def parts_kernel(norms_ref, table_ref, *refs):
@@ -442,8 +451,8 @@
     both = jnp.concatenate([mine] + near, axis=0)
     rows.append(last)
     far = lax.ppermute(both, "row", cores)
-    table, norms, share = make_table(n_rows, blocks, far, sums, totals)
-    parts = parts_of(norms, table, rows)
+    table, norms, share, part = make_table(n_rows, blocks, far, sums, totals, rows[-1])
+    parts = [*parts_of(norms, table, rows[:-1]), part]
     parts = [lax.ppermute(x, "grp", pairs) for x, pairs in zip(parts, back)]
     scores = scores_of(alive, norms, table, vectors)
     scores = merge(picks, alive, parts, scores)

time: 37.5 us -> 36.6 us (0.976)
  waiting for transfers between devices: 4.04 us -> 3.54 us
  Pallas kernels: 15.3 us -> 14.9 us
    ppermute x2, waiting for transfers between devices: 0.51 us -> 0.01 us  [local(): rows = [lax.ppermute(x, 'grp', pairs) for x, pairs in zip(rows, there)]]
  transfers between devices with their start and end apart: 13 -> 13, of which waited for: 5 -> 4; matrix products, arithmetic and copies ran while one was open for 0% -> 0% of each run, Pallas kernels for 25% -> 28%
where the time goes in v7:
time: 36.6 us; the launch traced here: 36.4 us
  starting transfers between devices  17.2 us (47%)
  Pallas kernels  14.9 us (41%)
  waiting for transfers between devices  3.54 us (10%)
  between operations  0.74 us (2%)
    pallas_call x1, Pallas kernels, scores_of(): pl.pallas_call(scores_kernel, out_shape=shaped((rows, lists), F32), in_sp...  5.59 us
    ppermute x3, starting transfers between devices, local(): lax.ppermute(x, 'grp', pairs)  4.6 us
    ppermute x3, starting transfers between devices, local(): near = [lax.ppermute(mine, 'row', along[i]) for i in order]  4.42 us
    ppermute x3, starting transfers between devices, local(): parts = [lax.ppermute(x, 'grp', pairs) for x, pairs in zip(parts, back)]  3.55 us
    pallas_call x1, Pallas kernels, movers(): pl.pallas_call(functools.partial(movers_kernel, n_groups, lists_group), o...  3.31 us
    ppermute x1, starting transfers between devices, local(): last = lax.ppermute(rows[-1], 'grp', there[-1])  2.85 us
    ppermute x3, waiting for transfers between devices, local(): near = [lax.ppermute(mine, 'row', along[i]) for i in order]  2.76 us
    ppermute x2, starting transfers between devices, local(): rows = [lax.ppermute(x, 'grp', pairs) for x, pairs in zip(rows, there)]  1.71 us
  transfers between devices with their start and end apart: 13, of which 4 were waited for; matrix products, arithmetic and copies ran while one was open for 0% of the time, Pallas kernels for 28%

profile of v7, /device:TPU:0, one launch (start us, length us, event | category | flops | bytes accessed | tf_op | source)
XLA Modules:
  0.0 36.4 jit_solution(4440446125757649938)
XLA Ops:
  0.6 3.3 %movers.1 = (f32[32,128]{1,0:T(8,128)S(1)}, f32[8,128]{1,0:T(8,128)S(1)}, s32[3]{0:T(128)S(1)}, f32[16,128]{1,0:T(8,128)S(1)}, f32[16,128]{1,0:T(8,128)S(1)}, /*...) custom-call(s32[1024]{0:T(1024)} %list_ref.1, ...), custom_call_target="tpu_custom_call" | custom-call | flops 786432 | bytes 2359296 | tf_op jit(solution)/shard_map/movers/pallas_call | solution.py:142
  4.0 4.0 %collective-permute-start = (f32[16,128]{1,0:T(8,128)S(1)}, f32[16,128]{1,0:T(8,128)S(1)}, u32[]{:S(2)}, u32[]{:S(2)}) collective-permute-start(f32[16,128]{1,0:T(8,128)S(1)} %get-tuple-element.28), channel_id=1, source_target_pairs={{0,24},{8,16},{16,8},{24,0},{1,25},{9,17},{17,9},{25,1},{2,26},{10... | collective-permute-start | bytes 24584 | tf_op jit(solution)/shard_map/ppermute | solution.py:441
  7.9 0.5 %collective-permute-start.1 = (f32[16,128]{1,0:T(8,128)S(1)}, f32[16,128]{1,0:T(8,128)S(1)}, u32[]{:S(2)}, u32[]{:S(2)}) collective-permute-start(f32[16,128]{1,0:T(8,128)S(1)} %get-tuple-element.29), channel_id=1, source_target_pairs={{0,16},{8,24},{16,0},{24,8},{1,17},{9,25},{17,1},{25,9},{2,18},{10... | collective-permute-start | bytes 24584 | tf_op jit(solution)/shard_map/ppermute | solution.py:441
  8.4 0.1 collective-permute-start.2
  8.6 2.8 %collective-permute-start.6 = (bf16[128,1024]{1,0:T(8,128)(2,1)S(1)}, bf16[128,1024]{1,0:T(8,128)(2,1)S(1)}, u32[]{:S(2)}, u32[]{:S(2)}) collective-permute-start(bf16[128,1024]{1,0:T(8,128)(2,1)S(1)} %get-tuple-element.34), channel_id=1, source_target_pairs={{0,24},{8,16},{16,8},{24,0},{1,25},{9,17},{17,9},{25,1},{2,26},{10... | collective-permute-start | bytes 786440 | tf_op jit(solution)/shard_map/ppermute | solution.py:443
  11.4 1.2 %block_sums.1.sums_ref = f32[32,1024]{1,0:T(8,128)S(1)} custom-call(f32[32,128]{1,0:T(8,128)S(1)} %get-tuple-element.27.alive_ref, bf16[4096,1024]{1,0:T(8,128)(2,1)S(1)} %copy-done), custom_call_target="tpu_custom_call" | custom-call | flops 67108864 | bytes 8388608 | tf_op jit(solution)/shard_map/block_sums/pallas_call | solution.py:177
  12.6 0.0 collective-permute-done.refs_0_
  12.6 0.0 collective-permute-done.1.refs_1_
  12.6 0.0 collective-permute-done.2.refs_2_
  12.6 0.0 copy-start.1
  12.6 0.2 pack.1.refs_0_
  12.8 3.6 %collective-permute-start.5 = (s16[8,4608]{1,0:T(8,128)(2,1)S(1)}, s16[8,4608]{1,0:T(8,128)(2,1)S(1)}, u32[]{:S(2)}, u32[]{:S(2)}) collective-permute-start(s16[8,4608]{1,0:T(8,128)(2,1)S(1)} %pack.1.refs_0_), channel_id=1, source_target_pairs={{0,6},{1,7},{2,4},{3,5},{4,2},{5,3},{6,0},{7,1},{8,14},{9,15},{10,... | collective-permute-start | bytes 221192 | tf_op jit(solution)/shard_map/ppermute | solution.py:448
  16.4 0.0 collective-permute-start.4
  16.4 0.8 %collective-permute-start.3 = (s16[8,4608]{1,0:T(8,128)(2,1)S(1)}, s16[8,4608]{1,0:T(8,128)(2,1)S(1)}, u32[]{:S(2)}, u32[]{:S(2)}) collective-permute-start(s16[8,4608]{1,0:T(8,128)(2,1)S(1)} %pack.1.refs_0_), channel_id=1, source_target_pairs={{0,4},{1,5},{2,6},{3,7},{4,0},{5,1},{6,2},{7,3},{8,12},{9,13},{10,... | collective-permute-start | bytes 221192 | tf_op jit(solution)/shard_map/ppermute | solution.py:448
  17.2 0.5 %collective-permute-start.8 = (bf16[128,1024]{1,0:T(8,128)(2,1)S(1)}, bf16[128,1024]{1,0:T(8,128)(2,1)S(1)}, u32[]{:S(2)}, u32[]{:S(2)}) collective-permute-start(bf16[128,1024]{1,0:T(8,128)(2,1)S(1)} %get-tuple-element.45), channel_id=1, source_target_pairs={{0,8},{8,0},{16,24},{24,16},{1,9},{9,1},{17,25},{25,17},{2,10},{10... | collective-permute-start | bytes 786440 | tf_op jit(solution)/shard_map/ppermute | solution.py:446
  17.8 1.3 %collective-permute-done.5.refs_3_ = s16[8,4608]{1,0:T(8,128)(2,1)S(1)} collective-permute-done((s16[8,4608]{1,0:T(8,128)(2,1)S(1)}, s16[8,4608]{1,0:T(8,128)(2,1)S(1)}, u32[]{:S(2)}, u32[]{:S(2)}) %collective-permute-start.5) | collective-permute-done | bytes 73760 | tf_op jit(solution)/shard_map/ppermute | solution.py:448
  19.1 1.2 %collective-permute-start.9 = (bf16[128,1024]{1,0:T(8,128)(2,1)S(1)}, bf16[128,1024]{1,0:T(8,128)(2,1)S(1)}, u32[]{:S(2)}, u32[]{:S(2)}) collective-permute-start(bf16[128,1024]{1,0:T(8,128)(2,1)S(1)} %get-tuple-element.46), channel_id=1, source_target_pairs={{0,16},{8,24},{16,0},{24,8},{1,17},{9,25},{17,1},{25,9},{2,18},{10... | collective-permute-start | bytes 786440 | tf_op jit(solution)/shard_map/ppermute | solution.py:446
  20.3 0.5 %collective-permute-done.4.refs_2_ = s16[8,4608]{1,0:T(8,128)(2,1)S(1)} collective-permute-done((s16[8,4608]{1,0:T(8,128)(2,1)S(1)}, s16[8,4608]{1,0:T(8,128)(2,1)S(1)}, u32[]{:S(2)}, u32[]{:S(2)}) %collective-permute-start.4) | collective-permute-done | bytes 73760 | tf_op jit(solution)/shard_map/ppermute | solution.py:448
  20.8 0.9 %collective-permute-done.3.refs_1_ = s16[8,4608]{1,0:T(8,128)(2,1)S(1)} collective-permute-done((s16[8,4608]{1,0:T(8,128)(2,1)S(1)}, s16[8,4608]{1,0:T(8,128)(2,1)S(1)}, u32[]{:S(2)}, u32[]{:S(2)}) %collective-permute-start.3) | collective-permute-done | bytes 73760 | tf_op jit(solution)/shard_map/ppermute | solution.py:448
  21.7 0.0 collective-permute-done.6.row_ref
  21.7 0.1 collective-permute-start.7
  21.8 0.8 %prior.1 = (f32[512,1024]{1,0:T(8,128)S(1)}, f32[512,128]{1,0:T(8,128)S(1)}) custom-call(s16[8,4608]{1,0:T(8,128)(2,1)S(1)} %pack.1.refs_0_, s16[8,4608]{1,0:T(8,128)(2,1)S(1)} %collective-permute-done.3.refs_1_, s16[8,4608]{1,0:T(8,128)(2,1)S(1)} %collective-permute-done.4.refs_2_, s16[8,4608]{1,0:T(8,128)(2,1)S(1)} %collective-permute-done.5.refs_3_, ...), custom_call_target="tpu_custom_call" | custom-call | flops 10485760000 | bytes 4194304 | tf_op jit(solution)/shard_map/prior/pallas_call | solution.py:268
  22.6 0.7 %collective-permute-done.7.far = s16[32,4608]{1,0:T(8,128)(2,1)S(1)} collective-permute-done((s16[32,4608]{1,0:T(8,128)(2,1)S(1)}, s16[32,4608]{1,0:T(8,128)(2,1)S(1)}, u32[]{:S(2)}, u32[]{:S(2)}) %collective-permute-start.7) | collective-permute-done | bytes 294944 | tf_op jit(solution)/shard_map/ppermute | solution.py:453
  23.4 1.6 %table.1 = (bf16[512,1024]{1,0:T(8,128)(2,1)S(1)}, f32[8,512]{1,0:T(8,128)S(1)}, bf16[64,1024]{1,0:T(8,128)(2,1)}, bf16[128,512]{1,0:T(8,128)(2,1)S(1)}) custom-call(s16[32,4608]{1,0:T(8,128)(2,1)S(1)} %collective-permute-done.7.far, f32[512,1024]{1,0:T(8,128)S(1)} %get-tuple-element.38.sums_ref, f32[512,128]{1,0:T(8,128)S(1)} %get-tuple-element.39.totals_ref, ...), custom_call_target="tpu_custom_call" | custom-call | flops 1048576000 | bytes 4194304 | tf_op jit(solution)/shard_map/table/pallas_call | solution.py:309
  25.0 1.1 %collective-permute-start.12 = (bf16[128,512]{1,0:T(8,128)(2,1)S(1)}, bf16[128,512]{1,0:T(8,128)(2,1)S(1)}, u32[]{:S(2)}, u32[]{:S(2)}) collective-permute-start(bf16[128,512]{1,0:T(8,128)(2,1)S(1)} %get-tuple-element.49), channel_id=1, source_target_pairs={{24,0},{16,8},{8,16},{0,24},{25,1},{17,9},{9,17},{1,25},{26,2},{18... | collective-permute-start | bytes 393224 | tf_op jit(solution)/shard_map/ppermute | solution.py:456
  26.1 0.8 %parts.1 = (bf16[128,512]{1,0:T(8,128)(2,1)S(1)}, bf16[128,512]{1,0:T(8,128)(2,1)S(1)}) custom-call(f32[8,512]{1,0:T(8,128)S(1)} %get-tuple-element.43.norms_ref, bf16[512,1024]{1,0:T(8,128)(2,1)S(1)} %get-tuple-element.44.table_ref, bf16[128,1024]{1,0:T(8,128)(2,1)S(1)} %collective-permute-done.8.refs_0_, bf16[128,1024]{1,0:T(8,128)(2,1)S(1)} %collective-permute-done.9.refs_1_), custom_call_target="tpu_custom_call" | custom-call | flops 268435456 | bytes 1048576 | tf_op jit(solution)/shard_map/parts/pallas_call | solution.py:337
  26.9 1.7 %collective-permute-start.10 = (bf16[128,512]{1,0:T(8,128)(2,1)S(1)}, bf16[128,512]{1,0:T(8,128)(2,1)S(1)}, u32[]{:S(2)}, u32[]{:S(2)}) collective-permute-start(bf16[128,512]{1,0:T(8,128)(2,1)S(1)} %get-tuple-element.47), channel_id=1, source_target_pairs={{8,0},{0,8},{24,16},{16,24},{9,1},{1,9},{25,17},{17,25},{10,2},{2,... | collective-permute-start | bytes 393224 | tf_op jit(solution)/shard_map/ppermute | solution.py:456
  28.6 0.7 %collective-permute-start.11 = (bf16[128,512]{1,0:T(8,128)(2,1)S(1)}, bf16[128,512]{1,0:T(8,128)(2,1)S(1)}, u32[]{:S(2)}, u32[]{:S(2)}) collective-permute-start(bf16[128,512]{1,0:T(8,128)(2,1)S(1)} %get-tuple-element.48), channel_id=1, source_target_pairs={{16,0},{24,8},{0,16},{8,24},{17,1},{25,9},{1,17},{9,25},{18,2},{26... | collective-permute-start | bytes 393224 | tf_op jit(solution)/shard_map/ppermute | solution.py:456
  29.4 5.6 %scores.1.refs_3_ = f32[4096,512]{1,0:T(8,128)} custom-call(f32[32,128]{1,0:T(8,128)S(1)} %get-tuple-element.27.alive_ref, f32[8,512]{1,0:T(8,128)S(1)} %get-tuple-element.43.norms_ref, bf16[512,1024]{1,0:T(8,128)(2,1)S(1)} %get-tuple-element.44.table_ref, bf16[4096,1024]{1,0:T(8,128)(2,1)S(1)} %copy-done), custom_call_target="tpu_custom_call" | custom-call | flops 4294967296 | bytes 8388608 | tf_op jit(solution)/shard_map/scores/pallas_call | solution.py:374
  35.0 0.0 collective-permute-done.10.refs_0_
  35.0 0.0 collective-permute-done.11.refs_1_
  35.0 1.4 %merge.1 = f32[4096,512]{1,0:T(8,128)} custom-call(s32[3]{0:T(128)S(1)} %get-tuple-element.42.picks_ref, f32[32,128]{1,0:T(8,128)S(1)} %get-tuple-element.27.alive_ref, bf16[128,512]{1,0:T(8,128)(2,1)S(1)} %collective-permute-done.10.refs_0_, bf16[128,512]{1,0:T(8,128)(2,1)S(1)} %collective-permute-done.11.refs_1_, ...), custom_call_target="tpu_custom_call", output_to_operand_aliasing={{}: (5, {})} | custom-call | flops 393216 | bytes 1179648 | tf_op jit(solution)/shard_map/merge/pallas_call | solution.py:414
  (7 shorter events, 0.0 us)
Async XLA Ops:
  0.6 10.8 %copy-start = (bf16[4096,1024]{1,0:T(8,128)(2,1)S(1)}, bf16[4096,1024]{1,0:T(8,128)(2,1)}, u32[]{:S(2)}) copy-start(bf16[4096,1024]{1,0:T(8,128)(2,1)} %vec_ref.5) | copy-start | bytes 25165828
  4.0 8.6 %collective-permute-start = (f32[16,128]{1,0:T(8,128)S(1)}, f32[16,128]{1,0:T(8,128)S(1)}, u32[]{:S(2)}, u32[]{:S(2)}) collective-permute-start(f32[16,128]{1,0:T(8,128)S(1)} %get-tuple-element.28), channel_id=1, source_target_pairs={{0,24},{8,16},{16,8},{24,0},{1,25},{9,17},{17,9},{25,1},{2,26},{10... | collective-permute-start | bytes 24584 | tf_op jit(solution)/shard_map/ppermute | solution.py:441
  7.9 4.7 %collective-permute-start.1 = (f32[16,128]{1,0:T(8,128)S(1)}, f32[16,128]{1,0:T(8,128)S(1)}, u32[]{:S(2)}, u32[]{:S(2)}) collective-permute-start(f32[16,128]{1,0:T(8,128)S(1)} %get-tuple-element.29), channel_id=1, source_target_pairs={{0,16},{8,24},{16,0},{24,8},{1,17},{9,25},{17,1},{25,9},{2,18},{10... | collective-permute-start | bytes 24584 | tf_op jit(solution)/shard_map/ppermute | solution.py:441
  8.4 4.2 %collective-permute-start.2 = (f32[16,128]{1,0:T(8,128)S(1)}, f32[16,128]{1,0:T(8,128)S(1)}, u32[]{:S(2)}, u32[]{:S(2)}) collective-permute-start(f32[16,128]{1,0:T(8,128)S(1)} %get-tuple-element.30), channel_id=1, source_target_pairs={{0,8},{8,0},{16,24},{24,16},{1,9},{9,1},{17,25},{25,17},{2,10},{10... | collective-permute-start | bytes 24584 | tf_op jit(solution)/shard_map/ppermute | solution.py:441
  8.6 13.1 %collective-permute-start.6 = (bf16[128,1024]{1,0:T(8,128)(2,1)S(1)}, bf16[128,1024]{1,0:T(8,128)(2,1)S(1)}, u32[]{:S(2)}, u32[]{:S(2)}) collective-permute-start(bf16[128,1024]{1,0:T(8,128)(2,1)S(1)} %get-tuple-element.34), channel_id=1, source_target_pairs={{0,24},{8,16},{16,8},{24,0},{1,25},{9,17},{17,9},{25,1},{2,26},{10... | collective-permute-start | bytes 786440 | tf_op jit(solution)/shard_map/ppermute | solution.py:443
  12.6 9.2 %copy-start.1 = (bf16[512,1024]{1,0:T(8,128)(2,1)S(1)}, bf16[512,1024]{1,0:T(8,128)(2,1)}, u32[]{:S(2)}) copy-start(bf16[512,1024]{1,0:T(8,128)(2,1)} %refs_4_.1) | copy-start | bytes 3145732
  12.8 6.3 %collective-permute-start.5 = (s16[8,4608]{1,0:T(8,128)(2,1)S(1)}, s16[8,4608]{1,0:T(8,128)(2,1)S(1)}, u32[]{:S(2)}, u32[]{:S(2)}) collective-permute-start(s16[8,4608]{1,0:T(8,128)(2,1)S(1)} %pack.1.refs_0_), channel_id=1, source_target_pairs={{0,6},{1,7},{2,4},{3,5},{4,2},{5,3},{6,0},{7,1},{8,14},{9,15},{10,... | collective-permute-start | bytes 221192 | tf_op jit(solution)/shard_map/ppermute | solution.py:448
  16.4 4.4 %collective-permute-start.4 = (s16[8,4608]{1,0:T(8,128)(2,1)S(1)}, s16[8,4608]{1,0:T(8,128)(2,1)S(1)}, u32[]{:S(2)}, u32[]{:S(2)}) collective-permute-start(s16[8,4608]{1,0:T(8,128)(2,1)S(1)} %pack.1.refs_0_), channel_id=1, source_target_pairs={{0,2},{1,3},{2,0},{3,1},{4,6},{5,7},{6,4},{7,5},{8,10},{9,11},{10,... | collective-permute-start | bytes 221192 | tf_op jit(solution)/shard_map/ppermute | solution.py:448
  16.4 5.3 %collective-permute-start.3 = (s16[8,4608]{1,0:T(8,128)(2,1)S(1)}, s16[8,4608]{1,0:T(8,128)(2,1)S(1)}, u32[]{:S(2)}, u32[]{:S(2)}) collective-permute-start(s16[8,4608]{1,0:T(8,128)(2,1)S(1)} %pack.1.refs_0_), channel_id=1, source_target_pairs={{0,4},{1,5},{2,6},{3,7},{4,0},{5,1},{6,2},{7,3},{8,12},{9,13},{10,... | collective-permute-start | bytes 221192 | tf_op jit(solution)/shard_map/ppermute | solution.py:448
  17.2 8.8 %collective-permute-start.8 = (bf16[128,1024]{1,0:T(8,128)(2,1)S(1)}, bf16[128,1024]{1,0:T(8,128)(2,1)S(1)}, u32[]{:S(2)}, u32[]{:S(2)}) collective-permute-start(bf16[128,1024]{1,0:T(8,128)(2,1)S(1)} %get-tuple-element.45), channel_id=1, source_target_pairs={{0,8},{8,0},{16,24},{24,16},{1,9},{9,1},{17,25},{25,17},{2,10},{10... | collective-permute-start | bytes 786440 | tf_op jit(solution)/shard_map/ppermute | solution.py:446
  19.1 7.0 %collective-permute-start.9 = (bf16[128,1024]{1,0:T(8,128)(2,1)S(1)}, bf16[128,1024]{1,0:T(8,128)(2,1)S(1)}, u32[]{:S(2)}, u32[]{:S(2)}) collective-permute-start(bf16[128,1024]{1,0:T(8,128)(2,1)S(1)} %get-tuple-element.46), channel_id=1, source_target_pairs={{0,16},{8,24},{16,0},{24,8},{1,17},{9,25},{17,1},{25,9},{2,18},{10... | collective-permute-start | bytes 786440 | tf_op jit(solution)/shard_map/ppermute | solution.py:446
  21.7 1.6 %collective-permute-start.7 = (s16[32,4608]{1,0:T(8,128)(2,1)S(1)}, s16[32,4608]{1,0:T(8,128)(2,1)S(1)}, u32[]{:S(2)}, u32[]{:S(2)}) collective-permute-start(s16[32,4608]{1,0:T(8,128)(2,1)S(1)} %pad_add_fusion), channel_id=1, source_target_pairs={{0,1},{1,0},{2,3},{3,2},{4,5},{5,4},{6,7},{7,6},{8,9},{9,8},{10,11... | collective-permute-start | bytes 884744 | tf_op jit(solution)/shard_map/ppermute | solution.py:453
  25.0 10.0 %collective-permute-start.12 = (bf16[128,512]{1,0:T(8,128)(2,1)S(1)}, bf16[128,512]{1,0:T(8,128)(2,1)S(1)}, u32[]{:S(2)}, u32[]{:S(2)}) collective-permute-start(bf16[128,512]{1,0:T(8,128)(2,1)S(1)} %get-tuple-element.49), channel_id=1, source_target_pairs={{24,0},{16,8},{8,16},{0,24},{25,1},{17,9},{9,17},{1,25},{26,2},{18... | collective-permute-start | bytes 393224 | tf_op jit(solution)/shard_map/ppermute | solution.py:456
  26.9 8.1 %collective-permute-start.10 = (bf16[128,512]{1,0:T(8,128)(2,1)S(1)}, bf16[128,512]{1,0:T(8,128)(2,1)S(1)}, u32[]{:S(2)}, u32[]{:S(2)}) collective-permute-start(bf16[128,512]{1,0:T(8,128)(2,1)S(1)} %get-tuple-element.47), channel_id=1, source_target_pairs={{8,0},{0,8},{24,16},{16,24},{9,1},{1,9},{25,17},{17,25},{10,2},{2,... | collective-permute-start | bytes 393224 | tf_op jit(solution)/shard_map/ppermute | solution.py:456
  28.6 6.3 %collective-permute-start.11 = (bf16[128,512]{1,0:T(8,128)(2,1)S(1)}, bf16[128,512]{1,0:T(8,128)(2,1)S(1)}, u32[]{:S(2)}, u32[]{:S(2)}) collective-permute-start(bf16[128,512]{1,0:T(8,128)(2,1)S(1)} %get-tuple-element.48), channel_id=1, source_target_pairs={{16,0},{24,8},{0,16},{8,24},{17,1},{25,9},{1,17},{9,25},{18,2},{26... | collective-permute-start | bytes 393224 | tf_op jit(solution)/shard_map/ppermute | solution.py:456

commit v8 on v7

--- a/solution.py
+++ b/solution.py
@@ -351,7 +351,7 @@
     factor = 1.0 / math.sqrt(width)
     norms = norms_ref[0:1, :]
     table = table_ref[...]
-    tile = 4
+    tile = 2
     stores = []
     for t in range(blocks // tile):
         span = slice(t * tile * block, (t + 1) * tile * block)
@@ -376,7 +376,7 @@
         out_shape=shaped((rows, lists), F32),
         in_specs=[VMEM] * 4,
         out_specs=HBM,
-        scratch_shapes=[pltpu.VMEM((rows, lists), F32), pltpu.SemaphoreType.DMA((blocks // 4,))],
+        scratch_shapes=[pltpu.VMEM((rows, lists), F32), pltpu.SemaphoreType.DMA((blocks // 2,))],
         compiler_params=params(24),
         cost_estimate=cost(2 * lists * rows * width, 4 * rows * lists),
         name="scores",
@@ -440,7 +440,8 @@
     alive, meta, picks, heads, rows = movers(n_groups, lists_group, block_list, home_pos, counts, keep, vectors)
     heads = [lax.ppermute(x, "grp", pairs) for x, pairs in zip(heads[::-1], there[::-1])][::-1]
     sums = block_sums(alive, vectors)
-    last = lax.ppermute(rows[-1], "grp", there[-1])
+    last, sums = lax.optimization_barrier((rows[-1], sums))
+    last = lax.ppermute(last, "grp", there[-1])
     mine = pack(meta, sums, heads)
     mine, *rows = lax.optimization_barrier((mine, *rows[:-1]))
     rows = [lax.ppermute(x, "grp", pairs) for x, pairs in zip(rows, there)]

time: 36.6 us -> 36.5 us (level)
  no operation moved by 1% of the time
where the time goes in v8:
time: 36.5 us; the launch traced here: 36.3 us
  starting transfers between devices  17 us (47%)
  Pallas kernels  14.8 us (41%)
  waiting for transfers between devices  3.75 us (10%)
  between operations  0.74 us (2%)
    pallas_call x1, Pallas kernels, scores_of(): pl.pallas_call(scores_kernel, out_shape=shaped((rows, lists), F32), in_sp...  5.48 us
    ppermute x3, starting transfers between devices, local(): lax.ppermute(x, 'grp', pairs)  4.6 us
    ppermute x3, starting transfers between devices, local(): near = [lax.ppermute(mine, 'row', along[i]) for i in order]  4.42 us
    ppermute x3, starting transfers between devices, local(): parts = [lax.ppermute(x, 'grp', pairs) for x, pairs in zip(parts, back)]  3.55 us
    pallas_call x1, Pallas kernels, movers(): pl.pallas_call(functools.partial(movers_kernel, n_groups, lists_group), o...  3.3 us
    ppermute x3, waiting for transfers between devices, local(): near = [lax.ppermute(mine, 'row', along[i]) for i in order]  2.99 us
    ppermute x1, starting transfers between devices, local(): last = lax.ppermute(last, 'grp', there[-1])  2.86 us
    pallas_call x1, Pallas kernels, make_table(): pl.pallas_call(functools.partial(table_kernel, blocks), out_shape=[shaped...  1.6 us
  transfers between devices with their start and end apart: 13, of which 4 were waited for; matrix products, arithmetic and copies ran while one was open for 0% of the time, Pallas kernels for 28%

profile of v8, /device:TPU:0, one launch (start us, length us, event | category | flops | bytes accessed | tf_op | source)
XLA Modules:
  0.0 36.3 jit_solution(12412502231844305267)
XLA Ops:
  0.6 3.3 %movers.1 = (f32[32,128]{1,0:T(8,128)S(1)}, f32[8,128]{1,0:T(8,128)S(1)}, s32[3]{0:T(128)S(1)}, f32[16,128]{1,0:T(8,128)S(1)}, f32[16,128]{1,0:T(8,128)S(1)}, /*...) custom-call(s32[1024]{0:T(1024)} %list_ref.1, ...), custom_call_target="tpu_custom_call" | custom-call | flops 786432 | bytes 2359296 | tf_op jit(solution)/shard_map/movers/pallas_call | solution.py:142
  4.0 4.0 %collective-permute-start = (f32[16,128]{1,0:T(8,128)S(1)}, f32[16,128]{1,0:T(8,128)S(1)}, u32[]{:S(2)}, u32[]{:S(2)}) collective-permute-start(f32[16,128]{1,0:T(8,128)S(1)} %get-tuple-element.32), channel_id=1, source_target_pairs={{0,24},{8,16},{16,8},{24,0},{1,25},{9,17},{17,9},{25,1},{2,26},{10... | collective-permute-start | bytes 24584 | tf_op jit(solution)/shard_map/ppermute | solution.py:441
  7.9 0.5 %collective-permute-start.1 = (f32[16,128]{1,0:T(8,128)S(1)}, f32[16,128]{1,0:T(8,128)S(1)}, u32[]{:S(2)}, u32[]{:S(2)}) collective-permute-start(f32[16,128]{1,0:T(8,128)S(1)} %get-tuple-element.33), channel_id=1, source_target_pairs={{0,16},{8,24},{16,0},{24,8},{1,17},{9,25},{17,1},{25,9},{2,18},{10... | collective-permute-start | bytes 24584 | tf_op jit(solution)/shard_map/ppermute | solution.py:441
  8.4 0.1 collective-permute-start.2
  8.6 1.2 %block_sums.1.sums_ref = f32[32,1024]{1,0:T(8,128)S(1)} custom-call(f32[32,128]{1,0:T(8,128)S(1)} %get-tuple-element.30.alive_ref, bf16[4096,1024]{1,0:T(8,128)(2,1)S(1)} %copy-done), custom_call_target="tpu_custom_call" | custom-call | flops 67108864 | bytes 8388608 | tf_op jit(solution)/shard_map/block_sums/pallas_call | solution.py:177
  9.8 2.9 %collective-permute-start.6 = (bf16[128,1024]{1,0:T(8,128)(2,1)S(1)}, bf16[128,1024]{1,0:T(8,128)(2,1)S(1)}, u32[]{:S(2)}, u32[]{:S(2)}) collective-permute-start(bf16[128,1024]{1,0:T(8,128)(2,1)S(1)} %get-tuple-element.38), channel_id=1, source_target_pairs={{0,24},{8,16},{16,8},{24,0},{1,25},{9,17},{17,9},{25,1},{2,26},{10... | collective-permute-start | bytes 786440 | tf_op jit(solution)/shard_map/ppermute | solution.py:444
  12.6 0.0 collective-permute-done.refs_0_
  12.6 0.0 collective-permute-done.1.refs_1_
  12.6 0.0 copy-start.1
  12.6 0.2 pack.1.refs_0_
  12.8 3.6 %collective-permute-start.5 = (s16[8,4608]{1,0:T(8,128)(2,1)S(1)}, s16[8,4608]{1,0:T(8,128)(2,1)S(1)}, u32[]{:S(2)}, u32[]{:S(2)}) collective-permute-start(s16[8,4608]{1,0:T(8,128)(2,1)S(1)} %pack.1.refs_0_), channel_id=1, source_target_pairs={{0,6},{1,7},{2,4},{3,5},{4,2},{5,3},{6,0},{7,1},{8,14},{9,15},{10,... | collective-permute-start | bytes 221192 | tf_op jit(solution)/shard_map/ppermute | solution.py:449
  16.4 0.8 %collective-permute-start.3 = (s16[8,4608]{1,0:T(8,128)(2,1)S(1)}, s16[8,4608]{1,0:T(8,128)(2,1)S(1)}, u32[]{:S(2)}, u32[]{:S(2)}) collective-permute-start(s16[8,4608]{1,0:T(8,128)(2,1)S(1)} %pack.1.refs_0_), channel_id=1, source_target_pairs={{0,4},{1,5},{2,6},{3,7},{4,0},{5,1},{6,2},{7,3},{8,12},{9,13},{10,... | collective-permute-start | bytes 221192 | tf_op jit(solution)/shard_map/ppermute | solution.py:449
  17.2 0.5 %collective-permute-start.8 = (bf16[128,1024]{1,0:T(8,128)(2,1)S(1)}, bf16[128,1024]{1,0:T(8,128)(2,1)S(1)}, u32[]{:S(2)}, u32[]{:S(2)}) collective-permute-start(bf16[128,1024]{1,0:T(8,128)(2,1)S(1)} %get-tuple-element.49), channel_id=1, source_target_pairs={{0,8},{8,0},{16,24},{24,16},{1,9},{9,1},{17,25},{25,17},{2,10},{10... | collective-permute-start | bytes 786440 | tf_op jit(solution)/shard_map/ppermute | solution.py:447
  17.8 1.4 %collective-permute-done.5.refs_3_ = s16[8,4608]{1,0:T(8,128)(2,1)S(1)} collective-permute-done((s16[8,4608]{1,0:T(8,128)(2,1)S(1)}, s16[8,4608]{1,0:T(8,128)(2,1)S(1)}, u32[]{:S(2)}, u32[]{:S(2)}) %collective-permute-start.5) | collective-permute-done | bytes 73760 | tf_op jit(solution)/shard_map/ppermute | solution.py:449
  19.1 0.9 %collective-permute-start.9 = (bf16[128,1024]{1,0:T(8,128)(2,1)S(1)}, bf16[128,1024]{1,0:T(8,128)(2,1)S(1)}, u32[]{:S(2)}, u32[]{:S(2)}) collective-permute-start(bf16[128,1024]{1,0:T(8,128)(2,1)S(1)} %get-tuple-element.50), channel_id=1, source_target_pairs={{0,16},{8,24},{16,0},{24,8},{1,17},{9,25},{17,1},{25,9},{2,18},{10... | collective-permute-start | bytes 786440 | tf_op jit(solution)/shard_map/ppermute | solution.py:447
  20.1 0.7 %collective-permute-done.4.refs_2_ = s16[8,4608]{1,0:T(8,128)(2,1)S(1)} collective-permute-done((s16[8,4608]{1,0:T(8,128)(2,1)S(1)}, s16[8,4608]{1,0:T(8,128)(2,1)S(1)}, u32[]{:S(2)}, u32[]{:S(2)}) %collective-permute-start.4) | collective-permute-done | bytes 73760 | tf_op jit(solution)/shard_map/ppermute | solution.py:449
  20.8 0.9 %collective-permute-done.3.refs_1_ = s16[8,4608]{1,0:T(8,128)(2,1)S(1)} collective-permute-done((s16[8,4608]{1,0:T(8,128)(2,1)S(1)}, s16[8,4608]{1,0:T(8,128)(2,1)S(1)}, u32[]{:S(2)}, u32[]{:S(2)}) %collective-permute-start.3) | collective-permute-done | bytes 73760 | tf_op jit(solution)/shard_map/ppermute | solution.py:449
  21.7 0.0 collective-permute-done.6.row_ref
  21.7 0.1 collective-permute-start.7
  21.8 0.8 %prior.1 = (f32[512,1024]{1,0:T(8,128)S(1)}, f32[512,128]{1,0:T(8,128)S(1)}) custom-call(s16[8,4608]{1,0:T(8,128)(2,1)S(1)} %pack.1.refs_0_, s16[8,4608]{1,0:T(8,128)(2,1)S(1)} %collective-permute-done.3.refs_1_, s16[8,4608]{1,0:T(8,128)(2,1)S(1)} %collective-permute-done.4.refs_2_, s16[8,4608]{1,0:T(8,128)(2,1)S(1)} %collective-permute-done.5.refs_3_, ...), custom_call_target="tpu_custom_call" | custom-call | flops 10485760000 | bytes 4194304 | tf_op jit(solution)/shard_map/prior/pallas_call | solution.py:268
  22.6 0.7 %collective-permute-done.7.far = s16[32,4608]{1,0:T(8,128)(2,1)S(1)} collective-permute-done((s16[32,4608]{1,0:T(8,128)(2,1)S(1)}, s16[32,4608]{1,0:T(8,128)(2,1)S(1)}, u32[]{:S(2)}, u32[]{:S(2)}) %collective-permute-start.7) | collective-permute-done | bytes 294944 | tf_op jit(solution)/shard_map/ppermute | solution.py:454
  23.4 1.6 %table.1 = (bf16[512,1024]{1,0:T(8,128)(2,1)S(1)}, f32[8,512]{1,0:T(8,128)S(1)}, bf16[64,1024]{1,0:T(8,128)(2,1)}, bf16[128,512]{1,0:T(8,128)(2,1)S(1)}) custom-call(s16[32,4608]{1,0:T(8,128)(2,1)S(1)} %collective-permute-done.7.far, f32[512,1024]{1,0:T(8,128)S(1)} %get-tuple-element.42.sums_ref, f32[512,128]{1,0:T(8,128)S(1)} %get-tuple-element.43.totals_ref, ...), custom_call_target="tpu_custom_call" | custom-call | flops 1048576000 | bytes 4194304 | tf_op jit(solution)/shard_map/table/pallas_call | solution.py:309
  25.0 1.1 %collective-permute-start.12 = (bf16[128,512]{1,0:T(8,128)(2,1)S(1)}, bf16[128,512]{1,0:T(8,128)(2,1)S(1)}, u32[]{:S(2)}, u32[]{:S(2)}) collective-permute-start(bf16[128,512]{1,0:T(8,128)(2,1)S(1)} %get-tuple-element.53), channel_id=1, source_target_pairs={{24,0},{16,8},{8,16},{0,24},{25,1},{17,9},{9,17},{1,25},{26,2},{18... | collective-permute-start | bytes 393224 | tf_op jit(solution)/shard_map/ppermute | solution.py:457
  26.0 0.0 collective-permute-done.8.refs_0_
  26.0 0.0 collective-permute-done.9.refs_1_
  26.0 0.8 %parts.1 = (bf16[128,512]{1,0:T(8,128)(2,1)S(1)}, bf16[128,512]{1,0:T(8,128)(2,1)S(1)}) custom-call(f32[8,512]{1,0:T(8,128)S(1)} %get-tuple-element.47.norms_ref, bf16[512,1024]{1,0:T(8,128)(2,1)S(1)} %get-tuple-element.48.table_ref, bf16[128,1024]{1,0:T(8,128)(2,1)S(1)} %collective-permute-done.8.refs_0_, bf16[128,1024]{1,0:T(8,128)(2,1)S(1)} %collective-permute-done.9.refs_1_), custom_call_target="tpu_custom_call" | custom-call | flops 268435456 | bytes 1048576 | tf_op jit(solution)/shard_map/parts/pallas_call | solution.py:337
  26.9 1.7 %collective-permute-start.10 = (bf16[128,512]{1,0:T(8,128)(2,1)S(1)}, bf16[128,512]{1,0:T(8,128)(2,1)S(1)}, u32[]{:S(2)}, u32[]{:S(2)}) collective-permute-start(bf16[128,512]{1,0:T(8,128)(2,1)S(1)} %get-tuple-element.51), channel_id=1, source_target_pairs={{8,0},{0,8},{24,16},{16,24},{9,1},{1,9},{25,17},{17,25},{10,2},{2,... | collective-permute-start | bytes 393224 | tf_op jit(solution)/shard_map/ppermute | solution.py:457
  28.6 0.8 %collective-permute-start.11 = (bf16[128,512]{1,0:T(8,128)(2,1)S(1)}, bf16[128,512]{1,0:T(8,128)(2,1)S(1)}, u32[]{:S(2)}, u32[]{:S(2)}) collective-permute-start(bf16[128,512]{1,0:T(8,128)(2,1)S(1)} %get-tuple-element.52), channel_id=1, source_target_pairs={{16,0},{24,8},{0,16},{8,24},{17,1},{25,9},{1,17},{9,25},{18,2},{26... | collective-permute-start | bytes 393224 | tf_op jit(solution)/shard_map/ppermute | solution.py:457
  29.4 5.5 %scores.1.refs_3_ = f32[4096,512]{1,0:T(8,128)} custom-call(f32[32,128]{1,0:T(8,128)S(1)} %get-tuple-element.30.alive_ref, f32[8,512]{1,0:T(8,128)S(1)} %get-tuple-element.47.norms_ref, bf16[512,1024]{1,0:T(8,128)(2,1)S(1)} %get-tuple-element.48.table_ref, bf16[4096,1024]{1,0:T(8,128)(2,1)S(1)} %copy-done), custom_call_target="tpu_custom_call" | custom-call | flops 4294967296 | bytes 8388608 | tf_op jit(solution)/shard_map/scores/pallas_call | solution.py:374
  34.9 0.0 collective-permute-done.10.refs_0_
  34.9 0.0 collective-permute-done.11.refs_1_
  34.9 1.4 %merge.1 = f32[4096,512]{1,0:T(8,128)} custom-call(s32[3]{0:T(128)S(1)} %get-tuple-element.46.picks_ref, f32[32,128]{1,0:T(8,128)S(1)} %get-tuple-element.30.alive_ref, bf16[128,512]{1,0:T(8,128)(2,1)S(1)} %collective-permute-done.10.refs_0_, bf16[128,512]{1,0:T(8,128)(2,1)S(1)} %collective-permute-done.11.refs_1_, ...), custom_call_target="tpu_custom_call", output_to_operand_aliasing={{}: (5, {})} | custom-call | flops 393216 | bytes 1179648 | tf_op jit(solution)/shard_map/merge/pallas_call | solution.py:414
  (7 shorter events, 0.0 us)
Async XLA Ops:
  0.6 7.9 %copy-start = (bf16[4096,1024]{1,0:T(8,128)(2,1)S(1)}, bf16[4096,1024]{1,0:T(8,128)(2,1)}, u32[]{:S(2)}) copy-start(bf16[4096,1024]{1,0:T(8,128)(2,1)} %vec_ref.5) | copy-start | bytes 25165828
  4.0 8.7 %collective-permute-start = (f32[16,128]{1,0:T(8,128)S(1)}, f32[16,128]{1,0:T(8,128)S(1)}, u32[]{:S(2)}, u32[]{:S(2)}) collective-permute-start(f32[16,128]{1,0:T(8,128)S(1)} %get-tuple-element.32), channel_id=1, source_target_pairs={{0,24},{8,16},{16,8},{24,0},{1,25},{9,17},{17,9},{25,1},{2,26},{10... | collective-permute-start | bytes 24584 | tf_op jit(solution)/shard_map/ppermute | solution.py:441
  7.9 4.7 %collective-permute-start.1 = (f32[16,128]{1,0:T(8,128)S(1)}, f32[16,128]{1,0:T(8,128)S(1)}, u32[]{:S(2)}, u32[]{:S(2)}) collective-permute-start(f32[16,128]{1,0:T(8,128)S(1)} %get-tuple-element.33), channel_id=1, source_target_pairs={{0,16},{8,24},{16,0},{24,8},{1,17},{9,25},{17,1},{25,9},{2,18},{10... | collective-permute-start | bytes 24584 | tf_op jit(solution)/shard_map/ppermute | solution.py:441
  8.4 4.2 %collective-permute-start.2 = (f32[16,128]{1,0:T(8,128)S(1)}, f32[16,128]{1,0:T(8,128)S(1)}, u32[]{:S(2)}, u32[]{:S(2)}) collective-permute-start(f32[16,128]{1,0:T(8,128)S(1)} %get-tuple-element.34), channel_id=1, source_target_pairs={{0,8},{8,0},{16,24},{24,16},{1,9},{9,1},{17,25},{25,17},{2,10},{10... | collective-permute-start | bytes 24584 | tf_op jit(solution)/shard_map/ppermute | solution.py:441
  9.8 11.9 %collective-permute-start.6 = (bf16[128,1024]{1,0:T(8,128)(2,1)S(1)}, bf16[128,1024]{1,0:T(8,128)(2,1)S(1)}, u32[]{:S(2)}, u32[]{:S(2)}) collective-permute-start(bf16[128,1024]{1,0:T(8,128)(2,1)S(1)} %get-tuple-element.38), channel_id=1, source_target_pairs={{0,24},{8,16},{16,8},{24,0},{1,25},{9,17},{17,9},{25,1},{2,26},{10... | collective-permute-start | bytes 786440 | tf_op jit(solution)/shard_map/ppermute | solution.py:444
  12.6 9.2 %copy-start.1 = (bf16[512,1024]{1,0:T(8,128)(2,1)S(1)}, bf16[512,1024]{1,0:T(8,128)(2,1)}, u32[]{:S(2)}) copy-start(bf16[512,1024]{1,0:T(8,128)(2,1)} %refs_4_.1) | copy-start | bytes 3145732
  12.8 6.3 %collective-permute-start.5 = (s16[8,4608]{1,0:T(8,128)(2,1)S(1)}, s16[8,4608]{1,0:T(8,128)(2,1)S(1)}, u32[]{:S(2)}, u32[]{:S(2)}) collective-permute-start(s16[8,4608]{1,0:T(8,128)(2,1)S(1)} %pack.1.refs_0_), channel_id=1, source_target_pairs={{0,6},{1,7},{2,4},{3,5},{4,2},{5,3},{6,0},{7,1},{8,14},{9,15},{10,... | collective-permute-start | bytes 221192 | tf_op jit(solution)/shard_map/ppermute | solution.py:449
  16.4 4.4 %collective-permute-start.4 = (s16[8,4608]{1,0:T(8,128)(2,1)S(1)}, s16[8,4608]{1,0:T(8,128)(2,1)S(1)}, u32[]{:S(2)}, u32[]{:S(2)}) collective-permute-start(s16[8,4608]{1,0:T(8,128)(2,1)S(1)} %pack.1.refs_0_), channel_id=1, source_target_pairs={{0,2},{1,3},{2,0},{3,1},{4,6},{5,7},{6,4},{7,5},{8,10},{9,11},{10,... | collective-permute-start | bytes 221192 | tf_op jit(solution)/shard_map/ppermute | solution.py:449
  16.4 5.3 %collective-permute-start.3 = (s16[8,4608]{1,0:T(8,128)(2,1)S(1)}, s16[8,4608]{1,0:T(8,128)(2,1)S(1)}, u32[]{:S(2)}, u32[]{:S(2)}) collective-permute-start(s16[8,4608]{1,0:T(8,128)(2,1)S(1)} %pack.1.refs_0_), channel_id=1, source_target_pairs={{0,4},{1,5},{2,6},{3,7},{4,0},{5,1},{6,2},{7,3},{8,12},{9,13},{10,... | collective-permute-start | bytes 221192 | tf_op jit(solution)/shard_map/ppermute | solution.py:449
  17.2 8.8 %collective-permute-start.8 = (bf16[128,1024]{1,0:T(8,128)(2,1)S(1)}, bf16[128,1024]{1,0:T(8,128)(2,1)S(1)}, u32[]{:S(2)}, u32[]{:S(2)}) collective-permute-start(bf16[128,1024]{1,0:T(8,128)(2,1)S(1)} %get-tuple-element.49), channel_id=1, source_target_pairs={{0,8},{8,0},{16,24},{24,16},{1,9},{9,1},{17,25},{25,17},{2,10},{10... | collective-permute-start | bytes 786440 | tf_op jit(solution)/shard_map/ppermute | solution.py:447
  19.1 6.9 %collective-permute-start.9 = (bf16[128,1024]{1,0:T(8,128)(2,1)S(1)}, bf16[128,1024]{1,0:T(8,128)(2,1)S(1)}, u32[]{:S(2)}, u32[]{:S(2)}) collective-permute-start(bf16[128,1024]{1,0:T(8,128)(2,1)S(1)} %get-tuple-element.50), channel_id=1, source_target_pairs={{0,16},{8,24},{16,0},{24,8},{1,17},{9,25},{17,1},{25,9},{2,18},{10... | collective-permute-start | bytes 786440 | tf_op jit(solution)/shard_map/ppermute | solution.py:447
  21.7 1.6 %collective-permute-start.7 = (s16[32,4608]{1,0:T(8,128)(2,1)S(1)}, s16[32,4608]{1,0:T(8,128)(2,1)S(1)}, u32[]{:S(2)}, u32[]{:S(2)}) collective-permute-start(s16[32,4608]{1,0:T(8,128)(2,1)S(1)} %pad_add_fusion), channel_id=1, source_target_pairs={{0,1},{1,0},{2,3},{3,2},{4,5},{5,4},{6,7},{7,6},{8,9},{9,8},{10,11... | collective-permute-start | bytes 884744 | tf_op jit(solution)/shard_map/ppermute | solution.py:454
  25.0 9.9 %collective-permute-start.12 = (bf16[128,512]{1,0:T(8,128)(2,1)S(1)}, bf16[128,512]{1,0:T(8,128)(2,1)S(1)}, u32[]{:S(2)}, u32[]{:S(2)}) collective-permute-start(bf16[128,512]{1,0:T(8,128)(2,1)S(1)} %get-tuple-element.53), channel_id=1, source_target_pairs={{24,0},{16,8},{8,16},{0,24},{25,1},{17,9},{9,17},{1,25},{26,2},{18... | collective-permute-start | bytes 393224 | tf_op jit(solution)/shard_map/ppermute | solution.py:457
  26.9 8.0 %collective-permute-start.10 = (bf16[128,512]{1,0:T(8,128)(2,1)S(1)}, bf16[128,512]{1,0:T(8,128)(2,1)S(1)}, u32[]{:S(2)}, u32[]{:S(2)}) collective-permute-start(bf16[128,512]{1,0:T(8,128)(2,1)S(1)} %get-tuple-element.51), channel_id=1, source_target_pairs={{8,0},{0,8},{24,16},{16,24},{9,1},{1,9},{25,17},{17,25},{10,2},{2,... | collective-permute-start | bytes 393224 | tf_op jit(solution)/shard_map/ppermute | solution.py:457
  28.6 6.3 %collective-permute-start.11 = (bf16[128,512]{1,0:T(8,128)(2,1)S(1)}, bf16[128,512]{1,0:T(8,128)(2,1)S(1)}, u32[]{:S(2)}, u32[]{:S(2)}) collective-permute-start(bf16[128,512]{1,0:T(8,128)(2,1)S(1)} %get-tuple-element.52), channel_id=1, source_target_pairs={{16,0},{24,8},{0,16},{8,24},{17,1},{25,9},{1,17},{9,25},{18,2},{26... | collective-permute-start | bytes 393224 | tf_op jit(solution)/shard_map/ppermute | solution.py:457

commit v9 on v8

--- a/solution.py
+++ b/solution.py
@@ -388,9 +388,12 @@
     parts, out_ref, held, sems = refs[:steps], refs[steps + 1], refs[steps + 2], refs[steps + 3]
     block, lists = parts[0].shape
 
-    def store(k):
-        start = pl.multiple_of(picks_ref[k] * block, block)
-        return pltpu.make_async_copy(held.at[k], out_ref.at[pl.ds(start, block), :], sems.at[k])
+    half = block // 2
+
+    def store(k, part):
+        start = pl.multiple_of(picks_ref[k] * block + part * half, half)
+        here = held.at[k, pl.ds(part * half, half), :]
+        return pltpu.make_async_copy(here, out_ref.at[pl.ds(start, half), :], sems.at[2 * k + part])
 
     for k in range(steps):
 
@@ -398,14 +401,17 @@
         def _():
             weights = turned_weights(alive_ref[pl.ds(picks_ref[k], 1), :])
             weights = jnp.concatenate([weights] * (lists // 128), axis=1)
-            held[k] = parts[k][...].astype(F32) * weights
-            store(k).start()
+            for part in range(2):
+                at = slice(part * half, (part + 1) * half)
+                held[k, at, :] = parts[k][at, :].astype(F32) * weights[at, :]
+                store(k, part).start()
 
     for k in range(steps):
 
         @pl.when(picks_ref[k] >= 0)
         def _():
-            store(k).wait()
+            store(k, 0).wait()
+            store(k, 1).wait()
 
 
 def merge(picks, alive, parts, scores):
@@ -416,7 +422,7 @@
         out_shape=shaped(scores.shape, scores.dtype),
         in_specs=[SMEM, VMEM] + [VMEM] * steps + [HBM],
         out_specs=HBM,
-        scratch_shapes=[pltpu.VMEM((steps, block, lists), F32), pltpu.SemaphoreType.DMA((steps,))],
+        scratch_shapes=[pltpu.VMEM((steps, block, lists), F32), pltpu.SemaphoreType.DMA((2 * steps,))],
         input_output_aliases={2 + steps: 0},
         compiler_params=params(8),
         cost_estimate=cost(2 * steps * block * lists, 6 * steps * block * lists),

time: 36.5 us -> 36.5 us (level)
  no operation moved by 1% of the time
where the time goes in v9:
time: 36.5 us; the launch traced here: 36.3 us
  starting transfers between devices  17 us (47%)
  Pallas kernels  14.8 us (41%)
  waiting for transfers between devices  3.76 us (10%)
  between operations  0.74 us (2%)
    pallas_call x1, Pallas kernels, scores_of(): pl.pallas_call(scores_kernel, out_shape=shaped((rows, lists), F32), in_sp...  5.48 us
    ppermute x3, starting transfers between devices, local(): lax.ppermute(x, 'grp', pairs)  4.6 us
    ppermute x3, starting transfers between devices, local(): near = [lax.ppermute(mine, 'row', along[i]) for i in order]  4.42 us
    ppermute x3, starting transfers between devices, local(): parts = [lax.ppermute(x, 'grp', pairs) for x, pairs in zip(parts, back)]  3.55 us
    pallas_call x1, Pallas kernels, movers(): pl.pallas_call(functools.partial(movers_kernel, n_groups, lists_group), o...  3.3 us
    ppermute x3, waiting for transfers between devices, local(): near = [lax.ppermute(mine, 'row', along[i]) for i in order]  3 us
    ppermute x1, starting transfers between devices, local(): last = lax.ppermute(last, 'grp', there[-1])  2.86 us
    pallas_call x1, Pallas kernels, make_table(): pl.pallas_call(functools.partial(table_kernel, blocks), out_shape=[shaped...  1.6 us
  transfers between devices with their start and end apart: 13, of which 4 were waited for; matrix products, arithmetic and copies ran while one was open for 0% of the time, Pallas kernels for 28%

profile of v9, /device:TPU:0, one launch (start us, length us, event | category | flops | bytes accessed | tf_op | source)
XLA Modules:
  0.0 36.3 jit_solution(9625481683647328068)
XLA Ops:
  0.6 3.3 %movers.1 = (f32[32,128]{1,0:T(8,128)S(1)}, f32[8,128]{1,0:T(8,128)S(1)}, s32[3]{0:T(128)S(1)}, f32[16,128]{1,0:T(8,128)S(1)}, f32[16,128]{1,0:T(8,128)S(1)}, /*...) custom-call(s32[1024]{0:T(1024)} %list_ref.1, ...), custom_call_target="tpu_custom_call" | custom-call | flops 786432 | bytes 2359296 | tf_op jit(solution)/shard_map/movers/pallas_call | solution.py:142
  4.0 4.0 %collective-permute-start = (f32[16,128]{1,0:T(8,128)S(1)}, f32[16,128]{1,0:T(8,128)S(1)}, u32[]{:S(2)}, u32[]{:S(2)}) collective-permute-start(f32[16,128]{1,0:T(8,128)S(1)} %get-tuple-element.32), channel_id=1, source_target_pairs={{0,24},{8,16},{16,8},{24,0},{1,25},{9,17},{17,9},{25,1},{2,26},{10... | collective-permute-start | bytes 24584 | tf_op jit(solution)/shard_map/ppermute | solution.py:447
  7.9 0.5 %collective-permute-start.1 = (f32[16,128]{1,0:T(8,128)S(1)}, f32[16,128]{1,0:T(8,128)S(1)}, u32[]{:S(2)}, u32[]{:S(2)}) collective-permute-start(f32[16,128]{1,0:T(8,128)S(1)} %get-tuple-element.33), channel_id=1, source_target_pairs={{0,16},{8,24},{16,0},{24,8},{1,17},{9,25},{17,1},{25,9},{2,18},{10... | collective-permute-start | bytes 24584 | tf_op jit(solution)/shard_map/ppermute | solution.py:447
  8.4 0.1 collective-permute-start.2
  8.6 1.2 %block_sums.1.sums_ref = f32[32,1024]{1,0:T(8,128)S(1)} custom-call(f32[32,128]{1,0:T(8,128)S(1)} %get-tuple-element.30.alive_ref, bf16[4096,1024]{1,0:T(8,128)(2,1)S(1)} %copy-done), custom_call_target="tpu_custom_call" | custom-call | flops 67108864 | bytes 8388608 | tf_op jit(solution)/shard_map/block_sums/pallas_call | solution.py:177
  9.8 2.9 %collective-permute-start.6 = (bf16[128,1024]{1,0:T(8,128)(2,1)S(1)}, bf16[128,1024]{1,0:T(8,128)(2,1)S(1)}, u32[]{:S(2)}, u32[]{:S(2)}) collective-permute-start(bf16[128,1024]{1,0:T(8,128)(2,1)S(1)} %get-tuple-element.38), channel_id=1, source_target_pairs={{0,24},{8,16},{16,8},{24,0},{1,25},{9,17},{17,9},{25,1},{2,26},{10... | collective-permute-start | bytes 786440 | tf_op jit(solution)/shard_map/ppermute | solution.py:450
  12.6 0.0 collective-permute-done.refs_0_
  12.6 0.0 collective-permute-done.1.refs_1_
  12.6 0.0 collective-permute-done.2.refs_2_
  12.6 0.0 copy-start.1
  12.6 0.2 pack.1.refs_0_
  12.8 3.6 %collective-permute-start.5 = (s16[8,4608]{1,0:T(8,128)(2,1)S(1)}, s16[8,4608]{1,0:T(8,128)(2,1)S(1)}, u32[]{:S(2)}, u32[]{:S(2)}) collective-permute-start(s16[8,4608]{1,0:T(8,128)(2,1)S(1)} %pack.1.refs_0_), channel_id=1, source_target_pairs={{0,6},{1,7},{2,4},{3,5},{4,2},{5,3},{6,0},{7,1},{8,14},{9,15},{10,... | collective-permute-start | bytes 221192 | tf_op jit(solution)/shard_map/ppermute | solution.py:455
  16.4 0.0 collective-permute-start.4
  16.4 0.8 %collective-permute-start.3 = (s16[8,4608]{1,0:T(8,128)(2,1)S(1)}, s16[8,4608]{1,0:T(8,128)(2,1)S(1)}, u32[]{:S(2)}, u32[]{:S(2)}) collective-permute-start(s16[8,4608]{1,0:T(8,128)(2,1)S(1)} %pack.1.refs_0_), channel_id=1, source_target_pairs={{0,4},{1,5},{2,6},{3,7},{4,0},{5,1},{6,2},{7,3},{8,12},{9,13},{10,... | collective-permute-start | bytes 221192 | tf_op jit(solution)/shard_map/ppermute | solution.py:455
  17.2 0.5 %collective-permute-start.8 = (bf16[128,1024]{1,0:T(8,128)(2,1)S(1)}, bf16[128,1024]{1,0:T(8,128)(2,1)S(1)}, u32[]{:S(2)}, u32[]{:S(2)}) collective-permute-start(bf16[128,1024]{1,0:T(8,128)(2,1)S(1)} %get-tuple-element.49), channel_id=1, source_target_pairs={{0,8},{8,0},{16,24},{24,16},{1,9},{9,1},{17,25},{25,17},{2,10},{10... | collective-permute-start | bytes 786440 | tf_op jit(solution)/shard_map/ppermute | solution.py:453
  17.8 1.4 %collective-permute-done.5.refs_3_ = s16[8,4608]{1,0:T(8,128)(2,1)S(1)} collective-permute-done((s16[8,4608]{1,0:T(8,128)(2,1)S(1)}, s16[8,4608]{1,0:T(8,128)(2,1)S(1)}, u32[]{:S(2)}, u32[]{:S(2)}) %collective-permute-start.5) | collective-permute-done | bytes 73760 | tf_op jit(solution)/shard_map/ppermute | solution.py:455
  19.1 0.9 %collective-permute-start.9 = (bf16[128,1024]{1,0:T(8,128)(2,1)S(1)}, bf16[128,1024]{1,0:T(8,128)(2,1)S(1)}, u32[]{:S(2)}, u32[]{:S(2)}) collective-permute-start(bf16[128,1024]{1,0:T(8,128)(2,1)S(1)} %get-tuple-element.50), channel_id=1, source_target_pairs={{0,16},{8,24},{16,0},{24,8},{1,17},{9,25},{17,1},{25,9},{2,18},{10... | collective-permute-start | bytes 786440 | tf_op jit(solution)/shard_map/ppermute | solution.py:453
  20.0 0.7 %collective-permute-done.4.refs_2_ = s16[8,4608]{1,0:T(8,128)(2,1)S(1)} collective-permute-done((s16[8,4608]{1,0:T(8,128)(2,1)S(1)}, s16[8,4608]{1,0:T(8,128)(2,1)S(1)}, u32[]{:S(2)}, u32[]{:S(2)}) %collective-permute-start.4) | collective-permute-done | bytes 73760 | tf_op jit(solution)/shard_map/ppermute | solution.py:455
  20.8 0.9 %collective-permute-done.3.refs_1_ = s16[8,4608]{1,0:T(8,128)(2,1)S(1)} collective-permute-done((s16[8,4608]{1,0:T(8,128)(2,1)S(1)}, s16[8,4608]{1,0:T(8,128)(2,1)S(1)}, u32[]{:S(2)}, u32[]{:S(2)}) %collective-permute-start.3) | collective-permute-done | bytes 73760 | tf_op jit(solution)/shard_map/ppermute | solution.py:455
  21.7 0.0 collective-permute-done.6.row_ref
  21.7 0.1 collective-permute-start.7
  21.8 0.8 %prior.1 = (f32[512,1024]{1,0:T(8,128)S(1)}, f32[512,128]{1,0:T(8,128)S(1)}) custom-call(s16[8,4608]{1,0:T(8,128)(2,1)S(1)} %pack.1.refs_0_, s16[8,4608]{1,0:T(8,128)(2,1)S(1)} %collective-permute-done.3.refs_1_, s16[8,4608]{1,0:T(8,128)(2,1)S(1)} %collective-permute-done.4.refs_2_, s16[8,4608]{1,0:T(8,128)(2,1)S(1)} %collective-permute-done.5.refs_3_, ...), custom_call_target="tpu_custom_call" | custom-call | flops 10485760000 | bytes 4194304 | tf_op jit(solution)/shard_map/prior/pallas_call | solution.py:268
  22.6 0.7 %collective-permute-done.7.far = s16[32,4608]{1,0:T(8,128)(2,1)S(1)} collective-permute-done((s16[32,4608]{1,0:T(8,128)(2,1)S(1)}, s16[32,4608]{1,0:T(8,128)(2,1)S(1)}, u32[]{:S(2)}, u32[]{:S(2)}) %collective-permute-start.7) | collective-permute-done | bytes 294944 | tf_op jit(solution)/shard_map/ppermute | solution.py:460
  23.4 1.6 %table.1 = (bf16[512,1024]{1,0:T(8,128)(2,1)S(1)}, f32[8,512]{1,0:T(8,128)S(1)}, bf16[64,1024]{1,0:T(8,128)(2,1)}, bf16[128,512]{1,0:T(8,128)(2,1)S(1)}) custom-call(s16[32,4608]{1,0:T(8,128)(2,1)S(1)} %collective-permute-done.7.far, f32[512,1024]{1,0:T(8,128)S(1)} %get-tuple-element.42.sums_ref, f32[512,128]{1,0:T(8,128)S(1)} %get-tuple-element.43.totals_ref, ...), custom_call_target="tpu_custom_call" | custom-call | flops 1048576000 | bytes 4194304 | tf_op jit(solution)/shard_map/table/pallas_call | solution.py:309
  25.0 1.1 %collective-permute-start.12 = (bf16[128,512]{1,0:T(8,128)(2,1)S(1)}, bf16[128,512]{1,0:T(8,128)(2,1)S(1)}, u32[]{:S(2)}, u32[]{:S(2)}) collective-permute-start(bf16[128,512]{1,0:T(8,128)(2,1)S(1)} %get-tuple-element.53), channel_id=1, source_target_pairs={{24,0},{16,8},{8,16},{0,24},{25,1},{17,9},{9,17},{1,25},{26,2},{18... | collective-permute-start | bytes 393224 | tf_op jit(solution)/shard_map/ppermute | solution.py:463
  26.0 0.8 %parts.1 = (bf16[128,512]{1,0:T(8,128)(2,1)S(1)}, bf16[128,512]{1,0:T(8,128)(2,1)S(1)}) custom-call(f32[8,512]{1,0:T(8,128)S(1)} %get-tuple-element.47.norms_ref, bf16[512,1024]{1,0:T(8,128)(2,1)S(1)} %get-tuple-element.48.table_ref, bf16[128,1024]{1,0:T(8,128)(2,1)S(1)} %collective-permute-done.8.refs_0_, bf16[128,1024]{1,0:T(8,128)(2,1)S(1)} %collective-permute-done.9.refs_1_), custom_call_target="tpu_custom_call" | custom-call | flops 268435456 | bytes 1048576 | tf_op jit(solution)/shard_map/parts/pallas_call | solution.py:337
  26.9 1.7 %collective-permute-start.10 = (bf16[128,512]{1,0:T(8,128)(2,1)S(1)}, bf16[128,512]{1,0:T(8,128)(2,1)S(1)}, u32[]{:S(2)}, u32[]{:S(2)}) collective-permute-start(bf16[128,512]{1,0:T(8,128)(2,1)S(1)} %get-tuple-element.51), channel_id=1, source_target_pairs={{8,0},{0,8},{24,16},{16,24},{9,1},{1,9},{25,17},{17,25},{10,2},{2,... | collective-permute-start | bytes 393224 | tf_op jit(solution)/shard_map/ppermute | solution.py:463
  28.6 0.8 %collective-permute-start.11 = (bf16[128,512]{1,0:T(8,128)(2,1)S(1)}, bf16[128,512]{1,0:T(8,128)(2,1)S(1)}, u32[]{:S(2)}, u32[]{:S(2)}) collective-permute-start(bf16[128,512]{1,0:T(8,128)(2,1)S(1)} %get-tuple-element.52), channel_id=1, source_target_pairs={{16,0},{24,8},{0,16},{8,24},{17,1},{25,9},{1,17},{9,25},{18,2},{26... | collective-permute-start | bytes 393224 | tf_op jit(solution)/shard_map/ppermute | solution.py:463
  29.4 5.5 %scores.1.refs_3_ = f32[4096,512]{1,0:T(8,128)} custom-call(f32[32,128]{1,0:T(8,128)S(1)} %get-tuple-element.30.alive_ref, f32[8,512]{1,0:T(8,128)S(1)} %get-tuple-element.47.norms_ref, bf16[512,1024]{1,0:T(8,128)(2,1)S(1)} %get-tuple-element.48.table_ref, bf16[4096,1024]{1,0:T(8,128)(2,1)S(1)} %copy-done), custom_call_target="tpu_custom_call" | custom-call | flops 4294967296 | bytes 8388608 | tf_op jit(solution)/shard_map/scores/pallas_call | solution.py:374
  34.9 0.0 collective-permute-done.12.refs_2_
  34.9 0.0 collective-permute-done.11.refs_1_
  34.9 1.4 %merge.1 = f32[4096,512]{1,0:T(8,128)} custom-call(s32[3]{0:T(128)S(1)} %get-tuple-element.46.picks_ref, f32[32,128]{1,0:T(8,128)S(1)} %get-tuple-element.30.alive_ref, bf16[128,512]{1,0:T(8,128)(2,1)S(1)} %collective-permute-done.10.refs_0_, bf16[128,512]{1,0:T(8,128)(2,1)S(1)} %collective-permute-done.11.refs_1_, ...), custom_call_target="tpu_custom_call", output_to_operand_aliasing={{}: (5, {})} | custom-call | flops 393216 | bytes 1179648 | tf_op jit(solution)/shard_map/merge/pallas_call | solution.py:420
  (7 shorter events, 0.0 us)
Async XLA Ops:
  0.6 7.9 %copy-start = (bf16[4096,1024]{1,0:T(8,128)(2,1)S(1)}, bf16[4096,1024]{1,0:T(8,128)(2,1)}, u32[]{:S(2)}) copy-start(bf16[4096,1024]{1,0:T(8,128)(2,1)} %vec_ref.5) | copy-start | bytes 25165828
  4.0 8.7 %collective-permute-start = (f32[16,128]{1,0:T(8,128)S(1)}, f32[16,128]{1,0:T(8,128)S(1)}, u32[]{:S(2)}, u32[]{:S(2)}) collective-permute-start(f32[16,128]{1,0:T(8,128)S(1)} %get-tuple-element.32), channel_id=1, source_target_pairs={{0,24},{8,16},{16,8},{24,0},{1,25},{9,17},{17,9},{25,1},{2,26},{10... | collective-permute-start | bytes 24584 | tf_op jit(solution)/shard_map/ppermute | solution.py:447
  7.9 4.7 %collective-permute-start.1 = (f32[16,128]{1,0:T(8,128)S(1)}, f32[16,128]{1,0:T(8,128)S(1)}, u32[]{:S(2)}, u32[]{:S(2)}) collective-permute-start(f32[16,128]{1,0:T(8,128)S(1)} %get-tuple-element.33), channel_id=1, source_target_pairs={{0,16},{8,24},{16,0},{24,8},{1,17},{9,25},{17,1},{25,9},{2,18},{10... | collective-permute-start | bytes 24584 | tf_op jit(solution)/shard_map/ppermute | solution.py:447
  8.4 4.2 %collective-permute-start.2 = (f32[16,128]{1,0:T(8,128)S(1)}, f32[16,128]{1,0:T(8,128)S(1)}, u32[]{:S(2)}, u32[]{:S(2)}) collective-permute-start(f32[16,128]{1,0:T(8,128)S(1)} %get-tuple-element.34), channel_id=1, source_target_pairs={{0,8},{8,0},{16,24},{24,16},{1,9},{9,1},{17,25},{25,17},{2,10},{10... | collective-permute-start | bytes 24584 | tf_op jit(solution)/shard_map/ppermute | solution.py:447
  9.8 11.9 %collective-permute-start.6 = (bf16[128,1024]{1,0:T(8,128)(2,1)S(1)}, bf16[128,1024]{1,0:T(8,128)(2,1)S(1)}, u32[]{:S(2)}, u32[]{:S(2)}) collective-permute-start(bf16[128,1024]{1,0:T(8,128)(2,1)S(1)} %get-tuple-element.38), channel_id=1, source_target_pairs={{0,24},{8,16},{16,8},{24,0},{1,25},{9,17},{17,9},{25,1},{2,26},{10... | collective-permute-start | bytes 786440 | tf_op jit(solution)/shard_map/ppermute | solution.py:450
  12.6 9.2 %copy-start.1 = (bf16[512,1024]{1,0:T(8,128)(2,1)S(1)}, bf16[512,1024]{1,0:T(8,128)(2,1)}, u32[]{:S(2)}) copy-start(bf16[512,1024]{1,0:T(8,128)(2,1)} %refs_4_.1) | copy-start | bytes 3145732
  12.8 6.3 %collective-permute-start.5 = (s16[8,4608]{1,0:T(8,128)(2,1)S(1)}, s16[8,4608]{1,0:T(8,128)(2,1)S(1)}, u32[]{:S(2)}, u32[]{:S(2)}) collective-permute-start(s16[8,4608]{1,0:T(8,128)(2,1)S(1)} %pack.1.refs_0_), channel_id=1, source_target_pairs={{0,6},{1,7},{2,4},{3,5},{4,2},{5,3},{6,0},{7,1},{8,14},{9,15},{10,... | collective-permute-start | bytes 221192 | tf_op jit(solution)/shard_map/ppermute | solution.py:455
  16.4 4.4 %collective-permute-start.4 = (s16[8,4608]{1,0:T(8,128)(2,1)S(1)}, s16[8,4608]{1,0:T(8,128)(2,1)S(1)}, u32[]{:S(2)}, u32[]{:S(2)}) collective-permute-start(s16[8,4608]{1,0:T(8,128)(2,1)S(1)} %pack.1.refs_0_), channel_id=1, source_target_pairs={{0,2},{1,3},{2,0},{3,1},{4,6},{5,7},{6,4},{7,5},{8,10},{9,11},{10,... | collective-permute-start | bytes 221192 | tf_op jit(solution)/shard_map/ppermute | solution.py:455
  16.4 5.3 %collective-permute-start.3 = (s16[8,4608]{1,0:T(8,128)(2,1)S(1)}, s16[8,4608]{1,0:T(8,128)(2,1)S(1)}, u32[]{:S(2)}, u32[]{:S(2)}) collective-permute-start(s16[8,4608]{1,0:T(8,128)(2,1)S(1)} %pack.1.refs_0_), channel_id=1, source_target_pairs={{0,4},{1,5},{2,6},{3,7},{4,0},{5,1},{6,2},{7,3},{8,12},{9,13},{10,... | collective-permute-start | bytes 221192 | tf_op jit(solution)/shard_map/ppermute | solution.py:455
  17.2 8.8 %collective-permute-start.8 = (bf16[128,1024]{1,0:T(8,128)(2,1)S(1)}, bf16[128,1024]{1,0:T(8,128)(2,1)S(1)}, u32[]{:S(2)}, u32[]{:S(2)}) collective-permute-start(bf16[128,1024]{1,0:T(8,128)(2,1)S(1)} %get-tuple-element.49), channel_id=1, source_target_pairs={{0,8},{8,0},{16,24},{24,16},{1,9},{9,1},{17,25},{25,17},{2,10},{10... | collective-permute-start | bytes 786440 | tf_op jit(solution)/shard_map/ppermute | solution.py:453
  19.1 6.9 %collective-permute-start.9 = (bf16[128,1024]{1,0:T(8,128)(2,1)S(1)}, bf16[128,1024]{1,0:T(8,128)(2,1)S(1)}, u32[]{:S(2)}, u32[]{:S(2)}) collective-permute-start(bf16[128,1024]{1,0:T(8,128)(2,1)S(1)} %get-tuple-element.50), channel_id=1, source_target_pairs={{0,16},{8,24},{16,0},{24,8},{1,17},{9,25},{17,1},{25,9},{2,18},{10... | collective-permute-start | bytes 786440 | tf_op jit(solution)/shard_map/ppermute | solution.py:453
  21.7 1.6 %collective-permute-start.7 = (s16[32,4608]{1,0:T(8,128)(2,1)S(1)}, s16[32,4608]{1,0:T(8,128)(2,1)S(1)}, u32[]{:S(2)}, u32[]{:S(2)}) collective-permute-start(s16[32,4608]{1,0:T(8,128)(2,1)S(1)} %pad_add_fusion), channel_id=1, source_target_pairs={{0,1},{1,0},{2,3},{3,2},{4,5},{5,4},{6,7},{7,6},{8,9},{9,8},{10,11... | collective-permute-start | bytes 884744 | tf_op jit(solution)/shard_map/ppermute | solution.py:460
  25.0 9.9 %collective-permute-start.12 = (bf16[128,512]{1,0:T(8,128)(2,1)S(1)}, bf16[128,512]{1,0:T(8,128)(2,1)S(1)}, u32[]{:S(2)}, u32[]{:S(2)}) collective-permute-start(bf16[128,512]{1,0:T(8,128)(2,1)S(1)} %get-tuple-element.53), channel_id=1, source_target_pairs={{24,0},{16,8},{8,16},{0,24},{25,1},{17,9},{9,17},{1,25},{26,2},{18... | collective-permute-start | bytes 393224 | tf_op jit(solution)/shard_map/ppermute | solution.py:463
  26.9 8.0 %collective-permute-start.10 = (bf16[128,512]{1,0:T(8,128)(2,1)S(1)}, bf16[128,512]{1,0:T(8,128)(2,1)S(1)}, u32[]{:S(2)}, u32[]{:S(2)}) collective-permute-start(bf16[128,512]{1,0:T(8,128)(2,1)S(1)} %get-tuple-element.51), channel_id=1, source_target_pairs={{8,0},{0,8},{24,16},{16,24},{9,1},{1,9},{25,17},{17,25},{10,2},{2,... | collective-permute-start | bytes 393224 | tf_op jit(solution)/shard_map/ppermute | solution.py:463
  28.6 6.3 %collective-permute-start.11 = (bf16[128,512]{1,0:T(8,128)(2,1)S(1)}, bf16[128,512]{1,0:T(8,128)(2,1)S(1)}, u32[]{:S(2)}, u32[]{:S(2)}) collective-permute-start(bf16[128,512]{1,0:T(8,128)(2,1)S(1)} %get-tuple-element.52), channel_id=1, source_target_pairs={{16,0},{24,8},{0,16},{8,24},{17,1},{25,9},{1,17},{9,25},{18,2},{26... | collective-permute-start | bytes 393224 | tf_op jit(solution)/shard_map/ppermute | solution.py:463
